TPU v7x, 512 devices: a whole 4x8x8 slice. The times are simulated.
512 devices in a mesh: ex: 128 (over y, x, z_hi), blk: 4 (over z_lo, core).
Axes of the slice: x: 4, y: 8, z: 8 (z_hi: 4, z_lo: 2; z = z_hi * 2 + z_lo), core: 2. Of those that a mesh axis runs over, the one named last changes fastest.
Arguments:
- train_grads: bfloat16 [1024, 10240], P('ex', 'blk'), may hold values from -0.0234375 to 0.0234375
- train_acts: bfloat16 [1024, 2560], P('ex', 'blk'), may hold values from -0.0234375 to 0.0234375
- train_mask: int32 [1024], P('ex'), may hold values 0 or 1
- query_grads: bfloat16 [512, 10240], P('ex', 'blk'), may hold values from -6 to 6
- query_acts: bfloat16 [512, 2560], P('ex', 'blk'), may hold values from -6 to 6
- grad_basis: bfloat16 [10240, 10240], P('blk', 'ex'), may hold values from -0.0625 to 0.0625
- act_basis: bfloat16 [2560, 2560], P('blk', 'ex'), may hold values from -0.125 to 0.125
- eigenvalues: float32 [10240, 2560], P('ex'), may hold values from 0.1 to 10
Outputs:
- scores: float32 [1024, 8], P(('ex', 'blk'))
All inputs are finite; a program needn't handle non-finite values. No bound on the sum of `train_mask` on one device may be relied on, other than what follows from the above.
Results may differ from a plain program's by a relative error of at most 0.0039.
Values may be sent and summed in bfloat16 or wider, within the bound.
No kernel may reach another device: no remote copies, remote signals or barrier semaphores. Data moves between devices by JAX's collectives and lax.ppermute only.
A program may use at most 64 MiB of HBM per device.

v0:
```python
import jax
import jax.numpy as jnp
from jax import lax
from jax.sharding import PartitionSpec as P

QRY = 8
QLEN = 64


damping = 0.1


def per_device(
    train_grads, train_acts, train_mask, query_grads, query_acts, grad_basis, act_basis, eigenvalues
):
    shard_count = lax.axis_size("ex")
    block_count = lax.axis_size("blk")
    local_tokens = train_grads.shape[0]
    local_queries = query_grads.shape[0]
    grad_cols = train_grads.shape[1]
    rot_grad_cols = grad_basis.shape[1]
    rot_act_cols = act_basis.shape[1]
    rot_cols = rot_grad_cols + rot_act_cols
    token_block = local_tokens // block_count
    masked = train_grads * train_mask[:, None].astype(jnp.bfloat16)
    joined = jnp.concatenate(
        [jnp.concatenate([masked, train_acts], 1), jnp.concatenate([query_grads, query_acts], 1)], 0
    )
    piece = lax.all_gather(joined, "ex", axis=0, tiled=True)
    grad_part = jnp.dot(piece[:, :grad_cols], grad_basis, preferred_element_type=jnp.float32)
    act_part = jnp.dot(piece[:, grad_cols:], act_basis, preferred_element_type=jnp.float32)
    rotated = jnp.concatenate([grad_part, act_part], 1)
    rotated = rotated.reshape(shard_count, local_tokens + local_queries, rot_cols)
    train_part = rotated[:, :local_tokens].reshape(shard_count, block_count, token_block, rot_cols)
    train_rot = lax.psum_scatter(train_part, "blk", scatter_dimension=1, tiled=True)
    query_rot = lax.psum(rotated[:, local_tokens:], "blk")
    train_rot = train_rot.reshape(shard_count * token_block, rot_cols)
    query_rot = query_rot.reshape(shard_count * local_queries, rot_cols)
    train_grad_rot = train_rot[:, :rot_grad_cols]
    train_act_part = train_rot[:, rot_grad_cols:].astype(jnp.bfloat16)
    query_grad_rot = query_rot[:, :rot_grad_cols].astype(jnp.bfloat16)
    query_act_part = query_rot[:, rot_grad_cols:].astype(jnp.bfloat16)
    train_act_full, query_act_full = (
        lax.all_gather(train_act_part, "ex", axis=1, tiled=True),
        lax.all_gather(query_act_part, "ex", axis=1, tiled=True),
    )
    query_grad_blocks = query_grad_rot.reshape(QRY, QLEN, rot_grad_cols)
    query_act_blocks = query_act_full.reshape(QRY, QLEN, query_act_full.shape[1])
    raw_blocks = jnp.einsum(
        "qsf,qsd->qfd", query_grad_blocks, query_act_blocks, preferred_element_type=jnp.float32
    )
    scaled = raw_blocks / (eigenvalues[None] + damping)
    flat_scaled = scaled.reshape(QRY * rot_grad_cols, scaled.shape[2])
    acts_rows = train_act_full.astype(jnp.float32)
    mixed = lax.dot_general(
        acts_rows,
        flat_scaled,
        (((1,), (1,)), ((), ())),
        precision=lax.Precision.HIGHEST,
        preferred_element_type=jnp.float32,
    )
    mixed = mixed.reshape(token_block * lax.axis_size("ex"), QRY, rot_grad_cols)
    return lax.psum_scatter(
        jnp.einsum("tf,tqf->tq", train_grad_rot, mixed, precision=lax.Precision.HIGHEST),
        "ex",
        scatter_dimension=0,
        tiled=True,
    )


def solution(mesh):
    placed = (
        P("ex", "blk"),
        P("ex", "blk"),
        P("ex"),
        P("ex", "blk"),
        P("ex", "blk"),
        P("blk", "ex"),
        P("blk", "ex"),
        P("ex", None),
    )
    return jax.shard_map(
        per_device, mesh=mesh, in_specs=placed, out_specs=P(("ex", "blk"), None), check_vma=False
    )
```

profile of v0, /device:TPU:64, one launch (start us, length us, event | category | flops | bytes accessed | tf_op | source)
XLA Modules:
  0.0 1291.5 jit_solution(6974952605424724284)
XLA Ops:
  6.5 0.7 convert_element_type.3
  7.2 0.9 broadcast_multiply_fusion
  8.1 1.4 maximum_bitcast_fusion
  9.6 193.7 %all-gather.7.cloned.1.call-done = bf16[128,12,3200]{2,1,0:T(8,128)(2,1)} async-done(((bf16[1,12,3200]{2,1,0:T(8,128)(2,1)}), bf16[128,12,3200]{2,1,0:T(8,128)(2,1)}) %all-gather.7.cloned.1.call-update) | async-done | bytes 9830416 | tf_op jit(solution)/shard_map/all_gather | solution.py:29
  203.2 16.5 %reshape.33 = bf16[1536,3200]{1,0:T(8,128)(2,1)} reshape(bf16[128,12,3200]{2,1,0:T(8,128)(2,1)} %all-gather.7.cloned.1.call-done) | data formatting | bytes 19660800
  219.8 5.7 fusion
  225.5 2.3 fusion.5
  227.8 0.3 copy.16
  228.1 0.1 reshape.26
  228.2 1.0 copy.17
  229.3 1.3 dynamic-slice
  230.6 42.7 %all-reduce.5.cloned.1.call-done = f32[128,4,2,100]{0,2,1,3:T(2,128)} async-done(((f32[128,4,2,100]{0,2,1,3:T(2,128)}), f32[128,4,2,100]{0,2,1,3:T(2,128)}) %all-reduce.5.cloned.1.call-update) | async-done | bytes 409616
  273.3 1.5 constant_dynamic-slice_fusion.1
  274.9 0.1 copy.18
  275.0 0.1 fusion.7
  275.1 0.7 copy.19
  275.9 14.6 %all-reduce.6 = bf16[512,100]{1,0:T(8,128)(2,1)S(1)} all-reduce(f32[512,100]{1,0:T(8,128)S(1)} %bitcast.40), channel_id=1, replica_groups=mesh['ex'=128,'blk'=4] {'blk'}, use_global_device_ids=true, to_apply=%region_1.0 | all-reduce | flops 51200 | bytes 307200 | tf_op jit(solution)/shard_map/psum | solution.py:36
  290.5 0.1 slice_bitcast_fusion
  290.6 0.7 copy.21
  291.3 1.3 dynamic-slice.2
  293.2 2.1 broadcast_add_fusion
  295.4 100.9 %all-gather.9.cloned.1.call-done = bf16[128,20,256]{2,1,0:T(8,128)(2,1)} async-done(((bf16[1,20,256]{2,1,0:T(8,128)(2,1)}), bf16[128,20,256]{2,1,0:T(8,128)(2,1)}) %all-gather.9.cloned.1.call-update) | async-done | bytes 1310736 | tf_op jit(solution)/shard_map/all_gather | solution.py:44
  396.3 3.3 reshape.38
  399.5 125.6 %all-gather.11.cloned.1.call-done = bf16[128,20,512]{2,1,0:T(8,128)(2,1)} async-done(((bf16[1,20,512]{2,1,0:T(8,128)(2,1)}), bf16[128,20,512]{2,1,0:T(8,128)(2,1)}) %all-gather.11.cloned.1.call-update) | async-done | bytes 2621456 | tf_op jit(solution)/shard_map/all_gather | solution.py:45
  525.1 3.6 reshape.37
  528.8 2.8 copy.22
  531.5 2.9 fusion.8
  534.5 3.3 fusion.2
  537.8 0.4 copy.25
  538.2 1.8 fusion.9
  540.1 744.3 %all-reduce.1 = f32[256,8]{1,0:T(8,128)S(1)} all-reduce(f32[256,8]{1,0:T(8,128)S(1)} %bitcast.43), channel_id=3, replica_groups=mesh['ex'=128,'blk'=4] {'ex'}, use_global_device_ids=true, to_apply=%region_2.0.clone | all-reduce | flops 2048 | bytes 16384
  1284.4 0.6 constant_dynamic-slice_fusion
  (19 shorter events, 0.3 us)
Async XLA Ops:
  6.5 213.2 %copy-start = (bf16[2560,80]{0,1:T(8,128)(2,1)S(1)}, bf16[2560,80]{0,1:T(8,128)(2,1)}, u32[]{:S(2)}) copy-start(bf16[2560,80]{0,1:T(8,128)(2,1)} %param.13) | copy-start | bytes 1228804
  6.5 196.7 %all-gather.7.cloned.1.call-start = ((), (), s32[]{:S(2)}) async-start(), calls=%async_computation | async-start | bytes 13209600 | tf_op jit(solution)/shard_map/all_gather | solution.py:29
  9.5 263.8 %all-reduce.5.cloned.1.call-start = ((), (), s32[]{:S(2)}) async-start(), calls=%async_computation.3 | async-start | bytes 819200
  219.8 5.7 copy-start.3
  229.2 167.0 %all-gather.9.cloned.1.call-start = ((), (), s32[]{:S(2)}) async-start(), calls=%async_computation.1 | async-start | bytes 1585152 | tf_op jit(solution)/shard_map/all_gather | solution.py:44
  275.8 249.3 %all-gather.11.cloned.1.call-start = ((), (), s32[]{:S(2)}) async-start(), calls=%async_computation.2 | async-start | bytes 3170304 | tf_op jit(solution)/shard_map/all_gather | solution.py:45
  531.5 2.9 copy-start.1
  531.5 3.0 copy-start.2
Sparse Core Ops, SparseCore 0:
  11.8 191.3 all-gather.6
  229.4 43.9 all-reduce.4
  278.4 117.8 all-gather.8
  401.4 123.7 all-gather.10
where the time goes:
time: 1290 us
  blocking collectives  759 us (59%)
  waiting for transfers between devices  463 us (36%)
  local copies, waits for them, and re-layouts  34.4 us (3%)
  matrix products  16 us (1%)
  between operations  13.9 us (1%)
    unnamed x1, blocking collectives  744 us
    all_gather x1, waiting for transfers between devices, per_device(): piece = lax.all_gather(joined, 'ex', axis=0, tiled=True)  194 us
    all_gather x1, waiting for transfers between devices, per_device(): lax.all_gather(query_act_part, 'ex', axis=1, tiled=True)  126 us
    all_gather x1, waiting for transfers between devices, per_device(): lax.all_gather(train_act_part, 'ex', axis=1, tiled=True)  101 us
    unnamed x5, waiting for transfers between devices  42.8 us
    unnamed x20, local copies, waits for them, and re-layouts  32.5 us
  transfers between devices with their start and end apart: 4, of which 4 were waited for; matrix products, arithmetic and copies ran while one was open for 1% of the time, Pallas kernels for 0%

commit v1 on v0

v1 whole, which is shorter than its diff:
```python
import functools

import jax
import jax.numpy as jnp
from jax import lax
from jax.experimental import pallas as pl
from jax.experimental.pallas import tpu as pltpu
from jax.sharding import Mesh, PartitionSpec as P

damping = 0.1

BF = jnp.bfloat16
F32 = jnp.float32


def pick(row_of, rows, cols, dtype=BF):
    r = lax.broadcasted_iota(jnp.int32, (rows, cols), 0)
    c = lax.broadcasted_iota(jnp.int32, (rows, cols), 1)
    return (row_of(r) == c).astype(dtype)


def high_low(v):
    high = v.astype(BF)
    return high, (v - high.astype(F32)).astype(BF)


def swap(v, axis):
    return lax.ppermute(v, axis, [(0, 1), (1, 0)])


def exchange(pieces, axis):
    n = lax.axis_size(axis)
    me = lax.axis_index(axis)
    received = [lax.dynamic_index_in_dim(pieces, me, 0, keepdims=False)]
    for step in range(1, n):
        out = lax.dynamic_index_in_dim(pieces, (me + step) % n, 0, keepdims=False)
        received.append(lax.ppermute(out, axis, [(i, (i + step) % n) for i in range(n)]))
    stacked = jnp.stack(received)
    order = (me - jnp.arange(n)) % n
    return jnp.concatenate(
        [lax.dynamic_index_in_dim(stacked, order[k], 0, keepdims=True) for k in range(n)], 0
    )


def spread(v, axes, count):
    return lax.all_to_all(jnp.broadcast_to(v[None], (count,) + v.shape), axes, 0, 0, tiled=True)


def rotate_kernel(full_ref, g0_ref, g1_ref, a0_ref, a1_ref, out_ref, *, X, H, L, tt, tq, gs, f_own):
    per = 2 * (tt + tq)
    inner = X // L
    wt, wq = inner * tt, inner * tq
    for l in range(L):
        g = a = 0.0
        for s, (bg, ba) in enumerate(((g0_ref, a0_ref), (g1_ref, a1_ref))):
            rows = [full_ref[pl.ds((l * inner + x) * per + s * tt, tt), :] for x in range(inner)]
            rows += [full_ref[pl.ds((l * inner + x) * per + 2 * tt + s * tq, tq), :] for x in range(inner)]
            tokens = jnp.concatenate(rows, 0)
            g += lax.dot_general(bg[...], tokens[:, :gs], (((1,), (1,)), ((), ())), preferred_element_type=F32)
            a += lax.dot_general(ba[...], tokens[:, gs:], (((1,), (1,)), ((), ())), preferred_element_type=F32)
        g_high, g_low = high_low(g[:, wt:])
        g_train = g[:, :wt].astype(BF)
        a_high, a_low = high_low(a)
        for h in range(H):
            m = h * L + l
            out_ref[m, :f_own, :wt] = g_train[h * f_own:(h + 1) * f_own]
            out_ref[m, :f_own, wt:wt + wq] = g_high[h * f_own:(h + 1) * f_own]
            out_ref[m, :f_own, wt + wq:] = g_low[h * f_own:(h + 1) * f_own]
        for m in range(H * L):
            r = slice(m * 16, m * 16 + 16)
            at = f_own + 16 * l
            out_ref[m, at:at + 16, :wt] = a_high[r, :wt]
            out_ref[m, at:at + 16, wt:] = a_low[r, :wt]
            at = f_own + 16 * L
            out_ref[m, at:at + 16, l * 2 * wq:l * 2 * wq + wq] = a_high[r, wt:]
            out_ref[m, at:at + 16, l * 2 * wq + wq:(l + 1) * 2 * wq] = a_low[r, wt:]


def combine_kernel(parts_ref, g_ref, a_ref, *, n, f_own, L, wt, wq, d_part):
    total = parts_ref[0].astype(F32)
    for k in range(1, n):
        total += parts_ref[k].astype(F32)
    g_train = total[:f_own, :wt].astype(BF)
    g_query = (total[:f_own, wt:wt + wq] + total[:f_own, wt + wq:]).astype(BF)
    for k in range(g_ref.shape[0]):
        g_ref[k, :, :wt] = g_train
        g_ref[k, :, wt:] = g_query
    a_train = [total[f_own + 16 * l:f_own + 16 * l + 16] for l in range(L)]
    a_train = jnp.concatenate([t[:, :wt] + t[:, wt:] for t in a_train], 1)
    last = total[f_own + 16 * L:]
    a_query = jnp.concatenate(
        [last[:, l * 2 * wq:l * 2 * wq + wq] + last[:, l * 2 * wq + wq:(l + 1) * 2 * wq] for l in range(L)], 1
    ).astype(BF)
    half = d_part // 2
    r = lax.broadcasted_iota(jnp.int32, (16, 16), 0)
    c = lax.broadcasted_iota(jnp.int32, (16, 16), 1)
    inside = (r >= d_part) & (r < d_part + half)
    sides = [
        jnp.dot((inside & (c == r - d_part + k * half)).astype(BF), a_query, preferred_element_type=F32)
        for k in range(2)
    ]
    packed = (a_train + jnp.concatenate(sides, 1)).astype(BF)
    for k in range(a_ref.shape[0]):
        a_ref[k] = packed


def score_kernel(a_ref, ao_ref, g_ref, go_ref, inv_ref, out_ref, *, Y, H, L, wt, wq, d_part, group):
    half = d_part // 2
    n = a_ref.shape[0]
    r = lax.broadcasted_iota(jnp.int32, (n, n), 0)
    c = lax.broadcasted_iota(jnp.int32, (n, n), 1)
    j = r % 16
    base = r - j + d_part
    unpack = [
        ((j >= k * half) & (j < (k + 1) * half) & (c == base + j - k * half)).astype(BF) for k in range(2)
    ]

    def query_acts(ref):
        width = ref.shape[1] // 2
        return (
            jnp.dot(unpack[0], ref[:, :width], preferred_element_type=F32)
            + jnp.dot(unpack[1], ref[:, width:], preferred_element_type=F32)
        ).astype(BF)

    def grads(ref, cols):
        return jnp.concatenate(
            [jnp.concatenate([ref[h * L + l, :, cols] for h in range(H)], 0) for l in range(L)], 1
        )

    qa = jnp.concatenate([query_acts(a_ref), query_acts(ao_ref)], 1)
    qg = jnp.concatenate([grads(g_ref, slice(wt, wt + wq)), grads(go_ref, slice(wt, wt + wq))], 1)
    g_train = grads(g_ref, slice(0, wt)).astype(F32)
    d_tile = inv_ref.shape[1] // 2
    r = lax.broadcasted_iota(jnp.int32, (d_tile, n), 0)
    c = lax.broadcasted_iota(jnp.int32, (d_tile, n), 1)
    place = (c == (r // d_part) * 16 + r % d_part).astype(BF)
    inv = jnp.dot(inv_ref[:, :d_tile], place, preferred_element_type=F32) + jnp.dot(
        inv_ref[:, d_tile:], place, preferred_element_type=F32
    )
    owner = (lax.broadcasted_iota(jnp.int32, qg.shape, 1) // group) % Y
    acts = a_ref[...]
    for q in range(Y):
        raw = lax.dot_general(
            jnp.where(owner == q, qg, jnp.zeros_like(qg)), qa, (((1,), (1,)), ((), ())), preferred_element_type=F32
        )
        mixed = jnp.dot((raw * inv).astype(BF), acts, preferred_element_type=F32)
        out_ref[q:q + 1, :] = jnp.sum(mixed * g_train, axis=0, keepdims=True)


def local_call(kernel, shapes, *args):
    return pl.pallas_call(
        kernel,
        out_shape=shapes,
        in_specs=[pl.BlockSpec(memory_space=pltpu.VMEM)] * len(args),
        out_specs=jax.tree.map(lambda _: pl.BlockSpec(memory_space=pltpu.VMEM), shapes),
        compiler_params=pltpu.CompilerParams(vmem_limit_bytes=40 * 2**20),
    )(*args)


def per_device(
    train_grads, train_acts, train_mask, query_grads, query_acts, grad_basis, act_basis, eigenvalues
):
    Y, X, H, L, C = (lax.axis_size(a) for a in ("y", "x", "zh", "zl", "c"))
    core = lax.axis_index("c")
    low = lax.axis_index("zl")
    gk, f_own = grad_basis.shape
    ak, d_own = act_basis.shape
    gs, as_ = gk // H, ak // H
    nt, nq = train_grads.shape[0], query_grads.shape[0]
    th, qh = nt // C, nq // C
    d_all = eigenvalues.shape[1]
    f_tile, d_block = f_own * H, d_own * H
    d_part = d_block // (H * L)
    d_tile = d_part * X * Y

    masked = train_grads * train_mask[:, None].astype(BF)
    grads = jnp.concatenate([masked.reshape(L, C, nt // (L * C), gk).transpose(1, 0, 2, 3).reshape(C, th, gk),
                             query_grads.reshape(C, qh, gk)], 1)
    acts = jnp.concatenate([train_acts.reshape(L, C, nt // (L * C), ak).transpose(1, 0, 2, 3).reshape(C, th, ak),
                            query_acts.reshape(C, qh, ak)], 1)
    both = jnp.concatenate([grads, acts], 2)
    mine = jnp.where(core == 0, both[0], both[1])
    theirs = jnp.where(core == 0, both[1], both[0])
    rows2 = jnp.stack([mine, swap(theirs, "c")])

    width = gs + as_
    slices = jnp.concatenate(
        [rows2[:, :, :gk].reshape(C, th + qh, H, gs), rows2[:, :, gk:].reshape(C, th + qh, H, as_)], 3
    ).transpose(2, 0, 1, 3)
    train_rows = slices[:, :, :th].reshape(H, C * th, width)
    query_rows = slices[:, :, th:].reshape(H, C * qh * 2, width // 2)
    message = jnp.concatenate([train_rows, query_rows], 2)
    message = jnp.broadcast_to(message[None], (Y,) + message.shape).reshape((Y * H,) + message.shape[1:])
    got = lax.all_to_all(message, ("y", "zh"), 0, 0, tiled=True)
    got = got.reshape(Y * H * C * th, width + width // 2)

    gb = grad_basis.T.reshape(f_own, H, gs).transpose(1, 0, 2)
    ab = act_basis.T.reshape(d_own, H, as_).transpose(1, 0, 2)
    ab = jnp.pad(ab, ((0, 0), (0, 0), (0, gs - as_)))
    own = exchange(jnp.concatenate([gb, ab], 1), "zh")
    other = swap(own, "c")

    def base(v):
        a = v[:, f_own:, :as_].reshape(H * L, d_part, as_)
        return v[:, :f_own].reshape(f_tile, gs), jnp.pad(a, ((0, 0), (0, 16 - d_part), (0, 0))).reshape(H * L * 16, as_)

    (g0, a0), (g1, a1) = base(own), base(other)

    G = Y * H
    src = C * th

    def train_row(r):
        s, rest = r // (G * th), r % (G * th)
        return (rest // th) * src + s * th + rest % th

    def query_row(half):
        def row(r):
            s, rest = r // (G * qh), r % (G * qh)
            return (rest // qh) * src + (s * qh + rest % qh) * 2 + half
        return row

    def move(row_of, rows, v):
        return jnp.dot(pick(row_of, rows, G * src), v, preferred_element_type=F32).astype(BF)

    t_rows, q_rows = G * C * th, G * C * qh
    moved_t = move(train_row, t_rows, got[:, :width])
    moved_q = jnp.concatenate(
        [move(query_row(h), q_rows, got[:, width:]) for h in range(2)], 1
    )
    block = jnp.concatenate([moved_t, moved_q], 0)
    block, g0, a0, g1, a1 = lax.optimization_barrier((block, g0, a0, g1, a1))
    full = spread(block, "x", X).reshape(X * (t_rows + q_rows), width)

    inverse = 1.0 / (eigenvalues + damping)

    def wanted(c):
        h, rest = c // d_tile, c % d_tile
        return (rest // d_part) * d_block + h * (L * d_part) + low * d_part + rest % d_part

    sel_r = lax.broadcasted_iota(jnp.int32, (d_all, H * d_tile), 0)
    sel_c = lax.broadcasted_iota(jnp.int32, (d_all, H * d_tile), 1)
    sel = (wanted(sel_c) == sel_r).astype(BF)
    inv_high, inv_low = high_low(inverse)
    chosen = jnp.dot(jnp.concatenate([inv_high, inv_low], 0), sel, preferred_element_type=F32).astype(BF)
    chosen = chosen.reshape(2, f_own, H, d_tile).transpose(2, 1, 0, 3).reshape(H, f_own, 2 * d_tile)
    inv = exchange(chosen, "zh").reshape(f_tile, 2 * d_tile)

    tt, tq = G * th, G * qh
    wt, wq = X // L * tt, X // L * tq
    parts = local_call(
        functools.partial(rotate_kernel, X=X, H=H, L=L, tt=tt, tq=tq, gs=gs, f_own=f_own),
        jax.ShapeDtypeStruct((H * L, f_own + 16 * L + 16, wt + 2 * wq), BF),
        full, g0, g1, a0, a1,
    )
    parts, inv = lax.optimization_barrier((parts, inv))
    parts = lax.all_to_all(parts, ("zh", "zl"), 0, 0, tiled=True)
    g_out, a_out = local_call(
        functools.partial(combine_kernel, n=H * L, f_own=f_own, L=L, wt=wt, wq=wq, d_part=d_part),
        (jax.ShapeDtypeStruct((H * L, f_own, wt + wq), BF), jax.ShapeDtypeStruct((Y * X, 16, L * wt), BF)),
        parts,
    )
    a_all = lax.all_to_all(a_out, ("y", "x"), 0, 0, tiled=True).reshape(Y * X * 16, L * wt)
    a_other = swap(a_all, "c")
    g_all = lax.all_to_all(g_out, ("zh", "zl"), 0, 0, tiled=True)
    g_other = swap(g_all, "c")
    scores = local_call(
        functools.partial(score_kernel, Y=Y, H=H, L=L, wt=wt, wq=wq, d_part=d_part, group=H * qh),
        jax.ShapeDtypeStruct((Y, L * wt), F32),
        a_all, a_other, g_all, g_other, inv,
    )
    n_out = Y * X * H * L
    scores = scores.T.reshape(n_out, scores.shape[1] // n_out * Y)
    mine = lax.all_to_all(scores, ("x", "y", "zh", "zl"), 0, 0, tiled=True).sum(0)
    return mine.reshape(-1, Y)


def factored(mesh):
    devices = mesh.devices
    ex, blk = devices.shape
    xs, cores = 4, 2
    zh = 4
    return Mesh(
        devices.reshape(ex // (xs * zh), xs, zh, blk // cores, cores), ("y", "x", "zh", "zl", "c")
    )


def solution(mesh):
    ex, blk = ("y", "x", "zh"), ("zl", "c")
    placed = (
        P(ex, blk),
        P(ex, blk),
        P(ex),
        P(ex, blk),
        P(ex, blk),
        P(blk, ex),
        P(blk, ex),
        P(ex, None),
    )
    return jax.shard_map(
        per_device, mesh=factored(mesh), in_specs=placed, out_specs=P(ex + blk, None), check_vma=False
    )
```

time: 1290 us -> 216 us (0.17)
  the two profiles are of different devices: /device:TPU:64 before, /device:TPU:1 now
where the time goes in v1:
time: 216 us; the launch traced here: 214 us
  blocking collectives  71.3 us (33%)
  starting transfers between devices  69.7 us (32%)
  waiting for transfers between devices  27.4 us (13%)
  local copies, waits for them, and re-layouts  20.3 us (9%)
  between operations  8.04 us (4%)
  Pallas kernels  6.63 us (3%)
  other arithmetic  6.13 us (3%)
  matrix products  4.6 us (2%)
    all_to_all x1, blocking collectives, per_device(): parts = lax.all_to_all(parts, ('zh', 'zl'), 0, 0, tiled=True)  28.4 us
    ppermute x4, starting transfers between devices, swap(): return lax.ppermute(v, axis, [(0, 1), (1, 0)])  26.2 us
    ppermute x6, starting transfers between devices, exchange(): lax.ppermute(out, axis, [(i, (i + step) % n) for i in range(n)])  22.9 us
    all_to_all x1, blocking collectives, per_device(): lax.all_to_all(scores, ('x', 'y', 'zh', 'zl'), 0, 0, tiled=True).sum(0)  22.3 us
    all_to_all x1, blocking collectives, per_device(): lax.all_to_all(a_out, ('y', 'x'), 0, 0, tiled=True)  20.6 us
    all_to_all x1, starting transfers between devices, per_device(): got = lax.all_to_all(message, ('y', 'zh'), 0, 0, tiled=True)  10.2 us
    all_to_all x1, waiting for transfers between devices, per_device(): got = lax.all_to_all(message, ('y', 'zh'), 0, 0, tiled=True)  8.43 us
    pallas_call x3, Pallas kernels, local_call(): pl.pallas_call(kernel, out_shape=shapes, in_specs=[pl.BlockSpec(memory_sp...  6.63 us
  transfers between devices with their start and end apart: 13, of which 7 were waited for; matrix products, arithmetic and copies ran while one was open for 9% of the time, Pallas kernels for 0%

profile of v1, /device:TPU:1, one launch (start us, length us, event | category | flops | bytes accessed | tf_op | source)
XLA Modules:
  0.0 214.2 jit_solution(15860242218478873296)
XLA Ops:
  4.1 8.8 %collective-permute-start = (bf16[6,3200]{1,0:T(8,128)(2,1)S(1)}, bf16[6,3200]{1,0:T(8,128)(2,1)S(1)}, u32[]{:S(2)}, u32[]{:S(2)}) collective-permute-start(bf16[6,3200]{1,0:T(8,128)(2,1)S(1)} %bitcast.86), channel_id=1, source_target_pairs={{0,1},{1,0},{2,3},{3,2},{4,5},{5,4},{6,7},{7,6},{8,9},{9,8},{10,11... | collective-permute-start | bytes 115208 | tf_op jit(solution)/shard_map/ppermute | solution.py:28
  13.8 1.1 reshape.100
  16.2 5.3 %collective-permute-start.3 = (bf16[100,640]{1,0:T(8,128)(2,1)S(1)}, bf16[100,640]{1,0:T(8,128)(2,1)S(1)}, u32[]{:S(2)}, u32[]{:S(2)}) collective-permute-start(bf16[100,640]{1,0:T(8,128)(2,1)S(1)} %bitcast.77), channel_id=1, source_target_pairs={{0,12},{4,0},{8,4},{12,8},{1,13},{5,1},{9,5},{13,9},{2,14},{6,2},{... | collective-permute-start | bytes 384008 | tf_op jit(solution)/shard_map/ppermute | solution.py:37
  21.5 1.9 collective-permute-start.2
  23.5 4.2 %collective-permute-start.1 = (bf16[100,640]{1,0:T(8,128)(2,1)S(1)}, bf16[100,640]{1,0:T(8,128)(2,1)S(1)}, u32[]{:S(2)}, u32[]{:S(2)}) collective-permute-start(bf16[100,640]{1,0:T(8,128)(2,1)S(1)} %bitcast.81), channel_id=1, source_target_pairs={{0,4},{4,8},{8,12},{12,0},{1,5},{5,9},{9,13},{13,1},{2,6},{6,10},{... | collective-permute-start | bytes 384008 | tf_op jit(solution)/shard_map/ppermute | solution.py:37
  37.6 10.2 %all-to-all-start = ((bf16[32,8,1200]{2,1,0:T(8,128)(2,1)}), bf16[32,8,1200]{2,1,0:T(8,128)(2,1)S(1)}, u32[]{:S(2)}, u32[]{:S(2)}) async-start(bf16[32,8,1200]{2,1,0:T(8,128)(2,1)} %bitcast.7), calls=%async_computation | async-start | bytes 1310720 | tf_op jit(solution)/shard_map/all_to_all | solution.py:194
  48.5 1.2 pad_maximum_fusion
  50.8 1.2 pad_maximum_fusion.1
  52.0 3.0 %collective-permute-start.4 = (bf16[4,100,640]{2,0,1:T(4,128)(2,1)S(1)}, bf16[4,100,640]{2,0,1:T(4,128)(2,1)}, u32[]{:S(2)}, u32[]{:S(2)}) collective-permute-start(bf16[4,100,640]{2,0,1:T(4,128)(2,1)S(1)} %pad_maximum_fusion.1), channel_id=1, source_target_pairs={{0,1},{1,0},{2,3},{3,2},{4,5},{5,4},{6,7},{7,6},{8,9},{9,8},{10,11... | collective-permute-start | bytes 1536008 | tf_op jit(solution)/shard_map/ppermute | solution.py:28
  55.5 1.2 collective-permute-done.4
  56.7 1.1 slice.81
  59.5 8.4 %all-to-all-done = bf16[32,8,1200]{2,1,0:T(8,128)(2,1)S(1)} async-done(((bf16[32,8,1200]{2,1,0:T(8,128)(2,1)}), bf16[32,8,1200]{2,1,0:T(8,128)(2,1)S(1)}, u32[]{:S(2)}, u32[]{:S(2)}) %all-to-all-start) | async-done | bytes 614432 | tf_op jit(solution)/shard_map/all_to_all | solution.py:194
  69.7 1.7 broadcast_in_dim.5
  71.3 4.7 %all-to-all-start.1 = ((bf16[4,384,800]{1,2,0:T(8,128)(2,1)}), bf16[4,384,800]{1,2,0:T(8,128)(2,1)}, u32[]{:S(2)}, u32[]{:S(2)}) async-start(bf16[4,384,800]{1,2,0:T(8,128)(2,1)} %broadcast_in_dim.5), calls=%async_computation.1 | async-start | bytes 4915200 | tf_op jit(solution)/shard_map/all_to_all | solution.py:46
  76.0 3.0 %fusion.27 = bf16[160,1280]{1,0:T(8,128)(2,1)S(1)} fusion(s32[]{:T(128)S(6)} %mul.63, s32[1280]{0:T(1024)S(1)} %get-tuple-element.59, s32[1280]{0:T(1024)S(1)} %get-tuple-element.62, s32[1280]{0:T(1024)S(1)} %get-tuple-element.60, s32[1280]{0:T(1024)S(1)} %get-tuple-element.61, pred[1280]{0:T(1024)(128)(4,1)S(1)} %get-tuple-element.63, ...), kind=kOutput, calls=%fused_computation.30 | convolution fusion | flops 1115955200 | bytes 1251844 | tf_op jit(solution)/shard_map/dot_general | solution.py:244
  80.5 3.6 %collective-permute-start.7 = (bf16[80,640]{1,0:T(8,128)(2,1)S(1)}, bf16[80,640]{1,0:T(8,128)(2,1)S(1)}, u32[]{:S(2)}, u32[]{:S(2)}) collective-permute-start(bf16[80,640]{1,0:T(8,128)(2,1)S(1)} %get-tuple-element.38), channel_id=1, source_target_pairs={{0,12},{4,0},{8,4},{12,8},{1,13},{5,1},{9,5},{13,9},{2,14},{6,2},{... | collective-permute-start | bytes 307208 | tf_op jit(solution)/shard_map/ppermute | solution.py:37
  84.1 4.2 %collective-permute-start.6 = (bf16[80,640]{1,0:T(8,128)(2,1)S(1)}, bf16[80,640]{1,0:T(8,128)(2,1)S(1)}, u32[]{:S(2)}, u32[]{:S(2)}) collective-permute-start(bf16[80,640]{1,0:T(8,128)(2,1)S(1)} %get-tuple-element.39), channel_id=1, source_target_pairs={{0,8},{4,12},{8,0},{12,4},{1,9},{5,13},{9,1},{13,5},{2,10},{6,14},... | collective-permute-start | bytes 307208 | tf_op jit(solution)/shard_map/ppermute | solution.py:37
  88.3 3.7 %collective-permute-start.5 = (bf16[80,640]{1,0:T(8,128)(2,1)S(1)}, bf16[80,640]{1,0:T(8,128)(2,1)S(1)}, u32[]{:S(2)}, u32[]{:S(2)}) collective-permute-start(bf16[80,640]{1,0:T(8,128)(2,1)S(1)} %get-tuple-element.40), channel_id=1, source_target_pairs={{0,4},{4,8},{8,12},{12,0},{1,5},{5,9},{9,13},{13,1},{2,6},{6,10},{... | collective-permute-start | bytes 307208 | tf_op jit(solution)/shard_map/ppermute | solution.py:37
  92.0 1.4 collective-permute-done.6
  93.4 3.4 %collective-permute-done.5 = bf16[80,640]{1,0:T(8,128)(2,1)S(1)} collective-permute-done((bf16[80,640]{1,0:T(8,128)(2,1)S(1)}, bf16[80,640]{1,0:T(8,128)(2,1)S(1)}, u32[]{:S(2)}, u32[]{:S(2)}) %collective-permute-start.5) | collective-permute-done | bytes 102432 | tf_op jit(solution)/shard_map/ppermute | solution.py:37
  97.8 6.2 %all-to-all-done.1 = bf16[4,384,800]{1,2,0:T(8,128)(2,1)} async-done(((bf16[4,384,800]{1,2,0:T(8,128)(2,1)}), bf16[4,384,800]{1,2,0:T(8,128)(2,1)}, u32[]{:S(2)}, u32[]{:S(2)}) %all-to-all-start.1) | async-done | bytes 2457632 | tf_op jit(solution)/shard_map/all_to_all | solution.py:46
  104.0 3.2 %copy.104 = bf16[4,384,800]{2,1,0:T(8,128)(2,1)S(1)} copy(bf16[4,384,800]{1,2,0:T(8,128)(2,1)} %all-to-all-done.1) | data formatting | bytes 4915200 | tf_op jit(solution)/shard_map/all_to_all | solution.py:46
  108.2 1.3 shard_map.82
  109.5 28.4 %all_to_all.34.parts_ref = bf16[8,128,512]{2,1,0:T(8,128)(2,1)S(1)} all-to-all(bf16[8,128,512]{2,1,0:T(8,128)(2,1)S(1)} %shard_map.82), channel_id=1, replica_groups=mesh['y'=8,'x'=4,'zh'=4,'zl'=2,'c'=2] {'zh','zl'}, dimensions={0} | all-to-all | bytes 2097152 | tf_op jit(solution)/shard_map/all_to_all | solution.py:256
  138.9 20.6 %all_to_all.35 = bf16[32,16,512]{2,1,0:T(8,128)(2,1)S(1)} all-to-all(bf16[32,16,512]{2,1,0:T(8,128)(2,1)S(1)} %get-tuple-element.20), channel_id=1, replica_groups=mesh['y'=8,'x'=4,'zh'=4,'zl'=2,'c'=2] {'y','x'}, dimensions={0} | all-to-all | bytes 1048576 | tf_op jit(solution)/shard_map/all_to_all | solution.py:262
  159.5 5.7 %all-to-all-start.4 = ((bf16[8,80,384]{2,1,0:T(8,128)(2,1)}), bf16[8,80,384]{2,1,0:T(8,128)(2,1)S(1)}, u32[]{:S(2)}, u32[]{:S(2)}) async-start(bf16[8,80,384]{2,1,0:T(8,128)(2,1)} %get-tuple-element.21), calls=%async_computation.4 | async-start | bytes 983040 | tf_op jit(solution)/shard_map/all_to_all | solution.py:264
  165.2 6.1 %collective-permute-start.8 = (bf16[512,512]{1,0:T(8,128)(2,1)S(1)}, bf16[512,512]{1,0:T(8,128)(2,1)S(1)}, u32[]{:S(2)}, u32[]{:S(2)}) collective-permute-start(bf16[512,512]{1,0:T(8,128)(2,1)S(1)} %bitcast.59), channel_id=1, source_target_pairs={{0,1},{1,0},{2,3},{3,2},{4,5},{5,4},{6,7},{7,6},{8,9},{9,8},{10,11... | collective-permute-start | bytes 1572872 | tf_op jit(solution)/shard_map/ppermute | solution.py:28
  171.3 5.3 %all-to-all-done.4.g_ref = bf16[8,80,384]{2,1,0:T(8,128)(2,1)S(1)} async-done(((bf16[8,80,384]{2,1,0:T(8,128)(2,1)}), bf16[8,80,384]{2,1,0:T(8,128)(2,1)S(1)}, u32[]{:S(2)}, u32[]{:S(2)}) %all-to-all-start.4) | async-done | bytes 491552 | tf_op jit(solution)/shard_map/all_to_all | solution.py:264
  176.6 8.3 %collective-permute-start.9 = (bf16[8,80,384]{2,1,0:T(8,128)(2,1)S(1)}, bf16[8,80,384]{2,1,0:T(8,128)(2,1)S(1)}, u32[]{:S(2)}, u32[]{:S(2)}) collective-permute-start(bf16[8,80,384]{2,1,0:T(8,128)(2,1)S(1)} %all-to-all-done.4.g_ref), channel_id=1, source_target_pairs={{0,1},{1,0},{2,3},{3,2},{4,5},{5,4},{6,7},{7,6},{8,9},{9,8},{10,11... | collective-permute-start | bytes 1474568 | tf_op jit(solution)/shard_map/ppermute | solution.py:28
  184.9 1.5 collective-permute-done.9.go_ref
  186.4 4.4 %shard_map.84 = f32[8,512]{1,0:T(8,128)S(1)} custom-call(bf16[512,512]{1,0:T(8,128)(2,1)S(1)} %bitcast.60, bf16[512,512]{1,0:T(8,128)(2,1)S(1)} %collective-permute-done.8.ao_ref, bf16[8,80,384]{2,1,0:T(8,128)(2,1)S(1)} %all-to-all-done.4.g_ref, bf16[8,80,384]{2,1,0:T(8,128)(2,1)S(1)} %collective-permute-done.9.go_ref, bf16[320,640]{1,0:T(8,128)(2,1)S(1)} %bitcast.63), custom_call_target="tpu_custom_call" | custom-call | tf_op jit(solution)/shard_map/pallas_call | solution.py:151
  191.0 22.3 %all_to_all.36 = f32[256,1,16]{2,1,0:T(1,128)S(1)} all-to-all(f32[256,1,16]{2,1,0:T(1,128)S(1)} %bitcast.72), channel_id=1, replica_groups=mesh['y'=8,'x'=4,'zh'=4,'zl'=2,'c'=2] {'x','y','zh','zl'}, dimensions={0} | all-to-all | bytes 32768 | tf_op jit(solution)/shard_map/all_to_all | solution.py:273
  (89 shorter events, 19.5 us)
Async XLA Ops:
  4.1 31.8 %collective-permute-start = (bf16[6,3200]{1,0:T(8,128)(2,1)S(1)}, bf16[6,3200]{1,0:T(8,128)(2,1)S(1)}, u32[]{:S(2)}, u32[]{:S(2)}) collective-permute-start(bf16[6,3200]{1,0:T(8,128)(2,1)S(1)} %bitcast.86), channel_id=1, source_target_pairs={{0,1},{1,0},{2,3},{3,2},{4,5},{5,4},{6,7},{7,6},{8,9},{9,8},{10,11... | collective-permute-start | bytes 115208 | tf_op jit(solution)/shard_map/ppermute | solution.py:28
  16.2 31.6 %collective-permute-start.3 = (bf16[100,640]{1,0:T(8,128)(2,1)S(1)}, bf16[100,640]{1,0:T(8,128)(2,1)S(1)}, u32[]{:S(2)}, u32[]{:S(2)}) collective-permute-start(bf16[100,640]{1,0:T(8,128)(2,1)S(1)} %bitcast.77), channel_id=1, source_target_pairs={{0,12},{4,0},{8,4},{12,8},{1,13},{5,1},{9,5},{13,9},{2,14},{6,2},{... | collective-permute-start | bytes 384008 | tf_op jit(solution)/shard_map/ppermute | solution.py:37
  21.5 26.5 %collective-permute-start.2 = (bf16[100,640]{1,0:T(8,128)(2,1)S(1)}, bf16[100,640]{1,0:T(8,128)(2,1)S(1)}, u32[]{:S(2)}, u32[]{:S(2)}) collective-permute-start(bf16[100,640]{1,0:T(8,128)(2,1)S(1)} %bitcast.79), channel_id=1, source_target_pairs={{0,8},{4,12},{8,0},{12,4},{1,9},{5,13},{9,1},{13,5},{2,10},{6,14},... | collective-permute-start | bytes 384008 | tf_op jit(solution)/shard_map/ppermute | solution.py:37
  23.5 24.8 %collective-permute-start.1 = (bf16[100,640]{1,0:T(8,128)(2,1)S(1)}, bf16[100,640]{1,0:T(8,128)(2,1)S(1)}, u32[]{:S(2)}, u32[]{:S(2)}) collective-permute-start(bf16[100,640]{1,0:T(8,128)(2,1)S(1)} %bitcast.81), channel_id=1, source_target_pairs={{0,4},{4,8},{8,12},{12,0},{1,5},{5,9},{9,13},{13,1},{2,6},{6,10},{... | collective-permute-start | bytes 384008 | tf_op jit(solution)/shard_map/ppermute | solution.py:37
  37.6 30.3 %all-to-all-start = ((bf16[32,8,1200]{2,1,0:T(8,128)(2,1)}), bf16[32,8,1200]{2,1,0:T(8,128)(2,1)S(1)}, u32[]{:S(2)}, u32[]{:S(2)}) async-start(bf16[32,8,1200]{2,1,0:T(8,128)(2,1)} %bitcast.7), calls=%async_computation | async-start | bytes 1310720 | tf_op jit(solution)/shard_map/all_to_all | solution.py:194
  48.3 6.7 %copy-start.2 = (f32[80,2560]{1,0:T(8,128)S(1)}, f32[80,2560]{1,0:T(8,128)}, u32[]{:S(2)}) copy-start(f32[80,2560]{1,0:T(8,128)} %param.15) | copy-start | bytes 2457604
  52.0 4.7 %collective-permute-start.4 = (bf16[4,100,640]{2,0,1:T(4,128)(2,1)S(1)}, bf16[4,100,640]{2,0,1:T(4,128)(2,1)}, u32[]{:S(2)}, u32[]{:S(2)}) collective-permute-start(bf16[4,100,640]{2,0,1:T(4,128)(2,1)S(1)} %pad_maximum_fusion.1), channel_id=1, source_target_pairs={{0,1},{1,0},{2,3},{3,2},{4,5},{5,4},{6,7},{7,6},{8,9},{9,8},{10,11... | collective-permute-start | bytes 1536008 | tf_op jit(solution)/shard_map/ppermute | solution.py:28
  71.3 32.6 %all-to-all-start.1 = ((bf16[4,384,800]{1,2,0:T(8,128)(2,1)}), bf16[4,384,800]{1,2,0:T(8,128)(2,1)}, u32[]{:S(2)}, u32[]{:S(2)}) async-start(bf16[4,384,800]{1,2,0:T(8,128)(2,1)} %broadcast_in_dim.5), calls=%async_computation.1 | async-start | bytes 4915200 | tf_op jit(solution)/shard_map/all_to_all | solution.py:46
  80.5 11.5 %collective-permute-start.7 = (bf16[80,640]{1,0:T(8,128)(2,1)S(1)}, bf16[80,640]{1,0:T(8,128)(2,1)S(1)}, u32[]{:S(2)}, u32[]{:S(2)}) collective-permute-start(bf16[80,640]{1,0:T(8,128)(2,1)S(1)} %get-tuple-element.38), channel_id=1, source_target_pairs={{0,12},{4,0},{8,4},{12,8},{1,13},{5,1},{9,5},{13,9},{2,14},{6,2},{... | collective-permute-start | bytes 307208 | tf_op jit(solution)/shard_map/ppermute | solution.py:37
  84.1 9.3 %collective-permute-start.6 = (bf16[80,640]{1,0:T(8,128)(2,1)S(1)}, bf16[80,640]{1,0:T(8,128)(2,1)S(1)}, u32[]{:S(2)}, u32[]{:S(2)}) collective-permute-start(bf16[80,640]{1,0:T(8,128)(2,1)S(1)} %get-tuple-element.39), channel_id=1, source_target_pairs={{0,8},{4,12},{8,0},{12,4},{1,9},{5,13},{9,1},{13,5},{2,10},{6,14},... | collective-permute-start | bytes 307208 | tf_op jit(solution)/shard_map/ppermute | solution.py:37
  88.3 8.6 %collective-permute-start.5 = (bf16[80,640]{1,0:T(8,128)(2,1)S(1)}, bf16[80,640]{1,0:T(8,128)(2,1)S(1)}, u32[]{:S(2)}, u32[]{:S(2)}) collective-permute-start(bf16[80,640]{1,0:T(8,128)(2,1)S(1)} %get-tuple-element.40), channel_id=1, source_target_pairs={{0,4},{4,8},{8,12},{12,0},{1,5},{5,9},{9,13},{13,1},{2,6},{6,10},{... | collective-permute-start | bytes 307208 | tf_op jit(solution)/shard_map/ppermute | solution.py:37
  107.2 1.0 copy-start
  109.5 76.8 %copy-start.1 = (bf16[4,80,640]{2,1,0:T(8,128)(2,1)S(1)}, bf16[4,80,640]{2,1,0:T(8,128)(2,1)}, u32[]{:S(2)}) copy-start(bf16[4,80,640]{2,1,0:T(8,128)(2,1)} %pad_maximum_fusion.3) | copy-start | bytes 1228804
  159.5 17.1 %all-to-all-start.4 = ((bf16[8,80,384]{2,1,0:T(8,128)(2,1)}), bf16[8,80,384]{2,1,0:T(8,128)(2,1)S(1)}, u32[]{:S(2)}, u32[]{:S(2)}) async-start(bf16[8,80,384]{2,1,0:T(8,128)(2,1)} %get-tuple-element.21), calls=%async_computation.4 | async-start | bytes 983040 | tf_op jit(solution)/shard_map/all_to_all | solution.py:264
  165.2 21.1 %collective-permute-start.8 = (bf16[512,512]{1,0:T(8,128)(2,1)S(1)}, bf16[512,512]{1,0:T(8,128)(2,1)S(1)}, u32[]{:S(2)}, u32[]{:S(2)}) collective-permute-start(bf16[512,512]{1,0:T(8,128)(2,1)S(1)} %bitcast.59), channel_id=1, source_target_pairs={{0,1},{1,0},{2,3},{3,2},{4,5},{5,4},{6,7},{7,6},{8,9},{9,8},{10,11... | collective-permute-start | bytes 1572872 | tf_op jit(solution)/shard_map/ppermute | solution.py:28
  176.6 9.7 %collective-permute-start.9 = (bf16[8,80,384]{2,1,0:T(8,128)(2,1)S(1)}, bf16[8,80,384]{2,1,0:T(8,128)(2,1)S(1)}, u32[]{:S(2)}, u32[]{:S(2)}) collective-permute-start(bf16[8,80,384]{2,1,0:T(8,128)(2,1)S(1)} %all-to-all-done.4.g_ref), channel_id=1, source_target_pairs={{0,1},{1,0},{2,3},{3,2},{4,5},{5,4},{6,7},{7,6},{8,9},{9,8},{10,11... | collective-permute-start | bytes 1474568 | tf_op jit(solution)/shard_map/ppermute | solution.py:28

commit v2 on v1

v2 whole, which is shorter than its diff:
```python
import functools

import jax
import jax.numpy as jnp
from jax import lax
from jax.experimental import pallas as pl
from jax.experimental.pallas import tpu as pltpu
from jax.sharding import Mesh, PartitionSpec as P

damping = 0.1

BF = jnp.bfloat16
F32 = jnp.float32


def high_low(v):
    high = v.astype(BF)
    return high, (v - high.astype(F32)).astype(BF)


def swap(v, axis):
    return lax.ppermute(v, axis, [(0, 1), (1, 0)])


def exchange(pieces, axis):
    n = lax.axis_size(axis)
    me = lax.axis_index(axis)
    received = [lax.dynamic_index_in_dim(pieces, me, 0, keepdims=False)]
    for step in range(1, n):
        out = lax.dynamic_index_in_dim(pieces, (me + step) % n, 0, keepdims=False)
        received.append(lax.ppermute(out, axis, [(i, (i + step) % n) for i in range(n)]))
    return received


def iota(shape, dim):
    return lax.broadcasted_iota(jnp.int32, shape, dim)


def matmul(a, b):
    return jnp.dot(a, b, preferred_element_type=F32)


def lanes(v, shift, start, stop):
    n = v.shape[1]
    if shift % n:
        v = pltpu.roll(v, shift % n, 1)
    c = iota(v.shape, 1)
    return jnp.where((c >= start) & (c < stop), v, 0.0)


LANES = 128


def message_kernel(tg_ref, ta_ref, mask_ref, qg_ref, qa_ref, mine_ref, theirs_ref, *, H, L, C):
    core = lax.axis_index("c")
    nt, nq = tg_ref.shape[0], qg_ref.shape[0]
    th, per = nt // C, nt // (L * C)
    r, c = iota((2 * nt, nt), 0), iota((2 * nt, nt), 1)
    first = r < th
    owner = jnp.where(first, core, 1 - core)
    k = r % th
    token = (k // per) * (C * per) + owner * per + k % per
    used = first | (r >= 2 * nt - th)
    pick = (used & (token == c)).astype(F32)
    masked = (pick * mask_ref[...].astype(F32)).astype(BF)
    pick = pick.astype(BF)
    r, c = iota((2 * nt, nq), 0), iota((2 * nt, nq), 1)
    first = r < th
    owner = jnp.where(first, core, 1 - core)
    used = first | (r >= 2 * nt - th)
    pick_q = (used & (owner * (nq // C) + (r % th) // 2 == c)).astype(BF)
    tg, ta = matmul(masked, tg_ref[...]), matmul(pick, ta_ref[...])
    qg, qa = matmul(pick_q, qg_ref[...]), matmul(pick_q, qa_ref[...])
    gs = tg.shape[1] // H
    wide = 3 * LANES
    out = []
    for h in range(H):
        low_half = iota((2 * nt, wide), 0) % 2 == 0
        q = qg[:, h * gs:(h + 1) * gs]
        q_high = jnp.concatenate([q[:, wide:], jnp.zeros((2 * nt, 2 * wide - gs), F32)], 1)
        q = jnp.where(low_half, q[:, :wide], q_high)
        low_half = low_half[:, :LANES]
        a_tile, rest = qa[:, h * LANES:(h + 1) * LANES], qa[:, H * LANES:]
        at = 32 * h
        b_tile = lanes(ta[:, H * LANES:], -at, 0, 32) + jnp.where(
            low_half,
            lanes(a_tile, 32, 32, 96) + lanes(rest, 96 - at, 96, 112),
            lanes(a_tile, -32, 32, 96) + lanes(rest, 80 - at, 96, 112),
        )
        out.append(
            jnp.concatenate([tg[:, h * gs:(h + 1) * gs], ta[:, h * LANES:(h + 1) * LANES], b_tile, q], 1)
        )
    mine_ref[...] = jnp.concatenate([v[:nt] for v in out], 0).astype(BF)
    theirs_ref[...] = jnp.concatenate([v[nt:] for v in out], 0).astype(BF)


def shuffle_kernel(got_ref, out_ref, *, G, th, qh, gs):
    src = 2 * th
    n = G * src
    r, c = iota((n, n), 0), iota((n, n), 1)
    rest = r % (G * th)
    pick = (c == (rest // th) * src + (r // (G * th)) * th + rest % th).astype(BF)
    qn = 2 * G * qh
    r, c = iota((qn, n), 0), iota((qn, n), 1)
    rest = r % (G * qh)
    row = (rest // qh) * src + ((r // (G * qh)) * qh + rest % qh) * 2
    picks = [(c == row + half).astype(BF) for half in range(2)]
    width = gs + LANES
    got = got_ref[...]
    train = matmul(pick, got[:, :width + LANES])
    wide = 3 * LANES
    q_grads = jnp.concatenate(
        [matmul(picks[0], got[:, width + LANES:]), matmul(picks[1], got[:, width + LANES:width + LANES + gs - wide])], 1
    )
    v0, v1 = (matmul(p, got[:, width:width + LANES]) for p in picks)
    q_a = lanes(v0, -32, 0, 64) + lanes(v1, 32, 64, 128)
    q_b = lanes(v0, 32, 0, 16) + lanes(v1, 48, 16, 32)
    body = jnp.concatenate([train[:, :width], jnp.concatenate([q_grads, q_a], 1)], 0).astype(BF)
    tail = jnp.concatenate([train[:, width:], q_b], 0)
    rows = tail.shape[0] // 4
    packed = sum(lanes(tail[g * rows:(g + 1) * rows], 32 * g, 32 * g, 32 * g + 32) for g in range(4)).astype(BF)
    tiles = width // LANES
    per = rows // tiles
    packed = jnp.concatenate([packed[k * per:(k + 1) * per] for k in range(tiles)], 1)
    for x in range(out_ref.shape[0]):
        out_ref[x, :n + qn] = body
        out_ref[x, n + qn:] = packed


def rotate_kernel(full_ref, own_ref, other_ref, out_ref, *, X, H, L, tt, tq, gs, f_own):
    me = lax.axis_index("zh")
    per = 2 * (tt + tq)
    inner = X // L
    wt, wq = inner * tt, inner * tq
    tiles = gs // LANES + 1
    group = per // 4
    fine = group // tiles
    grads = [jnp.concatenate([b[s, :f_own] for s in range(H)], 0) for b in (own_ref, other_ref)]
    acts = [jnp.concatenate([b[s, f_own:, :2 * LANES] for s in range(H)], 0) for b in (own_ref, other_ref)]
    for l in range(L):
        blocks = []
        for x in range(inner):
            at = l * inner + x
            packed = jnp.concatenate(
                [full_ref[at, per:, k * LANES:(k + 1) * LANES].astype(F32) for k in range(tiles)], 0
            )
            tail = jnp.concatenate([lanes(packed, -32 * g, 0, 32) for g in range(4)], 0).astype(BF)
            blocks.append((full_ref.at[at], tail))
        g = a = 0.0
        for s in range(2):
            spans = [(b, t, s * tt, tt) for b, t in blocks] + [(b, t, 2 * tt + s * tq, tq) for b, t in blocks]
            tokens = jnp.concatenate([b[p:p + m, :gs] for b, _, p, m in spans], 0)
            inputs = jnp.concatenate(
                [jnp.concatenate([b[p:p + m, gs:], t[p:p + m]], 1) for b, t, p, m in spans], 0
            )
            g += lax.dot_general(grads[s], tokens, (((1,), (1,)), ((), ())), preferred_element_type=F32)
            a += lax.dot_general(acts[s], inputs, (((1,), (1,)), ((), ())), preferred_element_type=F32)
        g_high, g_low = high_low(g[:, wt:])
        g_train = g[:, :wt].astype(BF)
        a_high, a_low = high_low(a)
        for s in range(H):
            h = lax.rem(me - s + H, H)
            m = h * L + l
            out_ref[m, :f_own, :wt] = g_train[s * f_own:(s + 1) * f_own]
            out_ref[m, :f_own, wt:wt + wq] = g_high[s * f_own:(s + 1) * f_own]
            out_ref[m, :f_own, wt + wq:] = g_low[s * f_own:(s + 1) * f_own]
            for k in range(L):
                m = h * L + k
                r = slice((s * L + k) * 16, (s * L + k) * 16 + 16)
                at = f_own + 16 * l
                out_ref[m, at:at + 16, :wt] = a_high[r, :wt]
                out_ref[m, at:at + 16, wt:] = a_low[r, :wt]
                at = f_own + 16 * L
                out_ref[m, at:at + 16, l * 2 * wq:l * 2 * wq + wq] = a_high[r, wt:]
                out_ref[m, at:at + 16, l * 2 * wq + wq:(l + 1) * 2 * wq] = a_low[r, wt:]


def combine_kernel(parts_ref, g_ref, a_ref, *, n, f_own, L, wt, wq, d_part):
    total = parts_ref[0].astype(F32)
    for k in range(1, n):
        total += parts_ref[k].astype(F32)
    g_train = total[:f_own, :wt].astype(BF)
    g_query = (total[:f_own, wt:wt + wq] + total[:f_own, wt + wq:]).astype(BF)
    g_ref[:, :wt] = g_train
    g_ref[:, wt:] = g_query
    a_train = [total[f_own + 16 * l:f_own + 16 * l + 16] for l in range(L)]
    a_train = jnp.concatenate([t[:, :wt] + t[:, wt:] for t in a_train], 1)
    last = total[f_own + 16 * L:]
    a_query = jnp.concatenate(
        [last[:, l * 2 * wq:l * 2 * wq + wq] + last[:, l * 2 * wq + wq:(l + 1) * 2 * wq] for l in range(L)], 1
    ).astype(BF)
    half = d_part // 2
    r = lax.broadcasted_iota(jnp.int32, (16, 16), 0)
    c = lax.broadcasted_iota(jnp.int32, (16, 16), 1)
    inside = (r >= d_part) & (r < d_part + half)
    sides = [
        jnp.dot((inside & (c == r - d_part + k * half)).astype(BF), a_query, preferred_element_type=F32)
        for k in range(2)
    ]
    packed = (a_train + jnp.concatenate(sides, 1)).astype(BF)
    for k in range(a_ref.shape[0]):
        a_ref[k] = packed


def score_kernel(
    a_ref, ao_ref, g0_ref, g1_ref, g2_ref, g3_ref, go_ref, inv_ref, out_ref, *, Y, L, wt, wq, d_part, group
):
    low = lax.axis_index("zl")
    pieces = (g0_ref, g1_ref, g2_ref, g3_ref)
    half = d_part // 2
    n = a_ref.shape[0]
    r, c = iota((n, n), 0), iota((n, n), 1)
    j = r % 16
    base = r - j + d_part
    unpack = [
        ((j >= k * half) & (j < (k + 1) * half) & (c == base + j - k * half)).astype(BF) for k in range(2)
    ]

    def query_acts(ref):
        width = ref.shape[1] // 2
        return (matmul(unpack[0], ref[:, :width]) + matmul(unpack[1], ref[:, width:])).astype(BF)

    def chunks(own, other):
        return jnp.concatenate([jnp.where(low == 0, own, other), jnp.where(low == 0, other, own)], 1)

    def grads(cols):
        return chunks(*(jnp.concatenate([p[k, :, cols] for p in pieces], 0).astype(F32) for k in range(L)))

    f_own = go_ref.shape[1]
    theirs = [jnp.concatenate([go_ref[s * L + k] for s in range(len(pieces))], 0).astype(F32) for k in range(L)]
    qa = jnp.concatenate([query_acts(a_ref), query_acts(ao_ref)], 1)
    qg = jnp.concatenate([grads(slice(wt, wt + wq)), chunks(*theirs)], 1).astype(BF)
    g_train = grads(slice(0, wt))
    d_tile = inv_ref.shape[1] // 2
    r, c = iota((d_tile, n), 0), iota((d_tile, n), 1)
    place = (c == (r // d_part) * 16 + r % d_part).astype(BF)
    inv = matmul(inv_ref[:, :d_tile], place) + matmul(inv_ref[:, d_tile:], place)
    owner = (iota(qg.shape, 1) // group) % Y
    acts = a_ref[...]
    for q in range(Y):
        raw = lax.dot_general(
            jnp.where(owner == q, qg, jnp.zeros_like(qg)), qa, (((1,), (1,)), ((), ())), preferred_element_type=F32
        )
        mixed = matmul((raw * inv).astype(BF), acts)
        out_ref[q:q + 1, :] = jnp.sum(mixed * g_train, axis=0, keepdims=True)


def local_call(kernel, shapes, *args):
    return pl.pallas_call(
        kernel,
        out_shape=shapes,
        in_specs=[pl.BlockSpec(memory_space=pltpu.VMEM)] * len(args),
        out_specs=jax.tree.map(lambda _: pl.BlockSpec(memory_space=pltpu.VMEM), shapes),
        compiler_params=pltpu.CompilerParams(vmem_limit_bytes=40 * 2**20),
    )(*args)


def per_device(
    train_grads, train_acts, train_mask, query_grads, query_acts, grad_basis, act_basis, eigenvalues
):
    Y, X, H, L, C = (lax.axis_size(a) for a in ("y", "x", "zh", "zl", "c"))
    low = lax.axis_index("zl")
    gk, f_own = grad_basis.shape
    ak, d_own = act_basis.shape
    gs, as_ = gk // H, ak // H
    nt, nq = train_grads.shape[0], query_grads.shape[0]
    th, qh = nt // C, nq // C
    d_all = eigenvalues.shape[1]
    f_tile, d_block = f_own * H, d_own * H
    d_part = d_block // (H * L)
    d_tile = d_part * X * Y

    mine, theirs = local_call(
        functools.partial(message_kernel, H=H, L=L, C=C),
        [jax.ShapeDtypeStruct((H * nt, 2 * gs), BF)] * 2,
        train_grads, train_acts, train_mask.reshape(1, nt), query_grads, query_acts,
    )
    message = mine + swap(theirs, "c")
    message = jnp.broadcast_to(message.reshape(1, H, nt, 2 * gs), (Y, H, nt, 2 * gs)).reshape(Y * H, nt, 2 * gs)
    message, grad_basis, act_basis, eigenvalues = lax.optimization_barrier(
        (message, grad_basis, act_basis, eigenvalues)
    )
    got = lax.all_to_all(message, ("y", "zh"), 0, 0, tiled=True)

    gb = grad_basis.T.reshape(f_own, H, gs).transpose(1, 0, 2)
    ab = act_basis.T
    main = ab[:, :H * LANES].reshape(d_own, H, LANES)
    rest = ab[:, H * LANES:].reshape(d_own, H, as_ - LANES)
    ab = jnp.concatenate([main, rest], 2).transpose(1, 0, 2).reshape(H, L, d_part, as_)
    ab = jnp.pad(ab, ((0, 0), (0, 0), (0, 16 - d_part), (0, gs - as_))).reshape(H, L * 16, gs)
    pieces = jnp.concatenate([gb, ab], 1)

    inverse = 1.0 / (eigenvalues + damping)

    def wanted(c):
        h, rest = c // d_tile, c % d_tile
        return (rest // d_part) * d_block + h * (L * d_part) + low * d_part + rest % d_part

    sel = (wanted(iota((d_all, H * d_tile), 1)) == iota((d_all, H * d_tile), 0)).astype(BF)
    inv_high, inv_low = high_low(inverse)
    chosen = jnp.dot(jnp.concatenate([inv_high, inv_low], 0), sel, preferred_element_type=F32).astype(BF)
    chosen = chosen.reshape(2, f_own, H, d_tile).transpose(2, 1, 0, 3).reshape(H, f_own, 2 * d_tile)
    got, pieces, chosen = lax.optimization_barrier((got, pieces, chosen))

    G = Y * H
    block = local_call(
        functools.partial(shuffle_kernel, G=G, th=th, qh=qh, gs=gs),
        jax.ShapeDtypeStruct((X, G * C * (th + qh) * 25 // 24, gs + LANES), BF),
        got.reshape(G * nt, 2 * gs),
    )
    full = lax.all_to_all(block, "x", 0, 0, tiled=True)
    own = jnp.stack(exchange(pieces, "zh"))
    other = swap(own, "c")

    tt, tq = G * th, G * qh
    wt, wq = X // L * tt, X // L * tq
    parts = local_call(
        functools.partial(rotate_kernel, X=X, H=H, L=L, tt=tt, tq=tq, gs=gs, f_own=f_own),
        jax.ShapeDtypeStruct((H * L, f_own + 16 * L + 16, wt + 2 * wq), BF),
        full, own, other,
    )
    parts, chosen = lax.optimization_barrier((parts, chosen))
    parts = lax.all_to_all(parts, ("zh", "zl"), 0, 0, tiled=True)
    inv = jnp.concatenate(exchange(chosen, "zh"), 0)
    parts, inv = lax.optimization_barrier((parts, inv))
    g_out, a_out = local_call(
        functools.partial(combine_kernel, n=H * L, f_own=f_own, L=L, wt=wt, wq=wq, d_part=d_part),
        (jax.ShapeDtypeStruct((f_own, wt + wq), BF), jax.ShapeDtypeStruct((Y * X, 16, L * wt), BF)),
        parts,
    )
    a_all = lax.all_to_all(a_out, ("y", "x"), 0, 0, tiled=True).reshape(Y * X * 16, L * wt)
    a_other = swap(a_all, "c")
    pair = jnp.stack([g_out, swap(g_out, "zl")])
    g_all = [pair] + [
        lax.ppermute(pair, "zh", [(i, (i + step) % H) for i in range(H)]) for step in range(1, H)
    ]
    g_other = swap(jnp.concatenate([p[:, :, wt:] for p in g_all], 0), "c")
    scores = local_call(
        functools.partial(score_kernel, Y=Y, L=L, wt=wt, wq=wq, d_part=d_part, group=H * qh),
        jax.ShapeDtypeStruct((Y, L * wt), F32),
        a_all, a_other, *g_all, g_other, inv,
    )
    n_out = Y * X * H * L
    scores = scores.T.reshape(n_out, scores.shape[1] // n_out * Y)
    mine = lax.all_to_all(scores, ("x", "y", "zh", "zl"), 0, 0, tiled=True).sum(0)
    return mine.reshape(-1, Y)


def factored(mesh):
    devices = mesh.devices
    ex, blk = devices.shape
    xs, cores = 4, 2
    zh = 4
    return Mesh(
        devices.reshape(ex // (xs * zh), xs, zh, blk // cores, cores), ("y", "x", "zh", "zl", "c")
    )


def solution(mesh):
    ex, blk = ("y", "x", "zh"), ("zl", "c")
    placed = (
        P(ex, blk),
        P(ex, blk),
        P(ex),
        P(ex, blk),
        P(ex, blk),
        P(blk, ex),
        P(blk, ex),
        P(ex, None),
    )
    return jax.shard_map(
        per_device, mesh=factored(mesh), in_specs=placed, out_specs=P(ex + blk, None), check_vma=False
    )
```

time: 216 us -> 206 us (0.954)
  blocking collectives: 71.3 us -> 24.8 us
  waiting for transfers between devices: 27.4 us -> 67.4 us
  starting transfers between devices: 69.7 us -> 89.1 us
  local copies, waits for them, and re-layouts: 20.3 us -> 10.4 us
  between operations: 8.04 us -> 0.41 us
  other arithmetic: 6.13 us -> 0.7 us
    all_to_all x2 -> x0, blocking collectives: 49.1 us -> none  [the longest x1 28.4 us: per_device(): parts = lax.all_to_all(parts, ('zh', 'zl'), 0, 0, tiled=True)]
    ppermute x6, waiting for transfers between devices: 4.86 us -> 27.2 us  [exchange(): lax.ppermute(out, axis, [(i, (i + step) % n) for i in range(n)])]
    ppermute x0 -> x3, starting transfers between devices: none -> 10.8 us  [per_device(): lax.ppermute(pair, 'zh', [(i, (i + step) % H) for i in range(H)])]
    ppermute x0 -> x3, waiting for transfers between devices: none -> 8.03 us  [per_device(): lax.ppermute(pair, 'zh', [(i, (i + step) % H) for i in range(H)])]
    all_to_all x2 -> x3, starting transfers between devices: 10.4 us -> 18 us  [the longest x1 8.48 us: per_device(): lax.all_to_all(a_out, ('y', 'x'), 0, 0, tiled=True)]
    all_to_all x1, waiting for transfers between devices: 8.43 us -> 15.2 us  [per_device(): got = lax.all_to_all(message, ('y', 'zh'), 0, 0, tiled=True)]
    unnamed x10 -> x23, local copies, waits for them, and re-layouts: 1.08 us -> 6.9 us
    slice x13 -> x5, local copies, waits for them, and re-layouts: 3.71 us -> 0.02 us  [the longest x3 0.01 us: per_device(): g_other = swap(jnp.concatenate([p[:, :, wt:] for p in g_all], 0), 'c')]
  transfers between devices with their start and end apart: 13 -> 18, of which waited for: 7 -> 13; matrix products, arithmetic and copies ran while one was open for 9% -> 2% of each run, Pallas kernels for 0% -> 0%
where the time goes in v2:
time: 206 us; the launch traced here: 204 us
  starting transfers between devices  89.1 us (43%)
  waiting for transfers between devices  67.4 us (33%)
  blocking collectives  24.8 us (12%)
  local copies, waits for them, and re-layouts  10.4 us (5%)
  Pallas kernels  8.61 us (4%)
  matrix products  2.95 us (1%)
    ppermute x6, waiting for transfers between devices, exchange(): lax.ppermute(out, axis, [(i, (i + step) % n) for i in range(n)])  27.2 us
    ppermute x6, starting transfers between devices, exchange(): lax.ppermute(out, axis, [(i, (i + step) % n) for i in range(n)])  25.3 us
    all_to_all x1, blocking collectives, per_device(): lax.all_to_all(scores, ('x', 'y', 'zh', 'zl'), 0, 0, tiled=True).sum(0)  24.8 us
    ppermute x5, starting transfers between devices, swap(): return lax.ppermute(v, axis, [(0, 1), (1, 0)])  24.7 us
    all_to_all x1, waiting for transfers between devices, per_device(): got = lax.all_to_all(message, ('y', 'zh'), 0, 0, tiled=True)  15.2 us
    all_to_all x1, waiting for transfers between devices, per_device(): lax.all_to_all(a_out, ('y', 'x'), 0, 0, tiled=True)  11.6 us
    ppermute x3, starting transfers between devices, per_device(): lax.ppermute(pair, 'zh', [(i, (i + step) % H) for i in range(H)])  10.8 us
    all_to_all x1, starting transfers between devices, per_device(): got = lax.all_to_all(message, ('y', 'zh'), 0, 0, tiled=True)  10.3 us
  transfers between devices with their start and end apart: 18, of which 13 were waited for; matrix products, arithmetic and copies ran while one was open for 2% of the time, Pallas kernels for 0%

profile of v2, /device:TPU:1, one launch (start us, length us, event | category | flops | bytes accessed | tf_op | source)
XLA Modules:
  0.0 204.4 jit_solution(16828014764959492021)
XLA Ops:
  3.9 8.8 %collective-permute-start = (bf16[32,1280]{1,0:T(8,128)(2,1)S(1)}, bf16[32,1280]{1,0:T(8,128)(2,1)S(1)}, u32[]{:S(2)}, u32[]{:S(2)}) collective-permute-start(bf16[32,1280]{1,0:T(8,128)(2,1)S(1)} %get-tuple-element.21), channel_id=1, source_target_pairs={{0,1},{1,0},{2,3},{3,2},{4,5},{5,4},{6,7},{7,6},{8,9},{9,8},{10,11... | collective-permute-start | bytes 245768 | tf_op jit(solution)/shard_map/ppermute | solution.py:22
  14.5 10.3 %all-to-all-start = ((bf16[32,8,1280]{2,1,0:T(8,128)(2,1)}), bf16[32,8,1280]{2,1,0:T(8,128)(2,1)S(1)}, u32[]{:S(2)}, u32[]{:S(2)}) async-start(bf16[32,8,1280]{2,1,0:T(8,128)(2,1)} %bitcast.2), calls=%async_computation | async-start | bytes 1310720 | tf_op jit(solution)/shard_map/all_to_all | solution.py:283
  24.9 2.9 %fusion.27 = bf16[160,1280]{1,0:T(8,128)(2,1)S(1)} fusion(s32[]{:T(128)S(6)} %mul.19, s32[1280]{0:T(1024)S(1)} %get-tuple-element.45, s32[1280]{0:T(1024)S(1)} %get-tuple-element.48, s32[1280]{0:T(1024)S(1)} %get-tuple-element.46, s32[1280]{0:T(1024)S(1)} %get-tuple-element.47, pred[1280]{0:T(1024)(128)(4,1)S(1)} %get-tuple-element.49, ...), kind=kOutput, calls=%fused_computation.30 | convolution fusion | flops 1115955200 | bytes 1251844 | tf_op jit(solution)/shard_map/dot_general | solution.py:301
  29.6 15.2 %all-to-all-done = bf16[32,8,1280]{2,1,0:T(8,128)(2,1)S(1)} async-done(((bf16[32,8,1280]{2,1,0:T(8,128)(2,1)}), bf16[32,8,1280]{2,1,0:T(8,128)(2,1)S(1)}, u32[]{:S(2)}, u32[]{:S(2)}) %all-to-all-start) | async-done | bytes 655392 | tf_op jit(solution)/shard_map/all_to_all | solution.py:283
  46.9 4.0 %all-to-all-start.1 = ((bf16[4,400,768]{2,1,0:T(8,128)(2,1)}), bf16[4,400,768]{2,1,0:T(8,128)(2,1)S(1)}, u32[]{:S(2)}, u32[]{:S(2)}) async-start(bf16[4,400,768]{2,1,0:T(8,128)(2,1)} %copy-done), calls=%async_computation.1 | async-start | bytes 4915200 | tf_op jit(solution)/shard_map/all_to_all | solution.py:311
  50.9 4.6 %collective-permute-start.3 = (bf16[112,640]{1,0:T(8,128)(2,1)S(1)}, bf16[112,640]{1,0:T(8,128)(2,1)S(1)}, u32[]{:S(2)}, u32[]{:S(2)}) collective-permute-start(bf16[112,640]{1,0:T(8,128)(2,1)S(1)} %get-tuple-element.38), channel_id=1, source_target_pairs={{0,12},{4,0},{8,4},{12,8},{1,13},{5,1},{9,5},{13,9},{2,14},{6,2},{... | collective-permute-start | bytes 430088 | tf_op jit(solution)/shard_map/ppermute | solution.py:31
  55.5 3.8 %collective-permute-start.2 = (bf16[112,640]{1,0:T(8,128)(2,1)S(1)}, bf16[112,640]{1,0:T(8,128)(2,1)S(1)}, u32[]{:S(2)}, u32[]{:S(2)}) collective-permute-start(bf16[112,640]{1,0:T(8,128)(2,1)S(1)} %get-tuple-element.39), channel_id=1, source_target_pairs={{0,8},{4,12},{8,0},{12,4},{1,9},{5,13},{9,1},{13,5},{2,10},{6,14},... | collective-permute-start | bytes 430088 | tf_op jit(solution)/shard_map/ppermute | solution.py:31
  59.3 3.5 %collective-permute-start.1 = (bf16[112,640]{1,0:T(8,128)(2,1)S(1)}, bf16[112,640]{1,0:T(8,128)(2,1)S(1)}, u32[]{:S(2)}, u32[]{:S(2)}) collective-permute-start(bf16[112,640]{1,0:T(8,128)(2,1)S(1)} %get-tuple-element.40), channel_id=1, source_target_pairs={{0,4},{4,8},{8,12},{12,0},{1,5},{5,9},{9,13},{13,1},{2,6},{6,10},{... | collective-permute-start | bytes 430088 | tf_op jit(solution)/shard_map/ppermute | solution.py:31
  62.8 3.1 %collective-permute-done.2 = bf16[112,640]{1,0:T(8,128)(2,1)S(1)} collective-permute-done((bf16[112,640]{1,0:T(8,128)(2,1)S(1)}, bf16[112,640]{1,0:T(8,128)(2,1)S(1)}, u32[]{:S(2)}, u32[]{:S(2)}) %collective-permute-start.2) | collective-permute-done | bytes 143392 | tf_op jit(solution)/shard_map/ppermute | solution.py:31
  66.0 4.1 %collective-permute-done.1 = bf16[112,640]{1,0:T(8,128)(2,1)S(1)} collective-permute-done((bf16[112,640]{1,0:T(8,128)(2,1)S(1)}, bf16[112,640]{1,0:T(8,128)(2,1)S(1)}, u32[]{:S(2)}, u32[]{:S(2)}) %collective-permute-start.1) | collective-permute-done | bytes 143392 | tf_op jit(solution)/shard_map/ppermute | solution.py:31
  70.1 4.1 %collective-permute-start.4 = (bf16[4,112,640]{2,1,0:T(8,128)(2,1)S(1)}, bf16[4,112,640]{2,1,0:T(8,128)(2,1)S(1)}, u32[]{:S(2)}, u32[]{:S(2)}) collective-permute-start(bf16[4,112,640]{2,1,0:T(8,128)(2,1)S(1)} %pad_maximum_fusion.1.own_ref), channel_id=1, source_target_pairs={{0,1},{1,0},{2,3},{3,2},{4,5},{5,4},{6,7},{7,6},{8,9},{9,8},{10,11... | collective-permute-start | bytes 1720328 | tf_op jit(solution)/shard_map/ppermute | solution.py:22
  74.2 1.6 collective-permute-done.4.other_ref
  76.6 2.1 %all-to-all-done.1.full_ref = bf16[4,400,768]{2,1,0:T(8,128)(2,1)S(1)} async-done(((bf16[4,400,768]{2,1,0:T(8,128)(2,1)}), bf16[4,400,768]{2,1,0:T(8,128)(2,1)S(1)}, u32[]{:S(2)}, u32[]{:S(2)}) %all-to-all-start.1) | async-done | bytes 2457632 | tf_op jit(solution)/shard_map/all_to_all | solution.py:311
  79.8 2.3 %shard_map.84 = bf16[8,128,512]{2,1,0:T(8,128)(2,1)} custom-call(bf16[4,400,768]{2,1,0:T(8,128)(2,1)S(1)} %all-to-all-done.1.full_ref, bf16[4,112,640]{2,1,0:T(8,128)(2,1)S(1)} %pad_maximum_fusion.1.own_ref, bf16[4,112,640]{2,1,0:T(8,128)(2,1)S(1)} %copy-done.2), custom_call_target="tpu_custom_call" | custom-call | tf_op jit(solution)/shard_map/pallas_call | solution.py:249
  82.1 5.5 %all-to-all-start.2 = ((bf16[8,128,512]{2,1,0:T(8,128)(2,1)}), bf16[8,128,512]{2,1,0:T(8,128)(2,1)S(1)}, u32[]{:S(2)}, u32[]{:S(2)}) async-start(bf16[8,128,512]{2,1,0:T(8,128)(2,1)} %shard_map.84), calls=%async_computation.2 | async-start | bytes 2097152 | tf_op jit(solution)/shard_map/all_to_all | solution.py:323
  87.7 5.5 %collective-permute-start.7 = (bf16[80,640]{1,0:T(8,128)(2,1)S(1)}, bf16[80,640]{1,0:T(8,128)(2,1)S(1)}, u32[]{:S(2)}, u32[]{:S(2)}) collective-permute-start(bf16[80,640]{1,0:T(8,128)(2,1)S(1)} %get-tuple-element.42), channel_id=1, source_target_pairs={{0,12},{4,0},{8,4},{12,8},{1,13},{5,1},{9,5},{13,9},{2,14},{6,2},{... | collective-permute-start | bytes 307208 | tf_op jit(solution)/shard_map/ppermute | solution.py:31
  93.2 4.0 %collective-permute-start.6 = (bf16[80,640]{1,0:T(8,128)(2,1)S(1)}, bf16[80,640]{1,0:T(8,128)(2,1)S(1)}, u32[]{:S(2)}, u32[]{:S(2)}) collective-permute-start(bf16[80,640]{1,0:T(8,128)(2,1)S(1)} %get-tuple-element.43), channel_id=1, source_target_pairs={{0,8},{4,12},{8,0},{12,4},{1,9},{5,13},{9,1},{13,5},{2,10},{6,14},... | collective-permute-start | bytes 307208 | tf_op jit(solution)/shard_map/ppermute | solution.py:31
  97.2 4.0 %collective-permute-start.5 = (bf16[80,640]{1,0:T(8,128)(2,1)S(1)}, bf16[80,640]{1,0:T(8,128)(2,1)S(1)}, u32[]{:S(2)}, u32[]{:S(2)}) collective-permute-start(bf16[80,640]{1,0:T(8,128)(2,1)S(1)} %get-tuple-element.44), channel_id=1, source_target_pairs={{0,4},{4,8},{8,12},{12,0},{1,5},{5,9},{9,13},{13,1},{2,6},{6,10},{... | collective-permute-start | bytes 307208 | tf_op jit(solution)/shard_map/ppermute | solution.py:31
  101.2 6.0 %collective-permute-done.7 = bf16[80,640]{1,0:T(8,128)(2,1)S(1)} collective-permute-done((bf16[80,640]{1,0:T(8,128)(2,1)S(1)}, bf16[80,640]{1,0:T(8,128)(2,1)S(1)}, u32[]{:S(2)}, u32[]{:S(2)}) %collective-permute-start.7) | collective-permute-done | bytes 102432 | tf_op jit(solution)/shard_map/ppermute | solution.py:31
  107.2 13.2 %collective-permute-done.6 = bf16[80,640]{1,0:T(8,128)(2,1)S(1)} collective-permute-done((bf16[80,640]{1,0:T(8,128)(2,1)S(1)}, bf16[80,640]{1,0:T(8,128)(2,1)S(1)}, u32[]{:S(2)}, u32[]{:S(2)}) %collective-permute-start.6) | collective-permute-done | bytes 102432 | tf_op jit(solution)/shard_map/ppermute | solution.py:31
  122.3 8.5 %all-to-all-start.3 = ((bf16[32,16,512]{2,1,0:T(8,128)(2,1)}), bf16[32,16,512]{2,1,0:T(8,128)(2,1)S(1)}, u32[]{:S(2)}, u32[]{:S(2)}) async-start(bf16[32,16,512]{2,1,0:T(8,128)(2,1)} %get-tuple-element.32), calls=%async_computation.3 | async-start | bytes 1048576 | tf_op jit(solution)/shard_map/all_to_all | solution.py:331
  130.7 3.6 %collective-permute-start.9 = (bf16[80,384]{1,0:T(8,128)(2,1)S(1)}, bf16[80,384]{1,0:T(8,128)(2,1)S(1)}, u32[]{:S(2)}, u32[]{:S(2)}) collective-permute-start(bf16[80,384]{1,0:T(8,128)(2,1)S(1)} %get-tuple-element.33), channel_id=1, source_target_pairs={{0,2},{2,0},{1,3},{3,1},{4,6},{6,4},{5,7},{7,5},{8,10},{10,8},{9,1... | collective-permute-start | bytes 184328 | tf_op jit(solution)/shard_map/ppermute | solution.py:22
  134.4 11.6 %all-to-all-done.3 = bf16[32,16,512]{2,1,0:T(8,128)(2,1)S(1)} async-done(((bf16[32,16,512]{2,1,0:T(8,128)(2,1)}), bf16[32,16,512]{2,1,0:T(8,128)(2,1)S(1)}, u32[]{:S(2)}, u32[]{:S(2)}) %all-to-all-start.3) | async-done | bytes 524320 | tf_op jit(solution)/shard_map/all_to_all | solution.py:331
  146.0 5.5 %collective-permute-start.8 = (bf16[512,512]{1,0:T(8,128)(2,1)S(1)}, bf16[512,512]{1,0:T(8,128)(2,1)S(1)}, u32[]{:S(2)}, u32[]{:S(2)}) collective-permute-start(bf16[512,512]{1,0:T(8,128)(2,1)S(1)} %bitcast.42), channel_id=1, source_target_pairs={{0,1},{1,0},{2,3},{3,2},{4,5},{5,4},{6,7},{7,6},{8,9},{9,8},{10,11... | collective-permute-start | bytes 1572872 | tf_op jit(solution)/shard_map/ppermute | solution.py:22
  151.5 4.6 %collective-permute-start.12 = (bf16[2,80,384]{2,1,0:T(8,128)(2,1)S(1)}, bf16[2,80,384]{2,1,0:T(8,128)(2,1)S(1)}, u32[]{:S(2)}, u32[]{:S(2)}) collective-permute-start(bf16[2,80,384]{2,1,0:T(8,128)(2,1)S(1)} %pad_maximum_fusion.4.g0_ref), channel_id=1, source_target_pairs={{0,12},{4,0},{8,4},{12,8},{1,13},{5,1},{9,5},{13,9},{2,14},{6,2},{... | collective-permute-start | bytes 368648 | tf_op jit(solution)/shard_map/ppermute | solution.py:335
  156.1 2.4 %collective-permute-start.11 = (bf16[2,80,384]{2,1,0:T(8,128)(2,1)S(1)}, bf16[2,80,384]{2,1,0:T(8,128)(2,1)S(1)}, u32[]{:S(2)}, u32[]{:S(2)}) collective-permute-start(bf16[2,80,384]{2,1,0:T(8,128)(2,1)S(1)} %pad_maximum_fusion.4.g0_ref), channel_id=1, source_target_pairs={{0,8},{4,12},{8,0},{12,4},{1,9},{5,13},{9,1},{13,5},{2,10},{6,14},... | collective-permute-start | bytes 368648 | tf_op jit(solution)/shard_map/ppermute | solution.py:335
  158.6 3.7 %collective-permute-start.10 = (bf16[2,80,384]{2,1,0:T(8,128)(2,1)S(1)}, bf16[2,80,384]{2,1,0:T(8,128)(2,1)S(1)}, u32[]{:S(2)}, u32[]{:S(2)}) collective-permute-start(bf16[2,80,384]{2,1,0:T(8,128)(2,1)S(1)} %pad_maximum_fusion.4.g0_ref), channel_id=1, source_target_pairs={{0,4},{4,8},{8,12},{12,0},{1,5},{5,9},{9,13},{13,1},{2,6},{6,10},{... | collective-permute-start | bytes 368648 | tf_op jit(solution)/shard_map/ppermute | solution.py:335
  162.3 4.9 %collective-permute-done.11.g2_ref = bf16[2,80,384]{2,1,0:T(8,128)(2,1)S(1)} collective-permute-done((bf16[2,80,384]{2,1,0:T(8,128)(2,1)S(1)}, bf16[2,80,384]{2,1,0:T(8,128)(2,1)S(1)}, u32[]{:S(2)}, u32[]{:S(2)}) %collective-permute-start.11) | collective-permute-done | bytes 122912 | tf_op jit(solution)/shard_map/ppermute | solution.py:335
  167.2 3.1 %collective-permute-done.10.g1_ref = bf16[2,80,384]{2,1,0:T(8,128)(2,1)S(1)} collective-permute-done((bf16[2,80,384]{2,1,0:T(8,128)(2,1)S(1)}, bf16[2,80,384]{2,1,0:T(8,128)(2,1)S(1)}, u32[]{:S(2)}, u32[]{:S(2)}) %collective-permute-start.10) | collective-permute-done | bytes 122912 | tf_op jit(solution)/shard_map/ppermute | solution.py:335
  170.4 2.8 %collective-permute-start.13 = (bf16[8,80,128]{2,1,0:T(8,128)(2,1)S(1)}, bf16[8,80,128]{2,1,0:T(8,128)(2,1)S(1)}, u32[]{:S(2)}, u32[]{:S(2)}) collective-permute-start(bf16[8,80,128]{2,1,0:T(8,128)(2,1)S(1)} %pad_maximum_fusion.3), channel_id=1, source_target_pairs={{0,1},{1,0},{2,3},{3,2},{4,5},{5,4},{6,7},{7,6},{8,9},{9,8},{10,11... | collective-permute-start | bytes 491528 | tf_op jit(solution)/shard_map/ppermute | solution.py:22
  174.0 4.4 %shard_map.86 = f32[8,512]{1,0:T(8,128)S(1)} custom-call(bf16[512,512]{1,0:T(8,128)(2,1)S(1)} %bitcast.43, bf16[512,512]{1,0:T(8,128)(2,1)S(1)} %collective-permute-done.8.ao_ref, bf16[2,80,384]{2,1,0:T(8,128)(2,1)S(1)} %pad_maximum_fusion.4.g0_ref, bf16[2,80,384]{2,1,0:T(8,128)(2,1)S(1)} %collective-permute-done.10.g1_ref, ...), custom_call_target="tpu_custom_call" | custom-call | tf_op jit(solution)/shard_map/pallas_call | solution.py:249
  178.6 24.8 %all_to_all.29 = f32[256,1,16]{2,1,0:T(1,128)S(1)} all-to-all(f32[256,1,16]{2,1,0:T(1,128)S(1)} %bitcast.51), channel_id=1, replica_groups=mesh['y'=8,'x'=4,'zh'=4,'zl'=2,'c'=2] {'x','y','zh','zl'}, dimensions={0} | all-to-all | bytes 32768 | tf_op jit(solution)/shard_map/all_to_all | solution.py:345
  (65 shorter events, 15.5 us)
Async XLA Ops:
  0.0 0.8 copy-start.3
  0.8 0.7 copy-start.4
  1.5 0.7 copy-start.5
  2.2 0.7 copy-start.6
  2.9 0.7 copy-start.7
  3.6 21.2 %copy-start.8 = (f32[80,2560]{1,0:T(8,128)S(1)}, f32[80,2560]{1,0:T(8,128)}, u32[]{:S(2)}) copy-start(f32[80,2560]{1,0:T(8,128)} %param.15) | copy-start | bytes 2457604
  3.9 9.7 %collective-permute-start = (bf16[32,1280]{1,0:T(8,128)(2,1)S(1)}, bf16[32,1280]{1,0:T(8,128)(2,1)S(1)}, u32[]{:S(2)}, u32[]{:S(2)}) collective-permute-start(bf16[32,1280]{1,0:T(8,128)(2,1)S(1)} %get-tuple-element.21), channel_id=1, source_target_pairs={{0,1},{1,0},{2,3},{3,2},{4,5},{5,4},{6,7},{7,6},{8,9},{9,8},{10,11... | collective-permute-start | bytes 245768 | tf_op jit(solution)/shard_map/ppermute | solution.py:22
  14.5 30.3 %all-to-all-start = ((bf16[32,8,1280]{2,1,0:T(8,128)(2,1)}), bf16[32,8,1280]{2,1,0:T(8,128)(2,1)S(1)}, u32[]{:S(2)}, u32[]{:S(2)}) async-start(bf16[32,8,1280]{2,1,0:T(8,128)(2,1)} %bitcast.2), calls=%async_computation | async-start | bytes 1310720 | tf_op jit(solution)/shard_map/all_to_all | solution.py:283
  24.9 3.0 %copy-start.10 = (bf16[640,20]{0,1:T(8,128)(2,1)S(1)}, bf16[640,20]{0,1:T(8,128)(2,1)}, u32[]{:S(2)}) copy-start(bf16[640,20]{0,1:T(8,128)(2,1)} %param.14) | copy-start | bytes 76804
  24.9 3.2 %copy-start.9 = (bf16[2560,80]{0,1:T(8,128)(2,1)S(1)}, bf16[2560,80]{0,1:T(8,128)(2,1)}, u32[]{:S(2)}) copy-start(bf16[2560,80]{0,1:T(8,128)(2,1)} %param.13) | copy-start | bytes 1228804
  45.4 1.5 copy-start
  46.9 31.9 %all-to-all-start.1 = ((bf16[4,400,768]{2,1,0:T(8,128)(2,1)}), bf16[4,400,768]{2,1,0:T(8,128)(2,1)S(1)}, u32[]{:S(2)}, u32[]{:S(2)}) async-start(bf16[4,400,768]{2,1,0:T(8,128)(2,1)} %copy-done), calls=%async_computation.1 | async-start | bytes 4915200 | tf_op jit(solution)/shard_map/all_to_all | solution.py:311
  50.9 11.9 %collective-permute-start.3 = (bf16[112,640]{1,0:T(8,128)(2,1)S(1)}, bf16[112,640]{1,0:T(8,128)(2,1)S(1)}, u32[]{:S(2)}, u32[]{:S(2)}) collective-permute-start(bf16[112,640]{1,0:T(8,128)(2,1)S(1)} %get-tuple-element.38), channel_id=1, source_target_pairs={{0,12},{4,0},{8,4},{12,8},{1,13},{5,1},{9,5},{13,9},{2,14},{6,2},{... | collective-permute-start | bytes 430088 | tf_op jit(solution)/shard_map/ppermute | solution.py:31
  55.5 10.5 %collective-permute-start.2 = (bf16[112,640]{1,0:T(8,128)(2,1)S(1)}, bf16[112,640]{1,0:T(8,128)(2,1)S(1)}, u32[]{:S(2)}, u32[]{:S(2)}) collective-permute-start(bf16[112,640]{1,0:T(8,128)(2,1)S(1)} %get-tuple-element.39), channel_id=1, source_target_pairs={{0,8},{4,12},{8,0},{12,4},{1,9},{5,13},{9,1},{13,5},{2,10},{6,14},... | collective-permute-start | bytes 430088 | tf_op jit(solution)/shard_map/ppermute | solution.py:31
  59.3 10.8 %collective-permute-start.1 = (bf16[112,640]{1,0:T(8,128)(2,1)S(1)}, bf16[112,640]{1,0:T(8,128)(2,1)S(1)}, u32[]{:S(2)}, u32[]{:S(2)}) collective-permute-start(bf16[112,640]{1,0:T(8,128)(2,1)S(1)} %get-tuple-element.40), channel_id=1, source_target_pairs={{0,4},{4,8},{8,12},{12,0},{1,5},{5,9},{9,13},{13,1},{2,6},{6,10},{... | collective-permute-start | bytes 430088 | tf_op jit(solution)/shard_map/ppermute | solution.py:31
  70.1 5.7 %collective-permute-start.4 = (bf16[4,112,640]{2,1,0:T(8,128)(2,1)S(1)}, bf16[4,112,640]{2,1,0:T(8,128)(2,1)S(1)}, u32[]{:S(2)}, u32[]{:S(2)}) collective-permute-start(bf16[4,112,640]{2,1,0:T(8,128)(2,1)S(1)} %pad_maximum_fusion.1.own_ref), channel_id=1, source_target_pairs={{0,1},{1,0},{2,3},{3,2},{4,5},{5,4},{6,7},{7,6},{8,9},{9,8},{10,11... | collective-permute-start | bytes 1720328 | tf_op jit(solution)/shard_map/ppermute | solution.py:22
  75.8 0.8 copy-start.1
  78.8 1.1 copy-start.2
  82.1 39.1 %all-to-all-start.2 = ((bf16[8,128,512]{2,1,0:T(8,128)(2,1)}), bf16[8,128,512]{2,1,0:T(8,128)(2,1)S(1)}, u32[]{:S(2)}, u32[]{:S(2)}) async-start(bf16[8,128,512]{2,1,0:T(8,128)(2,1)} %shard_map.84), calls=%async_computation.2 | async-start | bytes 2097152 | tf_op jit(solution)/shard_map/all_to_all | solution.py:323
  87.7 19.5 %collective-permute-start.7 = (bf16[80,640]{1,0:T(8,128)(2,1)S(1)}, bf16[80,640]{1,0:T(8,128)(2,1)S(1)}, u32[]{:S(2)}, u32[]{:S(2)}) collective-permute-start(bf16[80,640]{1,0:T(8,128)(2,1)S(1)} %get-tuple-element.42), channel_id=1, source_target_pairs={{0,12},{4,0},{8,4},{12,8},{1,13},{5,1},{9,5},{13,9},{2,14},{6,2},{... | collective-permute-start | bytes 307208 | tf_op jit(solution)/shard_map/ppermute | solution.py:31
  93.2 27.2 %collective-permute-start.6 = (bf16[80,640]{1,0:T(8,128)(2,1)S(1)}, bf16[80,640]{1,0:T(8,128)(2,1)S(1)}, u32[]{:S(2)}, u32[]{:S(2)}) collective-permute-start(bf16[80,640]{1,0:T(8,128)(2,1)S(1)} %get-tuple-element.43), channel_id=1, source_target_pairs={{0,8},{4,12},{8,0},{12,4},{1,9},{5,13},{9,1},{13,5},{2,10},{6,14},... | collective-permute-start | bytes 307208 | tf_op jit(solution)/shard_map/ppermute | solution.py:31
  97.2 24.0 %collective-permute-start.5 = (bf16[80,640]{1,0:T(8,128)(2,1)S(1)}, bf16[80,640]{1,0:T(8,128)(2,1)S(1)}, u32[]{:S(2)}, u32[]{:S(2)}) collective-permute-start(bf16[80,640]{1,0:T(8,128)(2,1)S(1)} %get-tuple-element.44), channel_id=1, source_target_pairs={{0,4},{4,8},{8,12},{12,0},{1,5},{5,9},{9,13},{13,1},{2,6},{6,10},{... | collective-permute-start | bytes 307208 | tf_op jit(solution)/shard_map/ppermute | solution.py:31
  122.3 23.7 %all-to-all-start.3 = ((bf16[32,16,512]{2,1,0:T(8,128)(2,1)}), bf16[32,16,512]{2,1,0:T(8,128)(2,1)S(1)}, u32[]{:S(2)}, u32[]{:S(2)}) async-start(bf16[32,16,512]{2,1,0:T(8,128)(2,1)} %get-tuple-element.32), calls=%async_computation.3 | async-start | bytes 1048576 | tf_op jit(solution)/shard_map/all_to_all | solution.py:331
  130.7 20.7 %collective-permute-start.9 = (bf16[80,384]{1,0:T(8,128)(2,1)S(1)}, bf16[80,384]{1,0:T(8,128)(2,1)S(1)}, u32[]{:S(2)}, u32[]{:S(2)}) collective-permute-start(bf16[80,384]{1,0:T(8,128)(2,1)S(1)} %get-tuple-element.33), channel_id=1, source_target_pairs={{0,2},{2,0},{1,3},{3,1},{4,6},{6,4},{5,7},{7,5},{8,10},{10,8},{9,1... | collective-permute-start | bytes 184328 | tf_op jit(solution)/shard_map/ppermute | solution.py:22
  146.0 28.0 %collective-permute-start.8 = (bf16[512,512]{1,0:T(8,128)(2,1)S(1)}, bf16[512,512]{1,0:T(8,128)(2,1)S(1)}, u32[]{:S(2)}, u32[]{:S(2)}) collective-permute-start(bf16[512,512]{1,0:T(8,128)(2,1)S(1)} %bitcast.42), channel_id=1, source_target_pairs={{0,1},{1,0},{2,3},{3,2},{4,5},{5,4},{6,7},{7,6},{8,9},{9,8},{10,11... | collective-permute-start | bytes 1572872 | tf_op jit(solution)/shard_map/ppermute | solution.py:22
  151.5 10.8 %collective-permute-start.12 = (bf16[2,80,384]{2,1,0:T(8,128)(2,1)S(1)}, bf16[2,80,384]{2,1,0:T(8,128)(2,1)S(1)}, u32[]{:S(2)}, u32[]{:S(2)}) collective-permute-start(bf16[2,80,384]{2,1,0:T(8,128)(2,1)S(1)} %pad_maximum_fusion.4.g0_ref), channel_id=1, source_target_pairs={{0,12},{4,0},{8,4},{12,8},{1,13},{5,1},{9,5},{13,9},{2,14},{6,2},{... | collective-permute-start | bytes 368648 | tf_op jit(solution)/shard_map/ppermute | solution.py:335
  156.1 11.1 %collective-permute-start.11 = (bf16[2,80,384]{2,1,0:T(8,128)(2,1)S(1)}, bf16[2,80,384]{2,1,0:T(8,128)(2,1)S(1)}, u32[]{:S(2)}, u32[]{:S(2)}) collective-permute-start(bf16[2,80,384]{2,1,0:T(8,128)(2,1)S(1)} %pad_maximum_fusion.4.g0_ref), channel_id=1, source_target_pairs={{0,8},{4,12},{8,0},{12,4},{1,9},{5,13},{9,1},{13,5},{2,10},{6,14},... | collective-permute-start | bytes 368648 | tf_op jit(solution)/shard_map/ppermute | solution.py:335
  158.6 11.8 %collective-permute-start.10 = (bf16[2,80,384]{2,1,0:T(8,128)(2,1)S(1)}, bf16[2,80,384]{2,1,0:T(8,128)(2,1)S(1)}, u32[]{:S(2)}, u32[]{:S(2)}) collective-permute-start(bf16[2,80,384]{2,1,0:T(8,128)(2,1)S(1)} %pad_maximum_fusion.4.g0_ref), channel_id=1, source_target_pairs={{0,4},{4,8},{8,12},{12,0},{1,5},{5,9},{9,13},{13,1},{2,6},{6,10},{... | collective-permute-start | bytes 368648 | tf_op jit(solution)/shard_map/ppermute | solution.py:335
  170.4 3.6 %collective-permute-start.13 = (bf16[8,80,128]{2,1,0:T(8,128)(2,1)S(1)}, bf16[8,80,128]{2,1,0:T(8,128)(2,1)S(1)}, u32[]{:S(2)}, u32[]{:S(2)}) collective-permute-start(bf16[8,80,128]{2,1,0:T(8,128)(2,1)S(1)} %pad_maximum_fusion.3), channel_id=1, source_target_pairs={{0,1},{1,0},{2,3},{3,2},{4,5},{5,4},{6,7},{7,6},{8,9},{9,8},{10,11... | collective-permute-start | bytes 491528 | tf_op jit(solution)/shard_map/ppermute | solution.py:22

commit v3 on v2

--- a/solution.py
+++ b/solution.py
@@ -22,14 +22,10 @@
     return lax.ppermute(v, axis, [(0, 1), (1, 0)])
 
 
-def exchange(pieces, axis):
+def exchange(pieces, axis, step):
     n = lax.axis_size(axis)
-    me = lax.axis_index(axis)
-    received = [lax.dynamic_index_in_dim(pieces, me, 0, keepdims=False)]
-    for step in range(1, n):
-        out = lax.dynamic_index_in_dim(pieces, (me + step) % n, 0, keepdims=False)
-        received.append(lax.ppermute(out, axis, [(i, (i + step) % n) for i in range(n)]))
-    return received
+    out = lax.dynamic_index_in_dim(pieces, (lax.axis_index(axis) + step) % n, 0, keepdims=False)
+    return out if step == 0 else lax.ppermute(out, axis, [(i, (i + step) % n) for i in range(n)])
 
 
 def iota(shape, dim):
@@ -119,30 +115,33 @@
     tail = jnp.concatenate([train[:, width:], q_b], 0)
     rows = tail.shape[0] // 4
     packed = sum(lanes(tail[g * rows:(g + 1) * rows], 32 * g, 32 * g, 32 * g + 32) for g in range(4)).astype(BF)
-    tiles = width // LANES
-    per = rows // tiles
-    packed = jnp.concatenate([packed[k * per:(k + 1) * per] for k in range(tiles)], 1)
+    packed = jnp.concatenate([packed[k:k + 16] for k in range(0, rows, 16)], 1)
     for x in range(out_ref.shape[0]):
         out_ref[x, :n + qn] = body
-        out_ref[x, n + qn:] = packed
-
-
-def rotate_kernel(full_ref, own_ref, other_ref, out_ref, *, X, H, L, tt, tq, gs, f_own):
+        out_ref[x, n + qn:, :packed.shape[1]] = packed
+
+
+def rotate_kernel(full_ref, own_ref, other_ref, out_ref, *, H, L, tt, tq, gs, f_own, d_part):
     me = lax.axis_index("zh")
     per = 2 * (tt + tq)
-    inner = X // L
+    inner = full_ref.shape[0] // L
     wt, wq = inner * tt, inner * tq
-    tiles = gs // LANES + 1
     group = per // 4
-    fine = group // tiles
-    grads = [jnp.concatenate([b[s, :f_own] for s in range(H)], 0) for b in (own_ref, other_ref)]
-    acts = [jnp.concatenate([b[s, f_own:, :2 * LANES] for s in range(H)], 0) for b in (own_ref, other_ref)]
+    grads = [jnp.concatenate([b[s, :f_own, :gs] for s in range(H)], 0) for b in (own_ref, other_ref)]
+    acts = [
+        jnp.concatenate([b[s, f_own:, k * 2 * LANES:(k + 1) * 2 * LANES] for s in range(H) for k in range(L)], 0)
+        for b in (own_ref, other_ref)
+    ]
+    r, c = iota((H * L * 32, H * L * 16), 0), iota((H * L * 32, H * L * 16), 1)
+    repeat = ((r % 32 < (L + 1) * d_part) & (c == (r // 32) * 16 + (r % 32) % d_part)).astype(BF)
+    acts = [matmul(repeat, v).astype(BF) for v in acts]
+    a_parts = []
     for l in range(L):
         blocks = []
         for x in range(inner):
             at = l * inner + x
             packed = jnp.concatenate(
-                [full_ref[at, per:, k * LANES:(k + 1) * LANES].astype(F32) for k in range(tiles)], 0
+                [full_ref[at, per:, k * LANES:(k + 1) * LANES].astype(F32) for k in range(group // 16)], 0
             )
             tail = jnp.concatenate([lanes(packed, -32 * g, 0, 32) for g in range(4)], 0).astype(BF)
             blocks.append((full_ref.at[at], tail))
@@ -155,24 +154,25 @@
             )
             g += lax.dot_general(grads[s], tokens, (((1,), (1,)), ((), ())), preferred_element_type=F32)
             a += lax.dot_general(acts[s], inputs, (((1,), (1,)), ((), ())), preferred_element_type=F32)
+        a_parts.append(a)
         g_high, g_low = high_low(g[:, wt:])
         g_train = g[:, :wt].astype(BF)
-        a_high, a_low = high_low(a)
         for s in range(H):
-            h = lax.rem(me - s + H, H)
-            m = h * L + l
+            m = lax.rem(me - s + H, H) * L + l
             out_ref[m, :f_own, :wt] = g_train[s * f_own:(s + 1) * f_own]
             out_ref[m, :f_own, wt:wt + wq] = g_high[s * f_own:(s + 1) * f_own]
             out_ref[m, :f_own, wt + wq:] = g_low[s * f_own:(s + 1) * f_own]
-            for k in range(L):
-                m = h * L + k
-                r = slice((s * L + k) * 16, (s * L + k) * 16 + 16)
-                at = f_own + 16 * l
-                out_ref[m, at:at + 16, :wt] = a_high[r, :wt]
-                out_ref[m, at:at + 16, wt:] = a_low[r, :wt]
-                at = f_own + 16 * L
-                out_ref[m, at:at + 16, l * 2 * wq:l * 2 * wq + wq] = a_high[r, wt:]
-                out_ref[m, at:at + 16, l * 2 * wq + wq:(l + 1) * 2 * wq] = a_low[r, wt:]
+    merged = jnp.concatenate([a[:, wt:] for a in a_parts], 1)
+    kind = (iota(merged.shape, 0) % 32) // d_part
+    for l in range(L):
+        merged = jnp.where(kind == l, a_parts[l][:, :wt], merged)
+    a_high, a_low = high_low(merged)
+    for s in range(H):
+        for k in range(L):
+            m = lax.rem(me - s + H, H) * L + k
+            r = slice((s * L + k) * 32, (s * L + k + 1) * 32)
+            out_ref[m, f_own:, :wt] = a_high[r]
+            out_ref[m, f_own:, wt:] = a_low[r]
 
 
 def combine_kernel(parts_ref, g_ref, a_ref, *, n, f_own, L, wt, wq, d_part):
@@ -183,12 +183,11 @@
     g_query = (total[:f_own, wt:wt + wq] + total[:f_own, wt + wq:]).astype(BF)
     g_ref[:, :wt] = g_train
     g_ref[:, wt:] = g_query
-    a_train = [total[f_own + 16 * l:f_own + 16 * l + 16] for l in range(L)]
-    a_train = jnp.concatenate([t[:, :wt] + t[:, wt:] for t in a_train], 1)
-    last = total[f_own + 16 * L:]
-    a_query = jnp.concatenate(
-        [last[:, l * 2 * wq:l * 2 * wq + wq] + last[:, l * 2 * wq + wq:(l + 1) * 2 * wq] for l in range(L)], 1
-    ).astype(BF)
+    act = total[f_own:, :wt] + total[f_own:, wt:]
+    inside = iota((16, wt), 0) < d_part
+    kinds = [jnp.where(inside, (pltpu.roll(act, 32 - k * d_part, 0) if k else act)[:16], 0.0) for k in range(L + 1)]
+    a_train = jnp.concatenate(kinds[:L], 1)
+    a_query = kinds[L].astype(BF)
     half = d_part // 2
     r = lax.broadcasted_iota(jnp.int32, (16, 16), 0)
     c = lax.broadcasted_iota(jnp.int32, (16, 16), 1)
@@ -203,10 +202,9 @@
 
 
 def score_kernel(
-    a_ref, ao_ref, g0_ref, g1_ref, g2_ref, g3_ref, go_ref, inv_ref, out_ref, *, Y, L, wt, wq, d_part, group
+    a_ref, ao_ref, g_ref, go_ref, inv_ref, invo_ref, out_ref, inv_acc, *, Y, YL, L, wt, wq, d_part, group, n_d
 ):
-    low = lax.axis_index("zl")
-    pieces = (g0_ref, g1_ref, g2_ref, g3_ref)
+    H, f_own, d_tile = g_ref.shape[0], g_ref.shape[2], n_d
     half = d_part // 2
     n = a_ref.shape[0]
     r, c = iota((n, n), 0), iota((n, n), 1)
@@ -220,22 +218,23 @@
         width = ref.shape[1] // 2
         return (matmul(unpack[0], ref[:, :width]) + matmul(unpack[1], ref[:, width:])).astype(BF)
 
-    def chunks(own, other):
-        return jnp.concatenate([jnp.where(low == 0, own, other), jnp.where(low == 0, other, own)], 1)
-
-    def grads(cols):
-        return chunks(*(jnp.concatenate([p[k, :, cols] for p in pieces], 0).astype(F32) for k in range(L)))
-
-    f_own = go_ref.shape[1]
-    theirs = [jnp.concatenate([go_ref[s * L + k] for s in range(len(pieces))], 0).astype(F32) for k in range(L)]
+    def grads(ref, cols):
+        return jnp.concatenate(
+            [jnp.concatenate([ref[h, k, :, cols] for h in range(H)], 0) for k in range(L)], 1
+        )
+
     qa = jnp.concatenate([query_acts(a_ref), query_acts(ao_ref)], 1)
-    qg = jnp.concatenate([grads(slice(wt, wt + wq)), chunks(*theirs)], 1).astype(BF)
-    g_train = grads(slice(0, wt))
-    d_tile = inv_ref.shape[1] // 2
+    qg = jnp.concatenate([grads(g_ref, slice(wt, wt + wq)), grads(go_ref, slice(0, wq))], 1)
+    g_train = grads(g_ref, slice(0, wt)).astype(F32)
     r, c = iota((d_tile, n), 0), iota((d_tile, n), 1)
     place = (c == (r // d_part) * 16 + r % d_part).astype(BF)
-    inv = matmul(inv_ref[:, :d_tile], place) + matmul(inv_ref[:, d_tile:], place)
-    owner = (iota(qg.shape, 1) // group) % Y
+    me = lax.axis_index("zh")
+    for s in range(H):
+        rows = pl.ds(pl.multiple_of(lax.rem(me - s + H, H) * f_own, f_own), f_own)
+        inv_acc[rows, :] = matmul(inv_ref[s, :f_own, -d_tile:], place) + matmul(invo_ref[s, :f_own, -d_tile:], place)
+    inv = inv_acc[...]
+    col = iota(qg.shape, 1)
+    owner = (col // group) % (Y // YL) * YL + (col // (group * (Y // YL))) % YL
     acts = a_ref[...]
     for q in range(Y):
         raw = lax.dot_general(
@@ -245,12 +244,24 @@
         out_ref[q:q + 1, :] = jnp.sum(mixed * g_train, axis=0, keepdims=True)
 
 
-def local_call(kernel, shapes, *args):
+def staged_call(kernel, shapes, *args):
+    whole = lambda v: pl.BlockSpec(v.shape, lambda i: (0,) * len(v.shape))
+    return pl.pallas_call(
+        kernel,
+        grid=(1,),
+        out_shape=shapes,
+        in_specs=[whole(v) for v in args],
+        out_specs=[whole(v) for v in shapes],
+    )(*args)
+
+
+def local_call(kernel, shapes, *args, scratch=()):
     return pl.pallas_call(
         kernel,
         out_shape=shapes,
         in_specs=[pl.BlockSpec(memory_space=pltpu.VMEM)] * len(args),
         out_specs=jax.tree.map(lambda _: pl.BlockSpec(memory_space=pltpu.VMEM), shapes),
+        scratch_shapes=scratch,
         compiler_params=pltpu.CompilerParams(vmem_limit_bytes=40 * 2**20),
     )(*args)
 
@@ -258,7 +269,8 @@
 def per_device(
     train_grads, train_acts, train_mask, query_grads, query_acts, grad_basis, act_basis, eigenvalues
 ):
-    Y, X, H, L, C = (lax.axis_size(a) for a in ("y", "x", "zh", "zl", "c"))
+    YH, YL, X, H, L, C = (lax.axis_size(a) for a in ("yh", "yl", "x", "zh", "zl", "c"))
+    Y = YH * YL
     low = lax.axis_index("zl")
     gk, f_own = grad_basis.shape
     ak, d_own = act_basis.shape
@@ -270,24 +282,25 @@
     d_part = d_block // (H * L)
     d_tile = d_part * X * Y
 
-    mine, theirs = local_call(
+    mine, theirs = staged_call(
         functools.partial(message_kernel, H=H, L=L, C=C),
         [jax.ShapeDtypeStruct((H * nt, 2 * gs), BF)] * 2,
         train_grads, train_acts, train_mask.reshape(1, nt), query_grads, query_acts,
     )
     message = mine + swap(theirs, "c")
-    message = jnp.broadcast_to(message.reshape(1, H, nt, 2 * gs), (Y, H, nt, 2 * gs)).reshape(Y * H, nt, 2 * gs)
+    message = jnp.broadcast_to(message.reshape(1, H, nt, 2 * gs), (YH, H, nt, 2 * gs)).reshape(YH * H, nt, 2 * gs)
     message, grad_basis, act_basis, eigenvalues = lax.optimization_barrier(
         (message, grad_basis, act_basis, eigenvalues)
     )
-    got = lax.all_to_all(message, ("y", "zh"), 0, 0, tiled=True)
+    got = lax.all_to_all(message, ("yh", "zh"), 0, 0, tiled=True)
 
     gb = grad_basis.T.reshape(f_own, H, gs).transpose(1, 0, 2)
     ab = act_basis.T
     main = ab[:, :H * LANES].reshape(d_own, H, LANES)
     rest = ab[:, H * LANES:].reshape(d_own, H, as_ - LANES)
-    ab = jnp.concatenate([main, rest], 2).transpose(1, 0, 2).reshape(H, L, d_part, as_)
-    ab = jnp.pad(ab, ((0, 0), (0, 0), (0, 16 - d_part), (0, gs - as_))).reshape(H, L * 16, gs)
+    ab = jnp.concatenate([main, rest], 2).reshape(L, d_part, H, as_).transpose(2, 1, 0, 3)
+    ab = jnp.pad(ab, ((0, 0), (0, 16 - d_part), (0, 0), (0, 2 * LANES - as_))).reshape(H, 16, L * 2 * LANES)
+    ab = jnp.pad(ab, ((0, 0), (0, 0), (0, gs - L * 2 * LANES)))
     pieces = jnp.concatenate([gb, ab], 1)
 
     inverse = 1.0 / (eigenvalues + damping)
@@ -298,66 +311,66 @@
 
     sel = (wanted(iota((d_all, H * d_tile), 1)) == iota((d_all, H * d_tile), 0)).astype(BF)
     inv_high, inv_low = high_low(inverse)
-    chosen = jnp.dot(jnp.concatenate([inv_high, inv_low], 0), sel, preferred_element_type=F32).astype(BF)
-    chosen = chosen.reshape(2, f_own, H, d_tile).transpose(2, 1, 0, 3).reshape(H, f_own, 2 * d_tile)
-    got, pieces, chosen = lax.optimization_barrier((got, pieces, chosen))
-
-    G = Y * H
+    half = jnp.where(lax.axis_index("c") == 0, inv_high, inv_low)
+    chosen = jnp.dot(half, sel, preferred_element_type=F32).astype(BF)
+    chosen = chosen.reshape(f_own, H, d_tile).transpose(1, 0, 2)
+    pieces = jnp.concatenate([pieces, jnp.pad(chosen, ((0, 0), (0, 16), (0, 0)))], 2)
+    got, pieces = lax.optimization_barrier((got, pieces))
+
+    G = YH * H
     block = local_call(
         functools.partial(shuffle_kernel, G=G, th=th, qh=qh, gs=gs),
-        jax.ShapeDtypeStruct((X, G * C * (th + qh) * 25 // 24, gs + LANES), BF),
+        jax.ShapeDtypeStruct((X * YL, G * C * (th + qh) + 16, gs + LANES), BF),
         got.reshape(G * nt, 2 * gs),
     )
-    full = lax.all_to_all(block, "x", 0, 0, tiled=True)
-    own = jnp.stack(exchange(pieces, "zh"))
+    full = lax.all_to_all(block, ("x", "yl"), 0, 0, tiled=True)
+    own = jnp.stack([exchange(pieces, "zh", k) for k in range(H)])
     other = swap(own, "c")
+    full, own, other = lax.optimization_barrier((full, own, other))
 
     tt, tq = G * th, G * qh
-    wt, wq = X // L * tt, X // L * tq
+    wt, wq = X // L * YL * tt, X // L * YL * tq
     parts = local_call(
-        functools.partial(rotate_kernel, X=X, H=H, L=L, tt=tt, tq=tq, gs=gs, f_own=f_own),
-        jax.ShapeDtypeStruct((H * L, f_own + 16 * L + 16, wt + 2 * wq), BF),
+        functools.partial(rotate_kernel, H=H, L=L, tt=tt, tq=tq, gs=gs, f_own=f_own, d_part=d_part),
+        jax.ShapeDtypeStruct((H * L, f_own + 32, wt + 2 * wq), BF),
         full, own, other,
     )
-    parts, chosen = lax.optimization_barrier((parts, chosen))
     parts = lax.all_to_all(parts, ("zh", "zl"), 0, 0, tiled=True)
-    inv = jnp.concatenate(exchange(chosen, "zh"), 0)
-    parts, inv = lax.optimization_barrier((parts, inv))
     g_out, a_out = local_call(
         functools.partial(combine_kernel, n=H * L, f_own=f_own, L=L, wt=wt, wq=wq, d_part=d_part),
         (jax.ShapeDtypeStruct((f_own, wt + wq), BF), jax.ShapeDtypeStruct((Y * X, 16, L * wt), BF)),
         parts,
     )
-    a_all = lax.all_to_all(a_out, ("y", "x"), 0, 0, tiled=True).reshape(Y * X * 16, L * wt)
+    a_all = lax.all_to_all(a_out, ("yh", "yl", "x"), 0, 0, tiled=True).reshape(Y * X * 16, L * wt)
+    g_all = lax.all_gather(lax.all_gather(g_out, "zl"), "zh")
+    a_all, g_all = lax.optimization_barrier((a_all, g_all))
     a_other = swap(a_all, "c")
-    pair = jnp.stack([g_out, swap(g_out, "zl")])
-    g_all = [pair] + [
-        lax.ppermute(pair, "zh", [(i, (i + step) % H) for i in range(H)]) for step in range(1, H)
-    ]
-    g_other = swap(jnp.concatenate([p[:, :, wt:] for p in g_all], 0), "c")
+    g_other = swap(g_all[..., wt:], "c")
     scores = local_call(
-        functools.partial(score_kernel, Y=Y, L=L, wt=wt, wq=wq, d_part=d_part, group=H * qh),
+        functools.partial(
+            score_kernel, Y=Y, YL=YL, L=L, wt=wt, wq=wq, d_part=d_part, group=H * qh, n_d=d_tile
+        ),
         jax.ShapeDtypeStruct((Y, L * wt), F32),
-        a_all, a_other, *g_all, g_other, inv,
+        a_all, a_other, g_all, g_other, own, other,
+        scratch=[pltpu.VMEM((f_tile, Y * X * 16), F32)],
     )
     n_out = Y * X * H * L
     scores = scores.T.reshape(n_out, scores.shape[1] // n_out * Y)
-    mine = lax.all_to_all(scores, ("x", "y", "zh", "zl"), 0, 0, tiled=True).sum(0)
+    mine = lax.all_to_all(scores, ("x", "yl", "yh", "zh", "zl"), 0, 0, tiled=True).sum(0)
     return mine.reshape(-1, Y)
 
 
 def factored(mesh):
     devices = mesh.devices
     ex, blk = devices.shape
-    xs, cores = 4, 2
-    zh = 4
+    yl, xs, zh, cores = 2, 4, 4, 2
     return Mesh(
-        devices.reshape(ex // (xs * zh), xs, zh, blk // cores, cores), ("y", "x", "zh", "zl", "c")
+        devices.reshape(ex // (yl * xs * zh), yl, xs, zh, blk // cores, cores), ("yh", "yl", "x", "zh", "zl", "c")
     )
 
 
 def solution(mesh):
-    ex, blk = ("y", "x", "zh"), ("zl", "c")
+    ex, blk = ("yh", "yl", "x", "zh"), ("zl", "c")
     placed = (
         P(ex, blk),
         P(ex, blk),

time: 206 us -> 179 us (0.87)
  blocking collectives: 24.8 us -> 76.8 us
  waiting for transfers between devices: 67.4 us -> 27.8 us
  starting transfers between devices: 89.1 us -> 52.5 us
  local copies, waits for them, and re-layouts: 10.4 us -> 5.79 us
    all_to_all x1 -> x2, blocking collectives: 24.8 us -> 59.1 us  [the longest x1 31 us: per_device(): parts = lax.all_to_all(parts, ('zh', 'zl'), 0, 0, tiled=True)]
    all_gather x0 -> x2, blocking collectives: none -> 17.8 us  [per_device(): g_all = lax.all_gather(lax.all_gather(g_out, 'zl'), 'zh')]
    all_to_all x4 -> x3, waiting for transfers between devices: 28.9 us -> 11.2 us  [the longest x1 10.2 us: per_device(): got = lax.all_to_all(message, ('yh', 'zh'), 0, 0, tiled=True)]
    ppermute x6 -> x3, starting transfers between devices: 25.3 us -> 9.73 us  [exchange(): lax.ppermute(out, axis, [(i, (i + step) % n) for i in range(n)])]
    ppermute x6 -> x3, waiting for transfers between devices: 27.2 us -> 12.3 us  [exchange(): lax.ppermute(out, axis, [(i, (i + step) % n) for i in range(n)])]
    ppermute x3 -> x0, starting transfers between devices: 10.8 us -> none  [per_device(): lax.ppermute(pair, 'zh', [(i, (i + step) % H) for i in range(H)])]
    ppermute x3 -> x0, waiting for transfers between devices: 8.03 us -> none  [per_device(): lax.ppermute(pair, 'zh', [(i, (i + step) % H) for i in range(H)])]
    all_to_all x4 -> x3, starting transfers between devices: 28.3 us -> 21.9 us  [the longest x1 10 us: per_device(): got = lax.all_to_all(message, ('yh', 'zh'), 0, 0, tiled=True)]
  transfers between devices with their start and end apart: 18 -> 10, of which waited for: 13 -> 7; matrix products, arithmetic and copies ran while one was open for 2% -> 3% of each run, Pallas kernels for 0% -> 0%
where the time goes in v3:
time: 179 us; the launch traced here: 178 us
  blocking collectives  76.8 us (43%)
  starting transfers between devices  52.5 us (29%)
  waiting for transfers between devices  27.8 us (16%)
  Pallas kernels  9.43 us (5%)
  local copies, waits for them, and re-layouts  5.79 us (3%)
  matrix products  4.03 us (2%)
    all_to_all x1, blocking collectives, per_device(): parts = lax.all_to_all(parts, ('zh', 'zl'), 0, 0, tiled=True)  31 us
    all_to_all x1, blocking collectives, per_device(): lax.all_to_all(scores, ('x', 'yl', 'yh', 'zh', 'zl'), 0, 0, tiled=True)  28 us
    ppermute x4, starting transfers between devices, swap(): return lax.ppermute(v, axis, [(0, 1), (1, 0)])  20.9 us
    all_gather x2, blocking collectives, per_device(): g_all = lax.all_gather(lax.all_gather(g_out, 'zl'), 'zh')  17.8 us
    ppermute x3, waiting for transfers between devices, exchange(): lax.ppermute(out, axis, [(i, (i + step) % n) for i in range(n)])  12.3 us
    all_to_all x1, waiting for transfers between devices, per_device(): got = lax.all_to_all(message, ('yh', 'zh'), 0, 0, tiled=True)  10.2 us
    all_to_all x1, starting transfers between devices, per_device(): got = lax.all_to_all(message, ('yh', 'zh'), 0, 0, tiled=True)  10 us
    ppermute x3, starting transfers between devices, exchange(): lax.ppermute(out, axis, [(i, (i + step) % n) for i in range(n)])  9.73 us
  transfers between devices with their start and end apart: 10, of which 7 were waited for; matrix products, arithmetic and copies ran while one was open for 3% of the time, Pallas kernels for 0%

profile of v3, /device:TPU:1, one launch (start us, length us, event | category | flops | bytes accessed | tf_op | source)
XLA Modules:
  0.0 178.2 jit_solution(2870345669604650660)
XLA Ops:
  0.0 1.8 shard_map.82
  1.8 8.8 %collective-permute-start = (bf16[32,1280]{1,0:T(8,128)(2,1)}, bf16[32,1280]{1,0:T(8,128)(2,1)S(1)}, u32[]{:S(2)}, u32[]{:S(2)}) collective-permute-start(bf16[32,1280]{1,0:T(8,128)(2,1)} %get-tuple-element.21), channel_id=1, source_target_pairs={{0,1},{1,0},{2,3},{3,2},{4,5},{5,4},{6,7},{7,6},{8,9},{9,8},{10,11... | collective-permute-start | bytes 245768 | tf_op jit(solution)/shard_map/ppermute | solution.py:22
  10.6 1.1 collective-permute-done
  11.7 0.9 add_bitcast_fusion
  12.6 0.7 broadcast_in_dim.8
  13.3 10.0 %all-to-all-start = ((bf16[16,8,1280]{2,1,0:T(8,128)(2,1)}), bf16[16,8,1280]{2,1,0:T(8,128)(2,1)S(1)}, u32[]{:S(2)}, u32[]{:S(2)}) async-start(bf16[16,8,1280]{2,1,0:T(8,128)(2,1)} %bitcast.2), calls=%async_computation | async-start | bytes 655360 | tf_op jit(solution)/shard_map/all_to_all | solution.py:295
  23.4 4.0 %fusion.27 = bf16[80,1280]{1,0:T(8,128)(2,1)S(1)} fusion(s32[]{:T(128)S(6)} %mul.19, s32[1280]{0:T(1024)S(1)} %get-tuple-element.39, s32[1280]{0:T(1024)S(1)} %get-tuple-element.42, s32[1280]{0:T(1024)S(1)} %get-tuple-element.40, s32[1280]{0:T(1024)S(1)} %get-tuple-element.41, pred[1280]{0:T(1024)(128)(4,1)S(1)} %get-tuple-element.43, ...), kind=kOutput, calls=%fused_computation.30 | convolution fusion | flops 591360000 | bytes 1047045 | tf_op jit(solution)/shard_map/dot_general | solution.py:315
  28.2 10.2 %all-to-all-done = bf16[16,8,1280]{2,1,0:T(8,128)(2,1)S(1)} async-done(((bf16[16,8,1280]{2,1,0:T(8,128)(2,1)}), bf16[16,8,1280]{2,1,0:T(8,128)(2,1)S(1)}, u32[]{:S(2)}, u32[]{:S(2)}) %all-to-all-start) | async-done | bytes 327712 | tf_op jit(solution)/shard_map/all_to_all | solution.py:295
  38.9 1.5 copy-done
  40.4 4.0 %all-to-all-start.1 = ((bf16[8,208,768]{2,1,0:T(8,128)(2,1)}), bf16[8,208,768]{2,1,0:T(8,128)(2,1)S(1)}, u32[]{:S(2)}, u32[]{:S(2)}) async-start(bf16[8,208,768]{2,1,0:T(8,128)(2,1)} %copy-done), calls=%async_computation.1 | async-start | bytes 5111808 | tf_op jit(solution)/shard_map/all_to_all | solution.py:326
  44.5 3.1 %collective-permute-start.3 = (bf16[96,960]{1,0:T(8,128)(2,1)S(1)}, bf16[96,960]{1,0:T(8,128)(2,1)S(1)}, u32[]{:S(2)}, u32[]{:S(2)}) collective-permute-start(bf16[96,960]{1,0:T(8,128)(2,1)S(1)} %get-tuple-element.36), channel_id=1, source_target_pairs={{0,12},{4,0},{8,4},{12,8},{1,13},{5,1},{9,5},{13,9},{2,14},{6,2},{... | collective-permute-start | bytes 552968 | tf_op jit(solution)/shard_map/ppermute | solution.py:28
  47.6 4.4 %collective-permute-start.2 = (bf16[96,960]{1,0:T(8,128)(2,1)S(1)}, bf16[96,960]{1,0:T(8,128)(2,1)S(1)}, u32[]{:S(2)}, u32[]{:S(2)}) collective-permute-start(bf16[96,960]{1,0:T(8,128)(2,1)S(1)} %get-tuple-element.37), channel_id=1, source_target_pairs={{0,8},{4,12},{8,0},{12,4},{1,9},{5,13},{9,1},{13,5},{2,10},{6,14},... | collective-permute-start | bytes 552968 | tf_op jit(solution)/shard_map/ppermute | solution.py:28
  52.0 2.2 %collective-permute-start.1 = (bf16[96,960]{1,0:T(8,128)(2,1)S(1)}, bf16[96,960]{1,0:T(8,128)(2,1)S(1)}, u32[]{:S(2)}, u32[]{:S(2)}) collective-permute-start(bf16[96,960]{1,0:T(8,128)(2,1)S(1)} %get-tuple-element.38), channel_id=1, source_target_pairs={{0,4},{4,8},{8,12},{12,0},{1,5},{5,9},{9,13},{13,1},{2,6},{6,10},{... | collective-permute-start | bytes 552968 | tf_op jit(solution)/shard_map/ppermute | solution.py:28
  54.2 8.6 %collective-permute-done.2 = bf16[96,960]{1,0:T(8,128)(2,1)S(1)} collective-permute-done((bf16[96,960]{1,0:T(8,128)(2,1)S(1)}, bf16[96,960]{1,0:T(8,128)(2,1)S(1)}, u32[]{:S(2)}, u32[]{:S(2)}) %collective-permute-start.2) | collective-permute-done | bytes 184352 | tf_op jit(solution)/shard_map/ppermute | solution.py:28
  62.8 3.7 %collective-permute-done.1 = bf16[96,960]{1,0:T(8,128)(2,1)S(1)} collective-permute-done((bf16[96,960]{1,0:T(8,128)(2,1)S(1)}, bf16[96,960]{1,0:T(8,128)(2,1)S(1)}, u32[]{:S(2)}, u32[]{:S(2)}) %collective-permute-start.1) | collective-permute-done | bytes 184352 | tf_op jit(solution)/shard_map/ppermute | solution.py:28
  66.6 3.9 %collective-permute-start.4 = (bf16[4,96,960]{2,1,0:T(8,128)(2,1)S(1)}, bf16[4,96,960]{2,1,0:T(8,128)(2,1)S(1)}, u32[]{:S(2)}, u32[]{:S(2)}) collective-permute-start(bf16[4,96,960]{2,1,0:T(8,128)(2,1)S(1)} %pad_maximum_fusion.own_ref.inv_ref), channel_id=1, source_target_pairs={{0,1},{1,0},{2,3},{3,2},{4,5},{5,4},{6,7},{7,6},{8,9},{9,8},{10,11... | collective-permute-start | bytes 2211848 | tf_op jit(solution)/shard_map/ppermute | solution.py:22
  70.5 1.9 %collective-permute-done.4.other_ref.invo_ref = bf16[4,96,960]{2,1,0:T(8,128)(2,1)S(1)} collective-permute-done((bf16[4,96,960]{2,1,0:T(8,128)(2,1)S(1)}, bf16[4,96,960]{2,1,0:T(8,128)(2,1)S(1)}, u32[]{:S(2)}, u32[]{:S(2)}) %collective-permute-start.4) | collective-permute-done | bytes 737312 | tf_op jit(solution)/shard_map/ppermute | solution.py:22
  72.4 0.9 copy-done.1
  73.3 1.0 all-to-all-done.1.full_ref
  74.2 1.1 copy-done.2
  75.4 1.5 shard_map.84
  76.9 31.0 %all_to_all.29.parts_ref = bf16[8,112,512]{2,1,0:T(8,128)(2,1)S(1)} all-to-all(bf16[8,112,512]{2,1,0:T(8,128)(2,1)S(1)} %shard_map.84), channel_id=1, replica_groups=mesh['yh'=4,'yl'=2,'x'=4,'zh'=4,'zl'=2,'c'=2] {'zh','zl'}, dimensions={0} | all-to-all | bytes 1835008 | tf_op jit(solution)/shard_map/all_to_all | solution.py:338
  107.9 1.1 shard_map.85
  109.0 7.9 %all-to-all-start.3 = ((bf16[32,16,512]{2,1,0:T(8,128)(2,1)}), bf16[32,16,512]{2,1,0:T(8,128)(2,1)S(1)}, u32[]{:S(2)}, u32[]{:S(2)}) async-start(bf16[32,16,512]{2,1,0:T(8,128)(2,1)} %get-tuple-element.31), calls=%async_computation.3 | async-start | bytes 1048576 | tf_op jit(solution)/shard_map/all_to_all | solution.py:344
  116.9 3.7 %all-gather = bf16[160,384]{1,0:T(8,128)(2,1)S(1)} all-gather(bf16[80,384]{1,0:T(8,128)(2,1)S(1)} %get-tuple-element.32), channel_id=2, replica_groups=mesh['yh'=4,'yl'=2,'x'=4,'zh'=4,'zl'=2,'c'=2] {'zl'}, dimensions={0}, use_global_device_ids=true | all-gather | bytes 184320 | tf_op jit(solution)/shard_map/all_gather | solution.py:345
  120.6 14.0 %all-gather.1 = bf16[8,80,384]{2,1,0:T(8,128)(2,1)S(1)} all-gather(bf16[2,80,384]{2,1,0:T(8,128)(2,1)S(1)} %bitcast.42), channel_id=3, replica_groups=mesh['yh'=4,'yl'=2,'x'=4,'zh'=4,'zl'=2,'c'=2] {'zh'}, dimensions={0}, use_global_device_ids=true | all-gather | bytes 614400 | tf_op jit(solution)/shard_map/all_gather | solution.py:345
  134.7 6.3 %collective-permute-start.5 = (bf16[512,512]{1,0:T(8,128)(2,1)S(1)}, bf16[512,512]{1,0:T(8,128)(2,1)S(1)}, u32[]{:S(2)}, u32[]{:S(2)}) collective-permute-start(bf16[512,512]{1,0:T(8,128)(2,1)S(1)} %bitcast.35), channel_id=1, source_target_pairs={{0,1},{1,0},{2,3},{3,2},{4,5},{5,4},{6,7},{7,6},{8,9},{9,8},{10,11... | collective-permute-start | bytes 1572872 | tf_op jit(solution)/shard_map/ppermute | solution.py:22
  141.0 1.9 %collective-permute-start.6 = (bf16[4,2,80,128]{3,2,1,0:T(8,128)(2,1)S(1)}, bf16[4,2,80,128]{3,2,1,0:T(8,128)(2,1)S(1)}, u32[]{:S(2)}, u32[]{:S(2)}) collective-permute-start(bf16[4,2,80,128]{3,2,1,0:T(8,128)(2,1)S(1)} %slice.11), channel_id=1, source_target_pairs={{0,1},{1,0},{2,3},{3,2},{4,5},{5,4},{6,7},{7,6},{8,9},{9,8},{10,11... | collective-permute-start | bytes 491528 | tf_op jit(solution)/shard_map/ppermute | solution.py:22
  143.0 1.4 collective-permute-done.6.go_ref
  144.3 4.6 %shard_map.86 = f32[8,512]{1,0:T(8,128)S(1)} custom-call(bf16[512,512]{1,0:T(8,128)(2,1)S(1)} %bitcast.36, bf16[512,512]{1,0:T(8,128)(2,1)S(1)} %collective-permute-done.5.ao_ref, bf16[4,2,80,384]{3,2,1,0:T(8,128)(2,1)S(1)} %bitcast.34, bf16[4,2,80,128]{3,2,1,0:T(8,128)(2,1)S(1)} %collective-permute-done.6.go_ref, ...), custom_call_target="tpu_custom_call" | custom-call | tf_op jit(solution)/shard_map/pallas_call | solution.py:259
  149.2 28.0 %all_to_all.30 = f32[256,1,16]{2,1,0:T(1,128)S(1)} all-to-all(f32[256,1,16]{2,1,0:T(1,128)S(1)} %bitcast.41), channel_id=1, replica_groups=mesh['yh'=4,'yl'=2,'x'=4,'zh'=4,'zl'=2,'c'=2] {'x','yl','yh','zh','zl'}, dimensions={0} | all-to-all | bytes 32768 | tf_op jit(solution)/shard_map/all_to_all | solution.py:359
  177.5 0.6 reshape.44
  (35 shorter events, 1.9 us)
Async XLA Ops:
  1.8 9.9 %collective-permute-start = (bf16[32,1280]{1,0:T(8,128)(2,1)}, bf16[32,1280]{1,0:T(8,128)(2,1)S(1)}, u32[]{:S(2)}, u32[]{:S(2)}) collective-permute-start(bf16[32,1280]{1,0:T(8,128)(2,1)} %get-tuple-element.21), channel_id=1, source_target_pairs={{0,1},{1,0},{2,3},{3,2},{4,5},{5,4},{6,7},{7,6},{8,9},{9,8},{10,11... | collective-permute-start | bytes 245768 | tf_op jit(solution)/shard_map/ppermute | solution.py:22
  13.3 25.2 %all-to-all-start = ((bf16[16,8,1280]{2,1,0:T(8,128)(2,1)}), bf16[16,8,1280]{2,1,0:T(8,128)(2,1)S(1)}, u32[]{:S(2)}, u32[]{:S(2)}) async-start(bf16[16,8,1280]{2,1,0:T(8,128)(2,1)} %bitcast.2), calls=%async_computation | async-start | bytes 655360 | tf_op jit(solution)/shard_map/all_to_all | solution.py:295
  23.3 4.1 %copy-start.5 = (bf16[640,20]{0,1:T(8,128)(2,1)S(1)}, bf16[640,20]{0,1:T(8,128)(2,1)}, u32[]{:S(2)}) copy-start(bf16[640,20]{0,1:T(8,128)(2,1)} %param.14) | copy-start | bytes 76804
  23.3 4.7 %copy-start.4 = (bf16[2560,80]{0,1:T(8,128)(2,1)S(1)}, bf16[2560,80]{0,1:T(8,128)(2,1)}, u32[]{:S(2)}) copy-start(bf16[2560,80]{0,1:T(8,128)(2,1)} %param.13) | copy-start | bytes 1228804
  38.9 1.5 copy-start
  40.4 33.8 %all-to-all-start.1 = ((bf16[8,208,768]{2,1,0:T(8,128)(2,1)}), bf16[8,208,768]{2,1,0:T(8,128)(2,1)S(1)}, u32[]{:S(2)}, u32[]{:S(2)}) async-start(bf16[8,208,768]{2,1,0:T(8,128)(2,1)} %copy-done), calls=%async_computation.1 | async-start | bytes 5111808 | tf_op jit(solution)/shard_map/all_to_all | solution.py:326
  44.5 9.8 %collective-permute-start.3 = (bf16[96,960]{1,0:T(8,128)(2,1)S(1)}, bf16[96,960]{1,0:T(8,128)(2,1)S(1)}, u32[]{:S(2)}, u32[]{:S(2)}) collective-permute-start(bf16[96,960]{1,0:T(8,128)(2,1)S(1)} %get-tuple-element.36), channel_id=1, source_target_pairs={{0,12},{4,0},{8,4},{12,8},{1,13},{5,1},{9,5},{13,9},{2,14},{6,2},{... | collective-permute-start | bytes 552968 | tf_op jit(solution)/shard_map/ppermute | solution.py:28
  47.6 15.3 %collective-permute-start.2 = (bf16[96,960]{1,0:T(8,128)(2,1)S(1)}, bf16[96,960]{1,0:T(8,128)(2,1)S(1)}, u32[]{:S(2)}, u32[]{:S(2)}) collective-permute-start(bf16[96,960]{1,0:T(8,128)(2,1)S(1)} %get-tuple-element.37), channel_id=1, source_target_pairs={{0,8},{4,12},{8,0},{12,4},{1,9},{5,13},{9,1},{13,5},{2,10},{6,14},... | collective-permute-start | bytes 552968 | tf_op jit(solution)/shard_map/ppermute | solution.py:28
  52.0 14.5 %collective-permute-start.1 = (bf16[96,960]{1,0:T(8,128)(2,1)S(1)}, bf16[96,960]{1,0:T(8,128)(2,1)S(1)}, u32[]{:S(2)}, u32[]{:S(2)}) collective-permute-start(bf16[96,960]{1,0:T(8,128)(2,1)S(1)} %get-tuple-element.38), channel_id=1, source_target_pairs={{0,4},{4,8},{8,12},{12,0},{1,5},{5,9},{9,13},{13,1},{2,6},{6,10},{... | collective-permute-start | bytes 552968 | tf_op jit(solution)/shard_map/ppermute | solution.py:28
  66.6 5.8 %collective-permute-start.4 = (bf16[4,96,960]{2,1,0:T(8,128)(2,1)S(1)}, bf16[4,96,960]{2,1,0:T(8,128)(2,1)S(1)}, u32[]{:S(2)}, u32[]{:S(2)}) collective-permute-start(bf16[4,96,960]{2,1,0:T(8,128)(2,1)S(1)} %pad_maximum_fusion.own_ref.inv_ref), channel_id=1, source_target_pairs={{0,1},{1,0},{2,3},{3,2},{4,5},{5,4},{6,7},{7,6},{8,9},{9,8},{10,11... | collective-permute-start | bytes 2211848 | tf_op jit(solution)/shard_map/ppermute | solution.py:22
  72.4 0.9 copy-start.1
  74.2 1.1 copy-start.2
  76.8 67.5 %copy-start.3 = (bf16[4,96,960]{2,1,0:T(8,128)(2,1)S(1)}, bf16[4,96,960]{2,1,0:T(8,128)(2,1)}, u32[]{:S(2)}) copy-start(bf16[4,96,960]{2,1,0:T(8,128)(2,1)} %copy-done.1) | copy-start | bytes 2211844
  109.0 25.6 %all-to-all-start.3 = ((bf16[32,16,512]{2,1,0:T(8,128)(2,1)}), bf16[32,16,512]{2,1,0:T(8,128)(2,1)S(1)}, u32[]{:S(2)}, u32[]{:S(2)}) async-start(bf16[32,16,512]{2,1,0:T(8,128)(2,1)} %get-tuple-element.31), calls=%async_computation.3 | async-start | bytes 1048576 | tf_op jit(solution)/shard_map/all_to_all | solution.py:344
  134.7 9.6 %collective-permute-start.5 = (bf16[512,512]{1,0:T(8,128)(2,1)S(1)}, bf16[512,512]{1,0:T(8,128)(2,1)S(1)}, u32[]{:S(2)}, u32[]{:S(2)}) collective-permute-start(bf16[512,512]{1,0:T(8,128)(2,1)S(1)} %bitcast.35), channel_id=1, source_target_pairs={{0,1},{1,0},{2,3},{3,2},{4,5},{5,4},{6,7},{7,6},{8,9},{9,8},{10,11... | collective-permute-start | bytes 1572872 | tf_op jit(solution)/shard_map/ppermute | solution.py:22
  141.0 3.3 %collective-permute-start.6 = (bf16[4,2,80,128]{3,2,1,0:T(8,128)(2,1)S(1)}, bf16[4,2,80,128]{3,2,1,0:T(8,128)(2,1)S(1)}, u32[]{:S(2)}, u32[]{:S(2)}) collective-permute-start(bf16[4,2,80,128]{3,2,1,0:T(8,128)(2,1)S(1)} %slice.11), channel_id=1, source_target_pairs={{0,1},{1,0},{2,3},{3,2},{4,5},{5,4},{6,7},{7,6},{8,9},{9,8},{10,11... | collective-permute-start | bytes 491528 | tf_op jit(solution)/shard_map/ppermute | solution.py:22

commit v4 on v3

--- a/solution.py
+++ b/solution.py
@@ -47,78 +47,85 @@
 LANES = 128
 
 
-def message_kernel(tg_ref, ta_ref, mask_ref, qg_ref, qa_ref, mine_ref, theirs_ref, *, H, L, C):
-    core = lax.axis_index("c")
+def message_kernel(tg_ref, ta_ref, mask_ref, qg_ref, qa_ref, out_ref, *, H, L, C):
     nt, nq = tg_ref.shape[0], qg_ref.shape[0]
     th, per = nt // C, nt // (L * C)
-    r, c = iota((2 * nt, nt), 0), iota((2 * nt, nt), 1)
-    first = r < th
-    owner = jnp.where(first, core, 1 - core)
-    k = r % th
-    token = (k // per) * (C * per) + owner * per + k % per
-    used = first | (r >= 2 * nt - th)
-    pick = (used & (token == c)).astype(F32)
-    masked = (pick * mask_ref[...].astype(F32)).astype(BF)
-    pick = pick.astype(BF)
-    r, c = iota((2 * nt, nq), 0), iota((2 * nt, nq), 1)
-    first = r < th
-    owner = jnp.where(first, core, 1 - core)
-    used = first | (r >= 2 * nt - th)
-    pick_q = (used & (owner * (nq // C) + (r % th) // 2 == c)).astype(BF)
-    tg, ta = matmul(masked, tg_ref[...]), matmul(pick, ta_ref[...])
+    rows = 2 * th * C
+
+    def pick(n, row_of, upper):
+        r, c = iota((rows, n), 0), iota((rows, n), 1)
+        owner, k = r // (2 * th), r % th
+        return ((r // th) % 2 == upper) & (row_of(owner, k) == c)
+
+    def train(owner, k):
+        return (k // per) * (C * per) + owner * per + k % per
+
+    def query(owner, k):
+        return owner * (nq // C) + k // 2
+
+    masked = (pick(nt, train, 0).astype(F32) * mask_ref[...].astype(F32)).astype(BF)
+    pick_q = pick(nq, query, 1).astype(BF)
+    tg, ta = matmul(masked, tg_ref[...]), matmul(pick(nt, train, 1).astype(BF), ta_ref[...])
     qg, qa = matmul(pick_q, qg_ref[...]), matmul(pick_q, qa_ref[...])
     gs = tg.shape[1] // H
     wide = 3 * LANES
-    out = []
+    low_half = iota((rows, wide), 0) % 2 == 0
     for h in range(H):
-        low_half = iota((2 * nt, wide), 0) % 2 == 0
         q = qg[:, h * gs:(h + 1) * gs]
-        q_high = jnp.concatenate([q[:, wide:], jnp.zeros((2 * nt, 2 * wide - gs), F32)], 1)
+        q_high = jnp.concatenate([q[:, wide:], jnp.zeros((rows, 2 * wide - gs), F32)], 1)
         q = jnp.where(low_half, q[:, :wide], q_high)
-        low_half = low_half[:, :LANES]
         a_tile, rest = qa[:, h * LANES:(h + 1) * LANES], qa[:, H * LANES:]
         at = 32 * h
         b_tile = lanes(ta[:, H * LANES:], -at, 0, 32) + jnp.where(
-            low_half,
+            low_half[:, :LANES],
             lanes(a_tile, 32, 32, 96) + lanes(rest, 96 - at, 96, 112),
             lanes(a_tile, -32, 32, 96) + lanes(rest, 80 - at, 96, 112),
         )
-        out.append(
-            jnp.concatenate([tg[:, h * gs:(h + 1) * gs], ta[:, h * LANES:(h + 1) * LANES], b_tile, q], 1)
-        )
-    mine_ref[...] = jnp.concatenate([v[:nt] for v in out], 0).astype(BF)
-    theirs_ref[...] = jnp.concatenate([v[nt:] for v in out], 0).astype(BF)
+        v = tg[:, h * gs:(h + 1) * gs] + jnp.concatenate([ta[:, h * LANES:(h + 1) * LANES], b_tile, q], 1)
+        v = v.astype(BF)
+        for y in range(out_ref.shape[0]):
+            out_ref[y, h * rows:(h + 1) * rows] = v
 
 
 def shuffle_kernel(got_ref, out_ref, *, G, th, qh, gs):
-    src = 2 * th
-    n = G * src
-    r, c = iota((n, n), 0), iota((n, n), 1)
-    rest = r % (G * th)
-    pick = (c == (rest // th) * src + (r // (G * th)) * th + rest % th).astype(BF)
-    qn = 2 * G * qh
-    r, c = iota((qn, n), 0), iota((qn, n), 1)
-    rest = r % (G * qh)
-    row = (rest // qh) * src + ((r // (G * qh)) * qh + rest % qh) * 2
-    picks = [(c == row + half).astype(BF) for half in range(2)]
-    width = gs + LANES
+    core = lax.axis_index("c")
+    n = got_ref.shape[0]
+    each = 2 * th
+
+    def pick(count, per, row_of):
+        r, c = iota((count, n), 0), iota((count, n), 1)
+        rest = r % (G * per)
+        source = (core + r // (G * per)) % 2
+        return (c == (rest // per) * (2 * each) + source * each + row_of(rest % per)).astype(BF)
+
+    tn, qn = 2 * G * th, 2 * G * qh
     got = got_ref[...]
-    train = matmul(pick, got[:, :width + LANES])
+    t_grads = matmul(pick(tn, th, lambda k: k), got)
+    t_acts = matmul(pick(tn, th, lambda k: th + k), got[:, :2 * LANES])
+    q0, q1 = (matmul(pick(qn, qh, lambda k: th + 2 * k + half), got) for half in range(2))
     wide = 3 * LANES
-    q_grads = jnp.concatenate(
-        [matmul(picks[0], got[:, width + LANES:]), matmul(picks[1], got[:, width + LANES:width + LANES + gs - wide])], 1
-    )
-    v0, v1 = (matmul(p, got[:, width:width + LANES]) for p in picks)
+    at = 2 * LANES
+    q_grads = jnp.concatenate([q0[:, at:], q1[:, at:at + gs - wide]], 1)
+    v0, v1 = q0[:, LANES:at], q1[:, LANES:at]
     q_a = lanes(v0, -32, 0, 64) + lanes(v1, 32, 64, 128)
     q_b = lanes(v0, 32, 0, 16) + lanes(v1, 48, 16, 32)
-    body = jnp.concatenate([train[:, :width], jnp.concatenate([q_grads, q_a], 1)], 0).astype(BF)
-    tail = jnp.concatenate([train[:, width:], q_b], 0)
+    body = jnp.concatenate(
+        [jnp.concatenate([t_grads, t_acts[:, :LANES]], 1), jnp.concatenate([q_grads, q_a], 1)], 0
+    ).astype(BF)
+    tail = jnp.concatenate([t_acts[:, LANES:], q_b], 0)
     rows = tail.shape[0] // 4
     packed = sum(lanes(tail[g * rows:(g + 1) * rows], 32 * g, 32 * g, 32 * g + 32) for g in range(4)).astype(BF)
     packed = jnp.concatenate([packed[k:k + 16] for k in range(0, rows, 16)], 1)
     for x in range(out_ref.shape[0]):
-        out_ref[x, :n + qn] = body
-        out_ref[x, n + qn:, :packed.shape[1]] = packed
+        out_ref[x, :tn + qn] = body
+        out_ref[x, tn + qn:, :packed.shape[1]] = packed
+
+
+def total_kernel(parts_ref, out_ref):
+    total = jnp.sum(parts_ref[...], axis=0, keepdims=True)
+    width = out_ref.shape[1]
+    for k in range(out_ref.shape[0]):
+        out_ref[k:k + 1, :] = total[:, k * width:(k + 1) * width]
 
 
 def rotate_kernel(full_ref, own_ref, other_ref, out_ref, *, H, L, tt, tq, gs, f_own, d_part):
@@ -128,10 +135,16 @@
     wt, wq = inner * tt, inner * tq
     group = per // 4
     grads = [jnp.concatenate([b[s, :f_own, :gs] for s in range(H)], 0) for b in (own_ref, other_ref)]
-    acts = [
-        jnp.concatenate([b[s, f_own:, k * 2 * LANES:(k + 1) * 2 * LANES] for s in range(H) for k in range(L)], 0)
-        for b in (own_ref, other_ref)
-    ]
+    r, c = iota((H * L * 16, H * f_own), 0), iota((H * L * 16, H * f_own), 1)
+    d = (r // 16) % L * d_part + r % 16
+    picks = [((r % 16 < d_part) & (c == r // (16 * L) * f_own + d * 4 + q)).astype(BF) for q in range(4)]
+    acts = []
+    for b in (own_ref, other_ref):
+        last = jnp.concatenate([b[s, :, b.shape[2] - LANES:] for s in range(H)], 0)
+        v = [matmul(p, last) for p in picks]
+        a_tile = sum(lanes(v[q], 32 * q - 64, 32 * q, 32 * q + 32) for q in range(4))
+        b_tile = sum(lanes(v[q], 8 * q - 96, 8 * q, 8 * q + 8) for q in range(4))
+        acts.append(jnp.concatenate([a_tile, b_tile], 1).astype(BF))
     r, c = iota((H * L * 32, H * L * 16), 0), iota((H * L * 32, H * L * 16), 1)
     repeat = ((r % 32 < (L + 1) * d_part) & (c == (r // 32) * 16 + (r % 32) % d_part)).astype(BF)
     acts = [matmul(repeat, v).astype(BF) for v in acts]
@@ -202,7 +215,7 @@
 
 
 def score_kernel(
-    a_ref, ao_ref, g_ref, go_ref, inv_ref, invo_ref, out_ref, inv_acc, *, Y, YL, L, wt, wq, d_part, group, n_d
+    a_ref, ao_ref, g_ref, go_ref, inv_ref, invo_ref, out_ref, inv_acc, *, Y, YL, L, wt, wq, d_part, group, n_g, n_d
 ):
     H, f_own, d_tile = g_ref.shape[0], g_ref.shape[2], n_d
     half = d_part // 2
@@ -231,7 +244,9 @@
     me = lax.axis_index("zh")
     for s in range(H):
         rows = pl.ds(pl.multiple_of(lax.rem(me - s + H, H) * f_own, f_own), f_own)
-        inv_acc[rows, :] = matmul(inv_ref[s, :f_own, -d_tile:], place) + matmul(invo_ref[s, :f_own, -d_tile:], place)
+        inv_acc[rows, :] = matmul(inv_ref[s, :, n_g:n_g + d_tile], place) + matmul(
+            invo_ref[s, :, n_g:n_g + d_tile], place
+        )
     inv = inv_acc[...]
     col = iota(qg.shape, 1)
     owner = (col // group) % (Y // YL) * YL + (col // (group * (Y // YL))) % YL
@@ -282,26 +297,22 @@
     d_part = d_block // (H * L)
     d_tile = d_part * X * Y
 
-    mine, theirs = staged_call(
+    message = staged_call(
         functools.partial(message_kernel, H=H, L=L, C=C),
-        [jax.ShapeDtypeStruct((H * nt, 2 * gs), BF)] * 2,
+        [jax.ShapeDtypeStruct((YH, H * C * 2 * th, gs), BF)],
         train_grads, train_acts, train_mask.reshape(1, nt), query_grads, query_acts,
-    )
-    message = mine + swap(theirs, "c")
-    message = jnp.broadcast_to(message.reshape(1, H, nt, 2 * gs), (YH, H, nt, 2 * gs)).reshape(YH * H, nt, 2 * gs)
+    )[0].reshape(YH * H * C, 2 * th, gs)
     message, grad_basis, act_basis, eigenvalues = lax.optimization_barrier(
         (message, grad_basis, act_basis, eigenvalues)
     )
-    got = lax.all_to_all(message, ("yh", "zh"), 0, 0, tiled=True)
+    got = lax.all_to_all(message, ("yh", "zh", "c"), 0, 0, tiled=True)
 
     gb = grad_basis.T.reshape(f_own, H, gs).transpose(1, 0, 2)
     ab = act_basis.T
     main = ab[:, :H * LANES].reshape(d_own, H, LANES)
     rest = ab[:, H * LANES:].reshape(d_own, H, as_ - LANES)
-    ab = jnp.concatenate([main, rest], 2).reshape(L, d_part, H, as_).transpose(2, 1, 0, 3)
-    ab = jnp.pad(ab, ((0, 0), (0, 16 - d_part), (0, 0), (0, 2 * LANES - as_))).reshape(H, 16, L * 2 * LANES)
-    ab = jnp.pad(ab, ((0, 0), (0, 0), (0, gs - L * 2 * LANES)))
-    pieces = jnp.concatenate([gb, ab], 1)
+    ab = jnp.concatenate([main.reshape(d_own, H, 4, -1), rest.reshape(d_own, H, 4, -1)], 3)
+    ab = ab.transpose(1, 0, 2, 3).reshape(H, f_own, as_ // 4)
 
     inverse = 1.0 / (eigenvalues + damping)
 
@@ -314,14 +325,15 @@
     half = jnp.where(lax.axis_index("c") == 0, inv_high, inv_low)
     chosen = jnp.dot(half, sel, preferred_element_type=F32).astype(BF)
     chosen = chosen.reshape(f_own, H, d_tile).transpose(1, 0, 2)
-    pieces = jnp.concatenate([pieces, jnp.pad(chosen, ((0, 0), (0, 16), (0, 0)))], 2)
+    spare = -(gs + d_tile + as_ // 4) % LANES
+    pieces = jnp.pad(jnp.concatenate([gb, chosen, ab], 2), ((0, 0), (0, 0), (0, spare)))
     got, pieces = lax.optimization_barrier((got, pieces))
 
     G = YH * H
     block = local_call(
         functools.partial(shuffle_kernel, G=G, th=th, qh=qh, gs=gs),
         jax.ShapeDtypeStruct((X * YL, G * C * (th + qh) + 16, gs + LANES), BF),
-        got.reshape(G * nt, 2 * gs),
+        got.reshape(G * C * 2 * th, gs),
     )
     full = lax.all_to_all(block, ("x", "yl"), 0, 0, tiled=True)
     own = jnp.stack([exchange(pieces, "zh", k) for k in range(H)])
@@ -348,7 +360,7 @@
     g_other = swap(g_all[..., wt:], "c")
     scores = local_call(
         functools.partial(
-            score_kernel, Y=Y, YL=YL, L=L, wt=wt, wq=wq, d_part=d_part, group=H * qh, n_d=d_tile
+            score_kernel, Y=Y, YL=YL, L=L, wt=wt, wq=wq, d_part=d_part, group=H * qh, n_g=gs, n_d=d_tile
         ),
         jax.ShapeDtypeStruct((Y, L * wt), F32),
         a_all, a_other, g_all, g_other, own, other,
@@ -356,8 +368,8 @@
     )
     n_out = Y * X * H * L
     scores = scores.T.reshape(n_out, scores.shape[1] // n_out * Y)
-    mine = lax.all_to_all(scores, ("x", "yl", "yh", "zh", "zl"), 0, 0, tiled=True).sum(0)
-    return mine.reshape(-1, Y)
+    mine = lax.all_to_all(scores, ("x", "yl", "yh", "zh", "zl"), 0, 0, tiled=True)
+    return local_call(total_kernel, jax.ShapeDtypeStruct((scores.shape[1] // Y, Y), F32), mine)
 
 
 def factored(mesh):

time: 179 us -> 173 us (0.966)
  starting transfers between devices: 52.5 us -> 46.8 us
  waiting for transfers between devices: 27.8 us -> 32.6 us
  blocking collectives: 76.8 us -> 72.6 us
    ppermute x4 -> x3, starting transfers between devices: 20.9 us -> 10.9 us  [swap(): return lax.ppermute(v, axis, [(0, 1), (1, 0)])]
    all_to_all x1, starting transfers between devices: 10 us -> 17.2 us  [per_device(): got = lax.all_to_all(message, ('yh', 'zh', 'c'), 0, 0, tiled=True)]
    all_to_all x1, waiting for transfers between devices: 0.95 us -> 5.56 us  [per_device(): full = lax.all_to_all(block, ('x', 'yl'), 0, 0, tiled=True)]
    all_to_all x1, blocking collectives: 31 us -> 27.3 us  [per_device(): parts = lax.all_to_all(parts, ('zh', 'zl'), 0, 0, tiled=True)]
    all_to_all x1, starting transfers between devices: 7.86 us -> 5.66 us  [per_device(): lax.all_to_all(a_out, ('yh', 'yl', 'x'), 0, 0, tiled=True)]
    pallas_call x4 -> x5, Pallas kernels: 7.66 us -> 8.83 us  [local_call(): pl.pallas_call(kernel, out_shape=shapes, in_specs=[pl.BlockSpec(memory_sp...]
    ppermute x4 -> x3, waiting for transfers between devices: 4.31 us -> 3.26 us  [swap(): return lax.ppermute(v, axis, [(0, 1), (1, 0)])]
  transfers between devices with their start and end apart: 10 -> 9, of which waited for: 7 -> 7; matrix products, arithmetic and copies ran while one was open for 3% -> 3% of each run, Pallas kernels for 0% -> 0%
where the time goes in v4:
time: 173 us; the launch traced here: 172 us
  blocking collectives  72.6 us (42%)
  starting transfers between devices  46.8 us (27%)
  waiting for transfers between devices  32.6 us (19%)
  Pallas kernels  10.7 us (6%)
  local copies, waits for them, and re-layouts  4.66 us (3%)
  matrix products  4.03 us (2%)
    all_to_all x1, blocking collectives, per_device(): lax.all_to_all(scores, ('x', 'yl', 'yh', 'zh', 'zl'), 0, 0, tiled=True)  28.1 us
    all_to_all x1, blocking collectives, per_device(): parts = lax.all_to_all(parts, ('zh', 'zl'), 0, 0, tiled=True)  27.3 us
    all_to_all x1, starting transfers between devices, per_device(): got = lax.all_to_all(message, ('yh', 'zh', 'c'), 0, 0, tiled=True)  17.2 us
    all_gather x2, blocking collectives, per_device(): g_all = lax.all_gather(lax.all_gather(g_out, 'zl'), 'zh')  17.2 us
    ppermute x3, waiting for transfers between devices, exchange(): lax.ppermute(out, axis, [(i, (i + step) % n) for i in range(n)])  12 us
    all_to_all x1, waiting for transfers between devices, per_device(): got = lax.all_to_all(message, ('yh', 'zh', 'c'), 0, 0, tiled=True)  11.7 us
    ppermute x3, starting transfers between devices, swap(): return lax.ppermute(v, axis, [(0, 1), (1, 0)])  10.9 us
    ppermute x3, starting transfers between devices, exchange(): lax.ppermute(out, axis, [(i, (i + step) % n) for i in range(n)])  9.08 us
  transfers between devices with their start and end apart: 9, of which 7 were waited for; matrix products, arithmetic and copies ran while one was open for 3% of the time, Pallas kernels for 0%

profile of v4, /device:TPU:1, one launch (start us, length us, event | category | flops | bytes accessed | tf_op | source)
XLA Modules:
  0.0 171.9 jit_solution(11804586119430307747)
XLA Ops:
  0.0 1.8 %shard_map.82 = bf16[4,64,640]{2,1,0:T(8,128)(2,1)} custom-call(bf16[8,2560]{1,0:T(8,128)(2,1)} %tg_ref.1, bf16[8,640]{1,0:T(8,128)(2,1)} %ta_ref.1, s32[1,8]{1,0:T(1,128)} %bitcast.56, bf16[4,2560]{1,0:T(4,128)(2,1)} %qg_ref.1, bf16[4,640]{1,0:T(4,128)(2,1)} %qa_ref.1), custom_call_target="tpu_custom_call" | custom-call | tf_op jit(solution)/shard_map/pallas_call | solution.py:264
  1.8 17.2 %all-to-all-start = ((bf16[32,8,640]{2,1,0:T(8,128)(2,1)}), bf16[32,8,640]{2,1,0:T(8,128)(2,1)S(1)}, u32[]{:S(2)}, u32[]{:S(2)}) async-start(bf16[32,8,640]{2,1,0:T(8,128)(2,1)} %bitcast.43), calls=%async_computation | async-start | bytes 655360 | tf_op jit(solution)/shard_map/all_to_all | solution.py:308
  19.1 4.0 %fusion.27 = bf16[80,1280]{1,0:T(8,128)(2,1)S(1)} fusion(s32[]{:T(128)S(6)} %mul.19, s32[1280]{0:T(1024)S(1)} %get-tuple-element.35, s32[1280]{0:T(1024)S(1)} %get-tuple-element.38, s32[1280]{0:T(1024)S(1)} %get-tuple-element.36, s32[1280]{0:T(1024)S(1)} %get-tuple-element.37, pred[1280]{0:T(1024)(128)(4,1)S(1)} %get-tuple-element.39, ...), kind=kOutput, calls=%fused_computation.30 | convolution fusion | flops 591360000 | bytes 1047045 | tf_op jit(solution)/shard_map/dot_general | solution.py:326
  23.6 0.2 copy.21
  23.8 0.3 reshape.28
  24.4 11.7 %all-to-all-done = bf16[32,8,640]{2,1,0:T(8,128)(2,1)S(1)} async-done(((bf16[32,8,640]{2,1,0:T(8,128)(2,1)}), bf16[32,8,640]{2,1,0:T(8,128)(2,1)S(1)}, u32[]{:S(2)}, u32[]{:S(2)}) %all-to-all-start) | async-done | bytes 327712 | tf_op jit(solution)/shard_map/all_to_all | solution.py:308
  36.1 0.4 shard_map.83
  36.6 1.5 copy-done
  38.1 4.0 %all-to-all-start.1 = ((bf16[8,208,768]{2,1,0:T(8,128)(2,1)}), bf16[8,208,768]{2,1,0:T(8,128)(2,1)S(1)}, u32[]{:S(2)}, u32[]{:S(2)}) async-start(bf16[8,208,768]{2,1,0:T(8,128)(2,1)} %copy-done), calls=%async_computation.1 | async-start | bytes 5111808 | tf_op jit(solution)/shard_map/all_to_all | solution.py:338
  42.1 2.3 %collective-permute-start.2 = (bf16[80,1024]{1,0:T(8,128)(2,1)S(1)}, bf16[80,1024]{1,0:T(8,128)(2,1)S(1)}, u32[]{:S(2)}, u32[]{:S(2)}) collective-permute-start(bf16[80,1024]{1,0:T(8,128)(2,1)S(1)} %get-tuple-element.32), channel_id=1, source_target_pairs={{0,12},{4,0},{8,4},{12,8},{1,13},{5,1},{9,5},{13,9},{2,14},{6,2},{... | collective-permute-start | bytes 491528 | tf_op jit(solution)/shard_map/ppermute | solution.py:28
  44.4 4.9 %collective-permute-start.1 = (bf16[80,1024]{1,0:T(8,128)(2,1)S(1)}, bf16[80,1024]{1,0:T(8,128)(2,1)S(1)}, u32[]{:S(2)}, u32[]{:S(2)}) collective-permute-start(bf16[80,1024]{1,0:T(8,128)(2,1)S(1)} %get-tuple-element.33), channel_id=1, source_target_pairs={{0,8},{4,12},{8,0},{12,4},{1,9},{5,13},{9,1},{13,5},{2,10},{6,14},... | collective-permute-start | bytes 491528 | tf_op jit(solution)/shard_map/ppermute | solution.py:28
  49.3 1.9 %collective-permute-start = (bf16[80,1024]{1,0:T(8,128)(2,1)S(1)}, bf16[80,1024]{1,0:T(8,128)(2,1)S(1)}, u32[]{:S(2)}, u32[]{:S(2)}) collective-permute-start(bf16[80,1024]{1,0:T(8,128)(2,1)S(1)} %get-tuple-element.34), channel_id=1, source_target_pairs={{0,4},{4,8},{8,12},{12,0},{1,5},{5,9},{9,13},{13,1},{2,6},{6,10},{... | collective-permute-start | bytes 491528 | tf_op jit(solution)/shard_map/ppermute | solution.py:28
  51.2 1.4 collective-permute-done.2
  52.7 6.6 %collective-permute-done.1 = bf16[80,1024]{1,0:T(8,128)(2,1)S(1)} collective-permute-done((bf16[80,1024]{1,0:T(8,128)(2,1)S(1)}, bf16[80,1024]{1,0:T(8,128)(2,1)S(1)}, u32[]{:S(2)}, u32[]{:S(2)}) %collective-permute-start.1) | collective-permute-done | bytes 163872 | tf_op jit(solution)/shard_map/ppermute | solution.py:28
  59.2 4.0 %collective-permute-done = bf16[80,1024]{1,0:T(8,128)(2,1)S(1)} collective-permute-done((bf16[80,1024]{1,0:T(8,128)(2,1)S(1)}, bf16[80,1024]{1,0:T(8,128)(2,1)S(1)}, u32[]{:S(2)}, u32[]{:S(2)}) %collective-permute-start) | collective-permute-done | bytes 163872 | tf_op jit(solution)/shard_map/ppermute | solution.py:28
  63.4 2.1 %collective-permute-start.3 = (bf16[4,80,1024]{2,1,0:T(8,128)(2,1)S(1)}, bf16[4,80,1024]{2,1,0:T(8,128)(2,1)S(1)}, u32[]{:S(2)}, u32[]{:S(2)}) collective-permute-start(bf16[4,80,1024]{2,1,0:T(8,128)(2,1)S(1)} %pad_maximum_fusion.own_ref.inv_ref), channel_id=1, source_target_pairs={{0,1},{1,0},{2,3},{3,2},{4,5},{5,4},{6,7},{7,6},{8,9},{9,8},{10,11... | collective-permute-start | bytes 1966088 | tf_op jit(solution)/shard_map/ppermute | solution.py:22
  65.5 1.9 %collective-permute-done.3.other_ref.invo_ref = bf16[4,80,1024]{2,1,0:T(8,128)(2,1)S(1)} collective-permute-done((bf16[4,80,1024]{2,1,0:T(8,128)(2,1)S(1)}, bf16[4,80,1024]{2,1,0:T(8,128)(2,1)S(1)}, u32[]{:S(2)}, u32[]{:S(2)}) %collective-permute-start.3) | collective-permute-done | bytes 655392 | tf_op jit(solution)/shard_map/ppermute | solution.py:22
  67.4 0.8 copy-done.1
  68.2 5.6 %all-to-all-done.1.full_ref = bf16[8,208,768]{2,1,0:T(8,128)(2,1)S(1)} async-done(((bf16[8,208,768]{2,1,0:T(8,128)(2,1)}), bf16[8,208,768]{2,1,0:T(8,128)(2,1)S(1)}, u32[]{:S(2)}, u32[]{:S(2)}) %all-to-all-start.1) | async-done | bytes 2555936 | tf_op jit(solution)/shard_map/all_to_all | solution.py:338
  73.8 1.1 copy-done.2
  74.8 1.9 %shard_map.84 = bf16[8,112,512]{2,1,0:T(8,128)(2,1)S(1)} custom-call(bf16[8,208,768]{2,1,0:T(8,128)(2,1)S(1)} %all-to-all-done.1.full_ref, bf16[4,80,1024]{2,1,0:T(8,128)(2,1)S(1)} %pad_maximum_fusion.own_ref.inv_ref, bf16[4,80,1024]{2,1,0:T(8,128)(2,1)S(1)} %copy-done.2), custom_call_target="tpu_custom_call" | custom-call | tf_op jit(solution)/shard_map/pallas_call | solution.py:274
  76.8 27.3 %all_to_all.31.parts_ref = bf16[8,112,512]{2,1,0:T(8,128)(2,1)S(1)} all-to-all(bf16[8,112,512]{2,1,0:T(8,128)(2,1)S(1)} %shard_map.84), channel_id=1, replica_groups=mesh['yh'=4,'yl'=2,'x'=4,'zh'=4,'zl'=2,'c'=2] {'zh','zl'}, dimensions={0} | all-to-all | bytes 1835008 | tf_op jit(solution)/shard_map/all_to_all | solution.py:350
  104.1 1.1 shard_map.85
  105.3 5.7 %all-to-all-start.3 = ((bf16[32,16,512]{2,1,0:T(8,128)(2,1)}), bf16[32,16,512]{2,1,0:T(8,128)(2,1)S(1)}, u32[]{:S(2)}, u32[]{:S(2)}) async-start(bf16[32,16,512]{2,1,0:T(8,128)(2,1)} %get-tuple-element.27), calls=%async_computation.3 | async-start | bytes 1048576 | tf_op jit(solution)/shard_map/all_to_all | solution.py:356
  110.9 3.7 %all-gather = bf16[160,384]{1,0:T(8,128)(2,1)S(1)} all-gather(bf16[80,384]{1,0:T(8,128)(2,1)S(1)} %get-tuple-element.28), channel_id=2, replica_groups=mesh['yh'=4,'yl'=2,'x'=4,'zh'=4,'zl'=2,'c'=2] {'zl'}, dimensions={0}, use_global_device_ids=true | all-gather | bytes 184320 | tf_op jit(solution)/shard_map/all_gather | solution.py:357
  114.7 13.4 %all-gather.1 = bf16[8,80,384]{2,1,0:T(8,128)(2,1)S(1)} all-gather(bf16[2,80,384]{2,1,0:T(8,128)(2,1)S(1)} %bitcast.49), channel_id=3, replica_groups=mesh['yh'=4,'yl'=2,'x'=4,'zh'=4,'zl'=2,'c'=2] {'zh'}, dimensions={0}, use_global_device_ids=true | all-gather | bytes 614400 | tf_op jit(solution)/shard_map/all_gather | solution.py:357
  128.1 6.8 %collective-permute-start.4 = (bf16[512,512]{1,0:T(8,128)(2,1)S(1)}, bf16[512,512]{1,0:T(8,128)(2,1)S(1)}, u32[]{:S(2)}, u32[]{:S(2)}) collective-permute-start(bf16[512,512]{1,0:T(8,128)(2,1)S(1)} %bitcast.37), channel_id=1, source_target_pairs={{0,1},{1,0},{2,3},{3,2},{4,5},{5,4},{6,7},{7,6},{8,9},{9,8},{10,11... | collective-permute-start | bytes 1572872 | tf_op jit(solution)/shard_map/ppermute | solution.py:22
  135.0 1.9 %collective-permute-start.5 = (bf16[4,2,80,128]{3,2,1,0:T(8,128)(2,1)S(1)}, bf16[4,2,80,128]{3,2,1,0:T(8,128)(2,1)S(1)}, u32[]{:S(2)}, u32[]{:S(2)}) collective-permute-start(bf16[4,2,80,128]{3,2,1,0:T(8,128)(2,1)S(1)} %slice.11), channel_id=1, source_target_pairs={{0,1},{1,0},{2,3},{3,2},{4,5},{5,4},{6,7},{7,6},{8,9},{9,8},{10,11... | collective-permute-start | bytes 491528 | tf_op jit(solution)/shard_map/ppermute | solution.py:22
  136.9 1.4 collective-permute-done.5.go_ref
  138.3 4.6 %shard_map.86 = f32[8,512]{1,0:T(8,128)S(1)} custom-call(bf16[512,512]{1,0:T(8,128)(2,1)S(1)} %bitcast.38, bf16[512,512]{1,0:T(8,128)(2,1)S(1)} %collective-permute-done.4.ao_ref, bf16[4,2,80,384]{3,2,1,0:T(8,128)(2,1)S(1)} %bitcast.36, bf16[4,2,80,128]{3,2,1,0:T(8,128)(2,1)S(1)} %collective-permute-done.5.go_ref, ...), custom_call_target="tpu_custom_call" | custom-call | tf_op jit(solution)/shard_map/pallas_call | solution.py:274
  143.2 28.1 %all_to_all.32 = f32[256,1,16]{2,1,0:T(1,128)S(1)} all-to-all(f32[256,1,16]{2,1,0:T(1,128)S(1)} %bitcast.47), channel_id=1, replica_groups=mesh['yh'=4,'yl'=2,'x'=4,'zh'=4,'zl'=2,'c'=2] {'x','yl','yh','zh','zl'}, dimensions={0} | all-to-all | bytes 32768 | tf_op jit(solution)/shard_map/all_to_all | solution.py:371
  171.3 0.7 shard_map.87
  (27 shorter events, 1.1 us)
Async XLA Ops:
  1.8 34.3 %all-to-all-start = ((bf16[32,8,640]{2,1,0:T(8,128)(2,1)}), bf16[32,8,640]{2,1,0:T(8,128)(2,1)S(1)}, u32[]{:S(2)}, u32[]{:S(2)}) async-start(bf16[32,8,640]{2,1,0:T(8,128)(2,1)} %bitcast.43), calls=%async_computation | async-start | bytes 655360 | tf_op jit(solution)/shard_map/all_to_all | solution.py:308
  19.1 4.1 %copy-start.5 = (bf16[640,20]{0,1:T(8,128)(2,1)S(1)}, bf16[640,20]{0,1:T(8,128)(2,1)}, u32[]{:S(2)}) copy-start(bf16[640,20]{0,1:T(8,128)(2,1)} %param.14) | copy-start | bytes 76804
  19.1 5.0 %copy-start.4 = (bf16[2560,80]{0,1:T(8,128)(2,1)S(1)}, bf16[2560,80]{0,1:T(8,128)(2,1)}, u32[]{:S(2)}) copy-start(bf16[2560,80]{0,1:T(8,128)(2,1)} %param.13) | copy-start | bytes 1228804
  36.6 1.5 copy-start
  38.1 35.7 %all-to-all-start.1 = ((bf16[8,208,768]{2,1,0:T(8,128)(2,1)}), bf16[8,208,768]{2,1,0:T(8,128)(2,1)S(1)}, u32[]{:S(2)}, u32[]{:S(2)}) async-start(bf16[8,208,768]{2,1,0:T(8,128)(2,1)} %copy-done), calls=%async_computation.1 | async-start | bytes 5111808 | tf_op jit(solution)/shard_map/all_to_all | solution.py:338
  42.1 10.5 %collective-permute-start.2 = (bf16[80,1024]{1,0:T(8,128)(2,1)S(1)}, bf16[80,1024]{1,0:T(8,128)(2,1)S(1)}, u32[]{:S(2)}, u32[]{:S(2)}) collective-permute-start(bf16[80,1024]{1,0:T(8,128)(2,1)S(1)} %get-tuple-element.32), channel_id=1, source_target_pairs={{0,12},{4,0},{8,4},{12,8},{1,13},{5,1},{9,5},{13,9},{2,14},{6,2},{... | collective-permute-start | bytes 491528 | tf_op jit(solution)/shard_map/ppermute | solution.py:28
  44.4 14.8 %collective-permute-start.1 = (bf16[80,1024]{1,0:T(8,128)(2,1)S(1)}, bf16[80,1024]{1,0:T(8,128)(2,1)S(1)}, u32[]{:S(2)}, u32[]{:S(2)}) collective-permute-start(bf16[80,1024]{1,0:T(8,128)(2,1)S(1)} %get-tuple-element.33), channel_id=1, source_target_pairs={{0,8},{4,12},{8,0},{12,4},{1,9},{5,13},{9,1},{13,5},{2,10},{6,14},... | collective-permute-start | bytes 491528 | tf_op jit(solution)/shard_map/ppermute | solution.py:28
  49.3 14.0 %collective-permute-start = (bf16[80,1024]{1,0:T(8,128)(2,1)S(1)}, bf16[80,1024]{1,0:T(8,128)(2,1)S(1)}, u32[]{:S(2)}, u32[]{:S(2)}) collective-permute-start(bf16[80,1024]{1,0:T(8,128)(2,1)S(1)} %get-tuple-element.34), channel_id=1, source_target_pairs={{0,4},{4,8},{8,12},{12,0},{1,5},{5,9},{9,13},{13,1},{2,6},{6,10},{... | collective-permute-start | bytes 491528 | tf_op jit(solution)/shard_map/ppermute | solution.py:28
  63.4 4.0 %collective-permute-start.3 = (bf16[4,80,1024]{2,1,0:T(8,128)(2,1)S(1)}, bf16[4,80,1024]{2,1,0:T(8,128)(2,1)S(1)}, u32[]{:S(2)}, u32[]{:S(2)}) collective-permute-start(bf16[4,80,1024]{2,1,0:T(8,128)(2,1)S(1)} %pad_maximum_fusion.own_ref.inv_ref), channel_id=1, source_target_pairs={{0,1},{1,0},{2,3},{3,2},{4,5},{5,4},{6,7},{7,6},{8,9},{9,8},{10,11... | collective-permute-start | bytes 1966088 | tf_op jit(solution)/shard_map/ppermute | solution.py:22
  67.4 0.8 copy-start.1
  73.8 1.1 copy-start.2
  76.8 61.5 %copy-start.3 = (bf16[4,80,1024]{2,1,0:T(8,128)(2,1)S(1)}, bf16[4,80,1024]{2,1,0:T(8,128)(2,1)}, u32[]{:S(2)}) copy-start(bf16[4,80,1024]{2,1,0:T(8,128)(2,1)} %copy-done.1) | copy-start | bytes 1966084
  105.3 22.8 %all-to-all-start.3 = ((bf16[32,16,512]{2,1,0:T(8,128)(2,1)}), bf16[32,16,512]{2,1,0:T(8,128)(2,1)S(1)}, u32[]{:S(2)}, u32[]{:S(2)}) async-start(bf16[32,16,512]{2,1,0:T(8,128)(2,1)} %get-tuple-element.27), calls=%async_computation.3 | async-start | bytes 1048576 | tf_op jit(solution)/shard_map/all_to_all | solution.py:356
  128.1 10.2 %collective-permute-start.4 = (bf16[512,512]{1,0:T(8,128)(2,1)S(1)}, bf16[512,512]{1,0:T(8,128)(2,1)S(1)}, u32[]{:S(2)}, u32[]{:S(2)}) collective-permute-start(bf16[512,512]{1,0:T(8,128)(2,1)S(1)} %bitcast.37), channel_id=1, source_target_pairs={{0,1},{1,0},{2,3},{3,2},{4,5},{5,4},{6,7},{7,6},{8,9},{9,8},{10,11... | collective-permute-start | bytes 1572872 | tf_op jit(solution)/shard_map/ppermute | solution.py:22
  135.0 3.3 %collective-permute-start.5 = (bf16[4,2,80,128]{3,2,1,0:T(8,128)(2,1)S(1)}, bf16[4,2,80,128]{3,2,1,0:T(8,128)(2,1)S(1)}, u32[]{:S(2)}, u32[]{:S(2)}) collective-permute-start(bf16[4,2,80,128]{3,2,1,0:T(8,128)(2,1)S(1)} %slice.11), channel_id=1, source_target_pairs={{0,1},{1,0},{2,3},{3,2},{4,5},{5,4},{6,7},{7,6},{8,9},{9,8},{10,11... | collective-permute-start | bytes 491528 | tf_op jit(solution)/shard_map/ppermute | solution.py:22

commit v5 on v4

--- a/solution.py
+++ b/solution.py
@@ -171,7 +171,7 @@
         g_high, g_low = high_low(g[:, wt:])
         g_train = g[:, :wt].astype(BF)
         for s in range(H):
-            m = lax.rem(me - s + H, H) * L + l
+            m = l * H + lax.rem(me - s + H, H)
             out_ref[m, :f_own, :wt] = g_train[s * f_own:(s + 1) * f_own]
             out_ref[m, :f_own, wt:wt + wq] = g_high[s * f_own:(s + 1) * f_own]
             out_ref[m, :f_own, wt + wq:] = g_low[s * f_own:(s + 1) * f_own]
@@ -182,7 +182,7 @@
     a_high, a_low = high_low(merged)
     for s in range(H):
         for k in range(L):
-            m = lax.rem(me - s + H, H) * L + k
+            m = k * H + lax.rem(me - s + H, H)
             r = slice((s * L + k) * 32, (s * L + k + 1) * 32)
             out_ref[m, f_own:, :wt] = a_high[r]
             out_ref[m, f_own:, wt:] = a_low[r]
@@ -347,7 +347,7 @@
         jax.ShapeDtypeStruct((H * L, f_own + 32, wt + 2 * wq), BF),
         full, own, other,
     )
-    parts = lax.all_to_all(parts, ("zh", "zl"), 0, 0, tiled=True)
+    parts = lax.all_to_all(parts, ("zl", "zh"), 0, 0, tiled=True)
     g_out, a_out = local_call(
         functools.partial(combine_kernel, n=H * L, f_own=f_own, L=L, wt=wt, wq=wq, d_part=d_part),
         (jax.ShapeDtypeStruct((f_own, wt + wq), BF), jax.ShapeDtypeStruct((Y * X, 16, L * wt), BF)),

time: 173 us -> 172 us (level)
    all_to_all x1, blocking collectives: 27.3 us -> 25.1 us  [per_device(): parts = lax.all_to_all(parts, ('zl', 'zh'), 0, 0, tiled=True)]
where the time goes in v5:
time: 172 us; the launch traced here: 171 us
  blocking collectives  73.1 us (42%)
  starting transfers between devices  45.7 us (27%)
  waiting for transfers between devices  32.6 us (19%)
  Pallas kernels  10.6 us (6%)
  local copies, waits for them, and re-layouts  4.66 us (3%)
  matrix products  4.03 us (2%)
    all_to_all x1, blocking collectives, per_device(): lax.all_to_all(scores, ('x', 'yl', 'yh', 'zh', 'zl'), 0, 0, tiled=True)  29.7 us
    all_to_all x1, blocking collectives, per_device(): parts = lax.all_to_all(parts, ('zl', 'zh'), 0, 0, tiled=True)  25.1 us
    all_gather x2, blocking collectives, per_device(): g_all = lax.all_gather(lax.all_gather(g_out, 'zl'), 'zh')  18.4 us
    all_to_all x1, starting transfers between devices, per_device(): got = lax.all_to_all(message, ('yh', 'zh', 'c'), 0, 0, tiled=True)  17.2 us
    ppermute x3, waiting for transfers between devices, exchange(): lax.ppermute(out, axis, [(i, (i + step) % n) for i in range(n)])  12 us
    all_to_all x1, waiting for transfers between devices, per_device(): got = lax.all_to_all(message, ('yh', 'zh', 'c'), 0, 0, tiled=True)  11.7 us
    ppermute x3, starting transfers between devices, swap(): return lax.ppermute(v, axis, [(0, 1), (1, 0)])  10.3 us
    ppermute x3, starting transfers between devices, exchange(): lax.ppermute(out, axis, [(i, (i + step) % n) for i in range(n)])  9.08 us
  transfers between devices with their start and end apart: 9, of which 7 were waited for; matrix products, arithmetic and copies ran while one was open for 3% of the time, Pallas kernels for 0%

profile of v5, /device:TPU:1, one launch (start us, length us, event | category | flops | bytes accessed | tf_op | source)
XLA Modules:
  0.0 171.3 jit_solution(11131850839599863712)
XLA Ops:
  0.0 1.8 %shard_map.82 = bf16[4,64,640]{2,1,0:T(8,128)(2,1)} custom-call(bf16[8,2560]{1,0:T(8,128)(2,1)} %tg_ref.1, bf16[8,640]{1,0:T(8,128)(2,1)} %ta_ref.1, s32[1,8]{1,0:T(1,128)} %bitcast.56, bf16[4,2560]{1,0:T(4,128)(2,1)} %qg_ref.1, bf16[4,640]{1,0:T(4,128)(2,1)} %qa_ref.1), custom_call_target="tpu_custom_call" | custom-call | tf_op jit(solution)/shard_map/pallas_call | solution.py:264
  1.8 17.2 %all-to-all-start = ((bf16[32,8,640]{2,1,0:T(8,128)(2,1)}), bf16[32,8,640]{2,1,0:T(8,128)(2,1)S(1)}, u32[]{:S(2)}, u32[]{:S(2)}) async-start(bf16[32,8,640]{2,1,0:T(8,128)(2,1)} %bitcast.43), calls=%async_computation | async-start | bytes 655360 | tf_op jit(solution)/shard_map/all_to_all | solution.py:308
  19.1 4.0 %fusion.27 = bf16[80,1280]{1,0:T(8,128)(2,1)S(1)} fusion(s32[]{:T(128)S(6)} %mul.19, s32[1280]{0:T(1024)S(1)} %get-tuple-element.35, s32[1280]{0:T(1024)S(1)} %get-tuple-element.38, s32[1280]{0:T(1024)S(1)} %get-tuple-element.36, s32[1280]{0:T(1024)S(1)} %get-tuple-element.37, pred[1280]{0:T(1024)(128)(4,1)S(1)} %get-tuple-element.39, ...), kind=kOutput, calls=%fused_computation.30 | convolution fusion | flops 591360000 | bytes 1047045 | tf_op jit(solution)/shard_map/dot_general | solution.py:326
  23.6 0.2 copy.21
  23.8 0.3 reshape.28
  24.4 11.7 %all-to-all-done = bf16[32,8,640]{2,1,0:T(8,128)(2,1)S(1)} async-done(((bf16[32,8,640]{2,1,0:T(8,128)(2,1)}), bf16[32,8,640]{2,1,0:T(8,128)(2,1)S(1)}, u32[]{:S(2)}, u32[]{:S(2)}) %all-to-all-start) | async-done | bytes 327712 | tf_op jit(solution)/shard_map/all_to_all | solution.py:308
  36.1 0.4 shard_map.83
  36.6 1.5 copy-done
  38.1 4.0 %all-to-all-start.1 = ((bf16[8,208,768]{2,1,0:T(8,128)(2,1)}), bf16[8,208,768]{2,1,0:T(8,128)(2,1)S(1)}, u32[]{:S(2)}, u32[]{:S(2)}) async-start(bf16[8,208,768]{2,1,0:T(8,128)(2,1)} %copy-done), calls=%async_computation.1 | async-start | bytes 5111808 | tf_op jit(solution)/shard_map/all_to_all | solution.py:338
  42.1 2.3 %collective-permute-start.2 = (bf16[80,1024]{1,0:T(8,128)(2,1)S(1)}, bf16[80,1024]{1,0:T(8,128)(2,1)S(1)}, u32[]{:S(2)}, u32[]{:S(2)}) collective-permute-start(bf16[80,1024]{1,0:T(8,128)(2,1)S(1)} %get-tuple-element.32), channel_id=1, source_target_pairs={{0,12},{4,0},{8,4},{12,8},{1,13},{5,1},{9,5},{13,9},{2,14},{6,2},{... | collective-permute-start | bytes 491528 | tf_op jit(solution)/shard_map/ppermute | solution.py:28
  44.4 4.9 %collective-permute-start.1 = (bf16[80,1024]{1,0:T(8,128)(2,1)S(1)}, bf16[80,1024]{1,0:T(8,128)(2,1)S(1)}, u32[]{:S(2)}, u32[]{:S(2)}) collective-permute-start(bf16[80,1024]{1,0:T(8,128)(2,1)S(1)} %get-tuple-element.33), channel_id=1, source_target_pairs={{0,8},{4,12},{8,0},{12,4},{1,9},{5,13},{9,1},{13,5},{2,10},{6,14},... | collective-permute-start | bytes 491528 | tf_op jit(solution)/shard_map/ppermute | solution.py:28
  49.3 1.9 %collective-permute-start = (bf16[80,1024]{1,0:T(8,128)(2,1)S(1)}, bf16[80,1024]{1,0:T(8,128)(2,1)S(1)}, u32[]{:S(2)}, u32[]{:S(2)}) collective-permute-start(bf16[80,1024]{1,0:T(8,128)(2,1)S(1)} %get-tuple-element.34), channel_id=1, source_target_pairs={{0,4},{4,8},{8,12},{12,0},{1,5},{5,9},{9,13},{13,1},{2,6},{6,10},{... | collective-permute-start | bytes 491528 | tf_op jit(solution)/shard_map/ppermute | solution.py:28
  51.2 1.4 collective-permute-done.2
  52.7 6.6 %collective-permute-done.1 = bf16[80,1024]{1,0:T(8,128)(2,1)S(1)} collective-permute-done((bf16[80,1024]{1,0:T(8,128)(2,1)S(1)}, bf16[80,1024]{1,0:T(8,128)(2,1)S(1)}, u32[]{:S(2)}, u32[]{:S(2)}) %collective-permute-start.1) | collective-permute-done | bytes 163872 | tf_op jit(solution)/shard_map/ppermute | solution.py:28
  59.2 4.0 %collective-permute-done = bf16[80,1024]{1,0:T(8,128)(2,1)S(1)} collective-permute-done((bf16[80,1024]{1,0:T(8,128)(2,1)S(1)}, bf16[80,1024]{1,0:T(8,128)(2,1)S(1)}, u32[]{:S(2)}, u32[]{:S(2)}) %collective-permute-start) | collective-permute-done | bytes 163872 | tf_op jit(solution)/shard_map/ppermute | solution.py:28
  63.4 2.1 %collective-permute-start.3 = (bf16[4,80,1024]{2,1,0:T(8,128)(2,1)S(1)}, bf16[4,80,1024]{2,1,0:T(8,128)(2,1)S(1)}, u32[]{:S(2)}, u32[]{:S(2)}) collective-permute-start(bf16[4,80,1024]{2,1,0:T(8,128)(2,1)S(1)} %pad_maximum_fusion.own_ref.inv_ref), channel_id=1, source_target_pairs={{0,1},{1,0},{2,3},{3,2},{4,5},{5,4},{6,7},{7,6},{8,9},{9,8},{10,11... | collective-permute-start | bytes 1966088 | tf_op jit(solution)/shard_map/ppermute | solution.py:22
  65.5 1.9 %collective-permute-done.3.other_ref.invo_ref = bf16[4,80,1024]{2,1,0:T(8,128)(2,1)S(1)} collective-permute-done((bf16[4,80,1024]{2,1,0:T(8,128)(2,1)S(1)}, bf16[4,80,1024]{2,1,0:T(8,128)(2,1)S(1)}, u32[]{:S(2)}, u32[]{:S(2)}) %collective-permute-start.3) | collective-permute-done | bytes 655392 | tf_op jit(solution)/shard_map/ppermute | solution.py:22
  67.4 0.8 copy-done.1
  68.2 5.6 %all-to-all-done.1.full_ref = bf16[8,208,768]{2,1,0:T(8,128)(2,1)S(1)} async-done(((bf16[8,208,768]{2,1,0:T(8,128)(2,1)}), bf16[8,208,768]{2,1,0:T(8,128)(2,1)S(1)}, u32[]{:S(2)}, u32[]{:S(2)}) %all-to-all-start.1) | async-done | bytes 2555936 | tf_op jit(solution)/shard_map/all_to_all | solution.py:338
  73.8 1.1 copy-done.2
  74.8 1.9 %shard_map.84 = bf16[8,112,512]{2,1,0:T(8,128)(2,1)S(1)} custom-call(bf16[8,208,768]{2,1,0:T(8,128)(2,1)S(1)} %all-to-all-done.1.full_ref, bf16[4,80,1024]{2,1,0:T(8,128)(2,1)S(1)} %pad_maximum_fusion.own_ref.inv_ref, bf16[4,80,1024]{2,1,0:T(8,128)(2,1)S(1)} %copy-done.2), custom_call_target="tpu_custom_call" | custom-call | tf_op jit(solution)/shard_map/pallas_call | solution.py:274
  76.8 25.1 %all_to_all.31.parts_ref = bf16[8,112,512]{2,1,0:T(8,128)(2,1)S(1)} all-to-all(bf16[8,112,512]{2,1,0:T(8,128)(2,1)S(1)} %shard_map.84), channel_id=1, replica_groups=mesh['yh'=4,'yl'=2,'x'=4,'zh'=4,'zl'=2,'c'=2] {'zl','zh'}, dimensions={0} | all-to-all | bytes 1835008 | tf_op jit(solution)/shard_map/all_to_all | solution.py:350
  101.9 1.1 shard_map.85
  103.1 5.1 %all-to-all-start.3 = ((bf16[32,16,512]{2,1,0:T(8,128)(2,1)}), bf16[32,16,512]{2,1,0:T(8,128)(2,1)S(1)}, u32[]{:S(2)}, u32[]{:S(2)}) async-start(bf16[32,16,512]{2,1,0:T(8,128)(2,1)} %get-tuple-element.27), calls=%async_computation.3 | async-start | bytes 1048576 | tf_op jit(solution)/shard_map/all_to_all | solution.py:356
  108.2 5.0 %all-gather = bf16[160,384]{1,0:T(8,128)(2,1)S(1)} all-gather(bf16[80,384]{1,0:T(8,128)(2,1)S(1)} %get-tuple-element.28), channel_id=2, replica_groups=mesh['yh'=4,'yl'=2,'x'=4,'zh'=4,'zl'=2,'c'=2] {'zl'}, dimensions={0}, use_global_device_ids=true | all-gather | bytes 184320 | tf_op jit(solution)/shard_map/all_gather | solution.py:357
  113.2 13.4 %all-gather.1 = bf16[8,80,384]{2,1,0:T(8,128)(2,1)S(1)} all-gather(bf16[2,80,384]{2,1,0:T(8,128)(2,1)S(1)} %bitcast.49), channel_id=3, replica_groups=mesh['yh'=4,'yl'=2,'x'=4,'zh'=4,'zl'=2,'c'=2] {'zh'}, dimensions={0}, use_global_device_ids=true | all-gather | bytes 614400 | tf_op jit(solution)/shard_map/all_gather | solution.py:357
  126.5 6.3 %collective-permute-start.4 = (bf16[512,512]{1,0:T(8,128)(2,1)S(1)}, bf16[512,512]{1,0:T(8,128)(2,1)S(1)}, u32[]{:S(2)}, u32[]{:S(2)}) collective-permute-start(bf16[512,512]{1,0:T(8,128)(2,1)S(1)} %bitcast.37), channel_id=1, source_target_pairs={{0,1},{1,0},{2,3},{3,2},{4,5},{5,4},{6,7},{7,6},{8,9},{9,8},{10,11... | collective-permute-start | bytes 1572872 | tf_op jit(solution)/shard_map/ppermute | solution.py:22
  132.9 1.9 %collective-permute-start.5 = (bf16[4,2,80,128]{3,2,1,0:T(8,128)(2,1)S(1)}, bf16[4,2,80,128]{3,2,1,0:T(8,128)(2,1)S(1)}, u32[]{:S(2)}, u32[]{:S(2)}) collective-permute-start(bf16[4,2,80,128]{3,2,1,0:T(8,128)(2,1)S(1)} %slice.11), channel_id=1, source_target_pairs={{0,1},{1,0},{2,3},{3,2},{4,5},{5,4},{6,7},{7,6},{8,9},{9,8},{10,11... | collective-permute-start | bytes 491528 | tf_op jit(solution)/shard_map/ppermute | solution.py:22
  134.8 1.4 collective-permute-done.5.go_ref
  136.2 4.6 %shard_map.86 = f32[8,512]{1,0:T(8,128)S(1)} custom-call(bf16[512,512]{1,0:T(8,128)(2,1)S(1)} %bitcast.38, bf16[512,512]{1,0:T(8,128)(2,1)S(1)} %collective-permute-done.4.ao_ref, bf16[4,2,80,384]{3,2,1,0:T(8,128)(2,1)S(1)} %bitcast.36, bf16[4,2,80,128]{3,2,1,0:T(8,128)(2,1)S(1)} %collective-permute-done.5.go_ref, ...), custom_call_target="tpu_custom_call" | custom-call | tf_op jit(solution)/shard_map/pallas_call | solution.py:274
  141.0 29.7 %all_to_all.32 = f32[256,1,16]{2,1,0:T(1,128)S(1)} all-to-all(f32[256,1,16]{2,1,0:T(1,128)S(1)} %bitcast.47), channel_id=1, replica_groups=mesh['yh'=4,'yl'=2,'x'=4,'zh'=4,'zl'=2,'c'=2] {'x','yl','yh','zh','zl'}, dimensions={0} | all-to-all | bytes 32768 | tf_op jit(solution)/shard_map/all_to_all | solution.py:371
  170.7 0.7 shard_map.87
  (27 shorter events, 1.1 us)
Async XLA Ops:
  1.8 34.3 %all-to-all-start = ((bf16[32,8,640]{2,1,0:T(8,128)(2,1)}), bf16[32,8,640]{2,1,0:T(8,128)(2,1)S(1)}, u32[]{:S(2)}, u32[]{:S(2)}) async-start(bf16[32,8,640]{2,1,0:T(8,128)(2,1)} %bitcast.43), calls=%async_computation | async-start | bytes 655360 | tf_op jit(solution)/shard_map/all_to_all | solution.py:308
  19.1 4.1 %copy-start.5 = (bf16[640,20]{0,1:T(8,128)(2,1)S(1)}, bf16[640,20]{0,1:T(8,128)(2,1)}, u32[]{:S(2)}) copy-start(bf16[640,20]{0,1:T(8,128)(2,1)} %param.14) | copy-start | bytes 76804
  19.1 5.0 %copy-start.4 = (bf16[2560,80]{0,1:T(8,128)(2,1)S(1)}, bf16[2560,80]{0,1:T(8,128)(2,1)}, u32[]{:S(2)}) copy-start(bf16[2560,80]{0,1:T(8,128)(2,1)} %param.13) | copy-start | bytes 1228804
  36.6 1.5 copy-start
  38.1 35.7 %all-to-all-start.1 = ((bf16[8,208,768]{2,1,0:T(8,128)(2,1)}), bf16[8,208,768]{2,1,0:T(8,128)(2,1)S(1)}, u32[]{:S(2)}, u32[]{:S(2)}) async-start(bf16[8,208,768]{2,1,0:T(8,128)(2,1)} %copy-done), calls=%async_computation.1 | async-start | bytes 5111808 | tf_op jit(solution)/shard_map/all_to_all | solution.py:338
  42.1 10.5 %collective-permute-start.2 = (bf16[80,1024]{1,0:T(8,128)(2,1)S(1)}, bf16[80,1024]{1,0:T(8,128)(2,1)S(1)}, u32[]{:S(2)}, u32[]{:S(2)}) collective-permute-start(bf16[80,1024]{1,0:T(8,128)(2,1)S(1)} %get-tuple-element.32), channel_id=1, source_target_pairs={{0,12},{4,0},{8,4},{12,8},{1,13},{5,1},{9,5},{13,9},{2,14},{6,2},{... | collective-permute-start | bytes 491528 | tf_op jit(solution)/shard_map/ppermute | solution.py:28
  44.4 14.8 %collective-permute-start.1 = (bf16[80,1024]{1,0:T(8,128)(2,1)S(1)}, bf16[80,1024]{1,0:T(8,128)(2,1)S(1)}, u32[]{:S(2)}, u32[]{:S(2)}) collective-permute-start(bf16[80,1024]{1,0:T(8,128)(2,1)S(1)} %get-tuple-element.33), channel_id=1, source_target_pairs={{0,8},{4,12},{8,0},{12,4},{1,9},{5,13},{9,1},{13,5},{2,10},{6,14},... | collective-permute-start | bytes 491528 | tf_op jit(solution)/shard_map/ppermute | solution.py:28
  49.3 14.0 %collective-permute-start = (bf16[80,1024]{1,0:T(8,128)(2,1)S(1)}, bf16[80,1024]{1,0:T(8,128)(2,1)S(1)}, u32[]{:S(2)}, u32[]{:S(2)}) collective-permute-start(bf16[80,1024]{1,0:T(8,128)(2,1)S(1)} %get-tuple-element.34), channel_id=1, source_target_pairs={{0,4},{4,8},{8,12},{12,0},{1,5},{5,9},{9,13},{13,1},{2,6},{6,10},{... | collective-permute-start | bytes 491528 | tf_op jit(solution)/shard_map/ppermute | solution.py:28
  63.4 4.0 %collective-permute-start.3 = (bf16[4,80,1024]{2,1,0:T(8,128)(2,1)S(1)}, bf16[4,80,1024]{2,1,0:T(8,128)(2,1)S(1)}, u32[]{:S(2)}, u32[]{:S(2)}) collective-permute-start(bf16[4,80,1024]{2,1,0:T(8,128)(2,1)S(1)} %pad_maximum_fusion.own_ref.inv_ref), channel_id=1, source_target_pairs={{0,1},{1,0},{2,3},{3,2},{4,5},{5,4},{6,7},{7,6},{8,9},{9,8},{10,11... | collective-permute-start | bytes 1966088 | tf_op jit(solution)/shard_map/ppermute | solution.py:22
  67.4 0.8 copy-start.1
  73.8 1.1 copy-start.2
  76.8 59.4 %copy-start.3 = (bf16[4,80,1024]{2,1,0:T(8,128)(2,1)S(1)}, bf16[4,80,1024]{2,1,0:T(8,128)(2,1)}, u32[]{:S(2)}) copy-start(bf16[4,80,1024]{2,1,0:T(8,128)(2,1)} %copy-done.1) | copy-start | bytes 1966084
  103.1 23.5 %all-to-all-start.3 = ((bf16[32,16,512]{2,1,0:T(8,128)(2,1)}), bf16[32,16,512]{2,1,0:T(8,128)(2,1)S(1)}, u32[]{:S(2)}, u32[]{:S(2)}) async-start(bf16[32,16,512]{2,1,0:T(8,128)(2,1)} %get-tuple-element.27), calls=%async_computation.3 | async-start | bytes 1048576 | tf_op jit(solution)/shard_map/all_to_all | solution.py:356
  126.5 9.6 %collective-permute-start.4 = (bf16[512,512]{1,0:T(8,128)(2,1)S(1)}, bf16[512,512]{1,0:T(8,128)(2,1)S(1)}, u32[]{:S(2)}, u32[]{:S(2)}) collective-permute-start(bf16[512,512]{1,0:T(8,128)(2,1)S(1)} %bitcast.37), channel_id=1, source_target_pairs={{0,1},{1,0},{2,3},{3,2},{4,5},{5,4},{6,7},{7,6},{8,9},{9,8},{10,11... | collective-permute-start | bytes 1572872 | tf_op jit(solution)/shard_map/ppermute | solution.py:22
  132.9 3.3 %collective-permute-start.5 = (bf16[4,2,80,128]{3,2,1,0:T(8,128)(2,1)S(1)}, bf16[4,2,80,128]{3,2,1,0:T(8,128)(2,1)S(1)}, u32[]{:S(2)}, u32[]{:S(2)}) collective-permute-start(bf16[4,2,80,128]{3,2,1,0:T(8,128)(2,1)S(1)} %slice.11), channel_id=1, source_target_pairs={{0,1},{1,0},{2,3},{3,2},{4,5},{5,4},{6,7},{7,6},{8,9},{9,8},{10,11... | collective-permute-start | bytes 491528 | tf_op jit(solution)/shard_map/ppermute | solution.py:22
